TPU v7x, 256 devices: a whole 4x4x8 slice. The times are simulated.
256 devices in a mesh: sec: 2 (over y_hi), gy: 16 (over y_lo, z), gx: 8 (over x, core).
Axes of the slice: x: 4, y: 4 (y_hi: 2, y_lo: 2; y = y_hi * 2 + y_lo), z: 8, core: 2. Of those that a mesh axis runs over, the one named last changes fastest.
Arguments:
- spectrum: float32 [36, 20, 512, 1024], P(None, None, ('sec', 'gy'), 'gx'), may hold values from 0.1 to 1
- sea_mask: int32 [512, 1024], P(('sec', 'gy', 'gx')), may hold values 0 or 1
- ocean_state: float32 [3, 768, 1536], P(None, ('sec', 'gy', 'gx')), may hold values from -3 to 3
- depth: float32 [768, 1536], P(('sec', 'gy', 'gx')), may hold values from 0.5 to 2
Outputs:
- spectrum_out: float32 [36, 20, 512, 1024], P(None, None, ('sec', 'gy'), 'gx')
- ocean_out: float32 [3, 768, 1536], P(None, ('sec', 'gy', 'gx'))
All inputs are finite; a program needn't handle non-finite values. No bound on the sum of `sea_mask` on one device may be relied on, other than what follows from the above.
Results may differ from a plain program's by a relative error of at most 0.0001.
Values sent between devices are 32-bit elements; how exact they have to be, the bound alone decides.
A program may use at most 128 MiB of HBM per device.

v0:
```python
import math

import jax
import jax.numpy as jnp
from jax import lax
from jax.sharding import PartitionSpec as P

BAND = 2
ITERS = 4


TWO_THIRDS = 2.0 / 3.0
ONE_THIRD = 1.0 / 3.0
GRAVITY_STEP = 0.3
CORIOLIS_STEP = 0.2
STRESS_GAIN = 2.0
TURN_GAIN = 0.2
SPEED_BASE = 0.35
SPEED_RATIO = 0.9


def extended(cells, sides, width):
    for axis, dim in sides:
        count = lax.axis_size(axis)
        ends = count - 1
        head = lax.slice_in_dim(cells, 0, width, axis=dim)
        tail = lax.slice_in_dim(cells, cells.shape[dim] - width, cells.shape[dim], axis=dim)
        cells = jnp.concatenate(
            [
                lax.ppermute(tail, axis, [(i, (i + 1) % count) for i in range(ends)]),
                cells,
                lax.ppermute(head, axis, [((i + 1) % count, i) for i in range(ends)]),
            ],
            axis=dim,
        )
    return cells


def to_wave_grid(field):

    def along_rows(values):
        shape = values.shape
        groups = values.reshape(shape[:-2] + (shape[-2] // 3, 3, shape[-1]))
        first = groups[..., 0, :]
        middle = groups[..., 1, :]
        last = groups[..., 2, :]
        lower = TWO_THIRDS * first + ONE_THIRD * middle
        upper = ONE_THIRD * middle + TWO_THIRDS * last
        return jnp.stack([lower, upper], axis=-2).reshape(
            shape[:-2] + (2 * (shape[-2] // 3), shape[-1])
        )

    rowwise = along_rows(field)
    return jnp.swapaxes(along_rows(jnp.swapaxes(rowwise, -1, -2)), -1, -2)


def to_ocean_grid(field):

    def along_rows(values):
        shape = values.shape
        groups = values.reshape(shape[:-2] + (shape[-2] // 2, 2, shape[-1]))
        first = groups[..., 0, :]
        second = groups[..., 1, :]
        middle = 0.5 * first + 0.5 * second
        return jnp.stack([first, middle, second], axis=-2).reshape(
            shape[:-2] + (3 * (shape[-2] // 2), shape[-1])
        )

    rowwise = along_rows(field)
    return jnp.swapaxes(along_rows(jnp.swapaxes(rowwise, -1, -2)), -1, -2)


def mask_to_ocean(field):

    def along_rows(values):
        shape = values.shape
        groups = values.reshape(shape[:-2] + (shape[-2] // 2, 2, shape[-1]))
        first = groups[..., 0, :]
        second = groups[..., 1, :]
        return jnp.stack([first, first, second], axis=-2).reshape(
            shape[:-2] + (3 * (shape[-2] // 2), shape[-1])
        )

    rowwise = along_rows(field)
    return jnp.swapaxes(along_rows(jnp.swapaxes(rowwise, -1, -2)), -1, -2)


def gradients(padded):
    along_x = (padded[..., 1:-1, 2:] - padded[..., 1:-1, :-2]) * 0.5
    along_y = (padded[..., 2:, 1:-1] - padded[..., :-2, 1:-1]) * 0.5
    return (along_x, along_y)


def wave_tables(ndir, nfreq):
    index_dir = jnp.arange(ndir, dtype=jnp.float32)
    heading = 2.0 * math.pi * (index_dir + 0.5) / ndir
    index_freq = jnp.arange(nfreq, dtype=jnp.float32)
    speed = SPEED_BASE * jnp.power(SPEED_RATIO, index_freq)
    cosine = jnp.cos(heading)
    sine = jnp.sin(heading)
    east_speed = cosine[:, None] * speed[None, :]
    north_speed = sine[:, None] * speed[None, :]
    stress_table = jnp.stack([0.5 * cosine * cosine, 0.5 * sine * cosine, 0.5 * sine * sine]) / (
        ndir * nfreq
    )
    return (east_speed, north_speed, stress_table)


def wave_update(
    masked,
    west_cells,
    east_cells,
    south_rows,
    north_rows,
    wave_mask,
    vorticity,
    divergence,
    east_speed,
    north_speed,
    stress_table,
):

    def parts(speed):
        return (
            jnp.maximum(speed, 0.0)[:, :, None, None],
            jnp.minimum(speed, 0.0)[:, :, None, None],
            jnp.abs(speed)[:, :, None, None],
        )

    east_pos, east_neg, east_abs = parts(east_speed)
    north_pos, north_neg, north_abs = parts(north_speed)
    east_term = east_pos * west_cells - east_abs * masked - east_neg * east_cells
    north_term = north_pos * south_rows - north_abs * masked - north_neg * north_rows
    turning = TURN_GAIN * jnp.tanh(vorticity)
    turn_pos = jnp.maximum(turning, 0.0)[None, None]
    turn_neg = jnp.minimum(turning, 0.0)[None, None]
    turn_abs = jnp.abs(turning)[None, None]
    turn_term = (
        turn_pos * jnp.roll(masked, 1, axis=0)
        - turn_abs * masked
        - turn_neg * jnp.roll(masked, -1, axis=0)
    )
    shifting = TURN_GAIN * jnp.tanh(divergence)
    shift_pos = jnp.maximum(shifting, 0.0)[None, None]
    shift_neg = jnp.minimum(shifting, 0.0)[None, None]
    faces = shift_pos * masked[:, :-1] + shift_neg * masked[:, 1:]
    padded_faces = jnp.pad(faces, ((0, 0), (1, 1), (0, 0), (0, 0)))
    shift_term = padded_faces[:, :-1] - padded_faces[:, 1:]
    updated = (masked + east_term + north_term + turn_term + shift_term) * wave_mask[None, None]
    stress = jnp.einsum("kjrx,sk->srx", updated, stress_table, precision=lax.Precision.HIGHEST)
    return (updated, stress)


def ocean_rim(stack):
    rows_added = extended(stack, ((("sec", "gy", "gx"), 1),), 1)
    return jnp.pad(rows_added, ((0, 0), (0, 0), (1, 1)))


def shards(spectrum, sea_mask, ocean_state, depth):
    ndir = spectrum.shape[0]
    nfreq = spectrum.shape[1]
    tile_rows = spectrum.shape[2]
    band_mask = sea_mask.astype(jnp.float32)
    ocean_mask = mask_to_ocean(band_mask)
    state = ocean_state * ocean_mask[None]
    surface, eastward, northward = (state[0], state[1], state[2])
    along_x, along_y = gradients(ocean_rim(state[1:3]))
    vorticity = to_wave_grid(along_x[1] - along_y[0])
    divergence = to_wave_grid(along_x[0] + along_y[1])
    outgoing = jnp.stack([vorticity, divergence, band_mask])
    tile_fields = lax.all_to_all(outgoing, "gx", split_axis=2, concat_axis=1, tiled=True)
    tile_vorticity, tile_divergence, tile_mask = (tile_fields[0], tile_fields[1], tile_fields[2])
    masked = spectrum * tile_mask[None, None]
    padded = extended(masked, ((("sec", "gy"), 2), ("gx", 3)), 1)
    east_speed, north_speed, stress_table = wave_tables(ndir, nfreq)
    block_rows = BAND

    def one_block(block, carry):
        result, stress = carry
        start = (block * block_rows).astype(jnp.int32)
        window = lax.dynamic_slice_in_dim(padded, start, block_rows + 2, 2)
        center = window[:, :, 1:-1, 1:-1]
        updated, rows_stress = wave_update(
            center,
            window[:, :, 1:-1, :-2],
            window[:, :, 1:-1, 2:],
            window[:, :, :-2, 1:-1],
            window[:, :, 2:, 1:-1],
            lax.dynamic_slice_in_dim(tile_mask, start, block_rows, 0),
            lax.dynamic_slice_in_dim(tile_vorticity, start, block_rows, 0),
            lax.dynamic_slice_in_dim(tile_divergence, start, block_rows, 0),
            east_speed,
            north_speed,
            stress_table,
        )
        result = lax.dynamic_update_slice_in_dim(result, updated, start, 2)
        stress = lax.dynamic_update_slice_in_dim(stress, rows_stress, start, 1)
        return (result, stress)

    spectrum_out, stress = lax.fori_loop(
        0,
        tile_rows // block_rows,
        one_block,
        (jnp.zeros_like(spectrum), jnp.zeros((3, tile_rows, spectrum.shape[3]), jnp.float32)),
    )
    band_stress = lax.all_to_all(stress, "gx", split_axis=1, concat_axis=2, tiled=True)
    along_x, along_y = gradients(ocean_rim(to_ocean_grid(band_stress)))
    force_x = -STRESS_GAIN * (along_x[0] + along_y[1]) / depth
    force_y = -STRESS_GAIN * (along_x[1] + along_y[2]) / depth
    for step in range(ITERS):
        along_x, along_y = gradients(ocean_rim(jnp.stack([depth * eastward, depth * northward])))
        surface = (surface - GRAVITY_STEP * (along_x[0] + along_y[1])) * ocean_mask
        along_x, along_y = gradients(ocean_rim(surface[None]))
        new_east = (
            eastward + GRAVITY_STEP * (CORIOLIS_STEP * northward - along_x[0]) + force_x
        ) * ocean_mask
        new_north = (
            northward + GRAVITY_STEP * (-CORIOLIS_STEP * eastward - along_y[0]) + force_y
        ) * ocean_mask
        eastward, northward = (new_east, new_north)
    return (spectrum_out, jnp.stack([surface, eastward, northward]))


def solution(mesh):
    return jax.shard_map(
        shards,
        mesh=mesh,
        in_specs=(
            P(None, None, ("sec", "gy"), "gx"),
            P(("sec", "gy", "gx"), None),
            P(None, ("sec", "gy", "gx"), None),
            P(("sec", "gy", "gx"), None),
        ),
        out_specs=(P(None, None, ("sec", "gy"), "gx"), P(None, ("sec", "gy", "gx"), None)),
        check_vma=False,
    )
```

profile of v0, /device:TPU:25, one launch (start us, length us, event | category | flops | bytes accessed | tf_op | source)
XLA Modules:
  0.0 528.2 jit_solution(17832933988546758790)
XLA Ops:
  3.8 3.7 collective-permute-start
  10.2 3.6 collective-permute-start.6
  13.8 6.8 %collective-permute-start.7 = (f32[2,1,1536]{2,1,0:T(1,128)S(1)}, f32[2,1,1536]{2,1,0:T(1,128)S(1)}, u32[]{:S(2)}, u32[]{:S(2)}) collective-permute-start(f32[2,1,1536]{2,1,0:T(1,128)S(1)} %get-tuple-element.498), channel_id=1, source_target_pairs={{1,0},{2,1},{3,2},{4,3},{5,4},{6,5},{7,6},{8,7},{9,8},{10,9},{11,1... | collective-permute-start | bytes 36872 | tf_op jit(solution)/shard_map/ppermute | solution.py:32
  27.6 9.2 %all-to-all-start = ((f32[8,1,768]{2,1,0:T(1,128)}), f32[8,1,768]{2,1,0:T(1,128)S(1)}, u32[]{:S(2)}, u32[]{:S(2)}) async-start(f32[8,1,768]{2,1,0:T(1,128)} %reshape.273), calls=%async_computation | async-start | bytes 49152 | tf_op jit(solution)/shard_map/all_to_all | solution.py:171
  37.0 4.5 all-to-all-done
  54.9 5.7 %collective-permute-start.3 = (f32[36,20,1,128]{3,2,1,0:T(1,128)S(1)}, f32[36,20,1,128]{3,2,1,0:T(1,128)S(1)}, u32[]{:S(2)}, u32[]{:S(2)}) collective-permute-start(f32[36,20,1,128]{3,2,1,0:T(1,128)S(1)} %get-tuple-element.453), channel_id=1, source_target_pairs={{8,0},{16,8},{24,16},{32,24},{40,32},{48,40},{56,48},{64,56},{72,6... | collective-permute-start | bytes 1105928 | tf_op jit(solution)/shard_map/ppermute | solution.py:32
  60.6 5.7 %collective-permute-done.2 = f32[36,20,1,128]{3,2,1,0:T(1,128)S(1)} collective-permute-done((f32[36,20,1,128]{3,2,1,0:T(1,128)S(1)}, f32[36,20,1,128]{3,2,1,0:T(1,128)S(1)}, u32[]{:S(2)}, u32[]{:S(2)}) %collective-permute-start.2) | collective-permute-done | bytes 368672 | tf_op jit(solution)/shard_map/ppermute | solution.py:30
  68.8 7.7 %fusion.156 = (f32[36,20,18,1]{3,2,1,0:T(8,128)}, f32[36,20,18,1]{3,2,1,0:T(8,128)}) fusion(f32[36,20,18,128]{3,2,1,0:T(8,128)S(1)} %pad_maximum_fusion.1), kind=kLoop, calls=%fused_computation.295 | loop fusion | bytes 207360 | tf_op jit(solution)/shard_map/slice | solution.py:27
  76.5 5.6 %copy.100 = f32[36,20,18,1]{0,3,2,1:T(1,128)S(1)} copy(f32[36,20,18,1]{3,2,1,0:T(8,128)} %get-tuple-element.450) | data formatting | bytes 103680 | tf_op jit(solution)/shard_map/slice | solution.py:27
  82.1 4.0 collective-permute-start.4
  86.1 6.2 %copy.101 = f32[36,20,18,1]{0,3,2,1:T(1,128)} copy(f32[36,20,18,1]{3,2,1,0:T(8,128)} %get-tuple-element.451) | data formatting | bytes 103680 | tf_op jit(solution)/shard_map/slice | solution.py:26
  95.3 6.5 %copy.102 = f32[36,20,18,1]{3,2,1,0:T(8,128)} copy(f32[36,20,18,1]{0,3,2,1:T(1,128)} %collective-permute-done.4) | data formatting | bytes 103680 | tf_op jit(solution)/shard_map/ppermute | solution.py:30
  101.8 6.4 %copy.103 = f32[36,20,18,1]{3,2,1,0:T(8,128)} copy(f32[36,20,18,1]{0,3,2,1:T(1,128)} %collective-permute-done.5) | data formatting | bytes 103680 | tf_op jit(solution)/shard_map/ppermute | solution.py:32
  108.2 19.0 %pad_maximum_fusion = f32[36,20,18,130]{3,2,1,0:T(8,128)} fusion(f32[36,20,18,1]{3,2,1,0:T(8,128)} %copy.103, f32[36,20,1,128]{3,2,1,0:T(1,128)S(1)} %collective-permute-done.3, f32[36,20,16,128]{3,2,1,0:T(8,128)} %copy-done, f32[36,20,1,128]{3,2,1,0:T(1,128)S(1)} %collective-permute-done.2, f32[36,20,18,1]{3,2,1,0:T(8,128)} %copy.102), kind=kLoop, calls=%fused_computation.51 | loop fusion | flops 6739200 | bytes 13478400 | tf_op jit(solution)/shard_map/concatenate | solution.py:28
  131.2 301.3 %while.20 = (s32[]{:T(128)}, f32[36,20,16,128]{3,2,1,0:T(8,128)}, f32[3,16,128]{2,0,1:T(4,128)}, f32[36,20,18,130]{3,2,1,0:T(8,128)}, f32[16,128]{1,0:T(8,128)S(...) while((s32[]{:T(128)}, f32[36,20,16,128]{3,2,1,0:T(8,128)}, ...), condition=%wide.region_2.3_spmd.clone.clone.clone, body=%wide.region_0.2_spmd.clone.clone.clone.sunk | while | flops 5280557 | bytes 13252864 | solution.py:200
  131.2 9.1 %fusion.180 = f32[36,19,2,128]{3,2,1,0:T(2,128)S(1)} fusion(f32[36,20,18,130]{3,2,1,0:T(8,128)} %get-tuple-element.668, s32[]{:T(128)S(6)} %add.572, s32[]{:T(128)S(6)} %add.574, f32[2,128]{1,0:T(2,128)S(1)} %get-tuple-element.610, f32[2,128]{1,0:T(2,128)S(1)} %get-tuple-element.611), kind=kLoop, calls=%fused_computation.24.clone.1 | loop fusion | flops 525312 | bytes 2103304 | tf_op jit(solution)/shard_map/while/body/eval_jaxpr/add | solution.py:146
  140.3 9.3 %constant_dynamic-slice_fusion.10 = (f32[35,20,2,128]{3,2,1,0:T(2,128)S(1)}, f32[35,20,2,128]{3,2,1,0:T(2,128)S(1)}) fusion(f32[36,20,18,130]{3,2,1,0:T(8,128)} %get-tuple-element.668, s32[]{:T(128)S(6)} %add.574, s32[]{:T(128)S(6)} %add.572), kind=kLoop, calls=%fused_computation.35.clone.1 | loop fusion | bytes 2867208 | tf_op jit(solution)/shard_map/while/body/eval_jaxpr/jit(_roll_static)/slice | solution.py:139
  151.0 15.8 %fusion.181 = (f32[36,2,128]{2,1,0:T(2,128)S(1)}, f32[36,20,2,128]{3,2,1,0:T(2,128)S(1)}) fusion(f32[2,128]{1,0:T(2,128)S(1)} %get-tuple-element.609, f32[36,19,2,128]{3,2,1,0:T(2,128)S(1)} %fusion.180, f32[1,20,2,128]{3,2,1,0:T(2,128)S(1)} %get-tuple-element.612, f32[35,20,2,128]{3,2,1,0:T(2,128)S(1)} %get-tuple-element.613, ...), kind=kLoop, calls=%fused_computation.294.clone.1 | loop fusion | flops 4414464 | bytes 6656916 | tf_op jit(solution)/shard_map/while/body/eval_jaxpr/kjrx,sk->srx/reduce_sum | solution.py:150
  168.7 9.1 %fusion.180 = f32[36,19,2,128]{3,2,1,0:T(2,128)S(1)} fusion(f32[36,20,18,130]{3,2,1,0:T(8,128)} %get-tuple-element.668, s32[]{:T(128)S(6)} %add.572, s32[]{:T(128)S(6)} %add.574, f32[2,128]{1,0:T(2,128)S(1)} %get-tuple-element.610, f32[2,128]{1,0:T(2,128)S(1)} %get-tuple-element.611), kind=kLoop, calls=%fused_computation.24.clone.1 | loop fusion | flops 525312 | bytes 2103304 | tf_op jit(solution)/shard_map/while/body/eval_jaxpr/add | solution.py:146
  177.8 9.3 %constant_dynamic-slice_fusion.10 = (f32[35,20,2,128]{3,2,1,0:T(2,128)S(1)}, f32[35,20,2,128]{3,2,1,0:T(2,128)S(1)}) fusion(f32[36,20,18,130]{3,2,1,0:T(8,128)} %get-tuple-element.668, s32[]{:T(128)S(6)} %add.574, s32[]{:T(128)S(6)} %add.572), kind=kLoop, calls=%fused_computation.35.clone.1 | loop fusion | bytes 2867208 | tf_op jit(solution)/shard_map/while/body/eval_jaxpr/jit(_roll_static)/slice | solution.py:139
  188.4 15.8 %fusion.181 = (f32[36,2,128]{2,1,0:T(2,128)S(1)}, f32[36,20,2,128]{3,2,1,0:T(2,128)S(1)}) fusion(f32[2,128]{1,0:T(2,128)S(1)} %get-tuple-element.609, f32[36,19,2,128]{3,2,1,0:T(2,128)S(1)} %fusion.180, f32[1,20,2,128]{3,2,1,0:T(2,128)S(1)} %get-tuple-element.612, f32[35,20,2,128]{3,2,1,0:T(2,128)S(1)} %get-tuple-element.613, ...), kind=kLoop, calls=%fused_computation.294.clone.1 | loop fusion | flops 4414464 | bytes 6656916 | tf_op jit(solution)/shard_map/while/body/eval_jaxpr/kjrx,sk->srx/reduce_sum | solution.py:150
  206.1 9.1 %fusion.180 = f32[36,19,2,128]{3,2,1,0:T(2,128)S(1)} fusion(f32[36,20,18,130]{3,2,1,0:T(8,128)} %get-tuple-element.668, s32[]{:T(128)S(6)} %add.572, s32[]{:T(128)S(6)} %add.574, f32[2,128]{1,0:T(2,128)S(1)} %get-tuple-element.610, f32[2,128]{1,0:T(2,128)S(1)} %get-tuple-element.611), kind=kLoop, calls=%fused_computation.24.clone.1 | loop fusion | flops 525312 | bytes 2103304 | tf_op jit(solution)/shard_map/while/body/eval_jaxpr/add | solution.py:146
  215.3 9.3 %constant_dynamic-slice_fusion.10 = (f32[35,20,2,128]{3,2,1,0:T(2,128)S(1)}, f32[35,20,2,128]{3,2,1,0:T(2,128)S(1)}) fusion(f32[36,20,18,130]{3,2,1,0:T(8,128)} %get-tuple-element.668, s32[]{:T(128)S(6)} %add.574, s32[]{:T(128)S(6)} %add.572), kind=kLoop, calls=%fused_computation.35.clone.1 | loop fusion | bytes 2867208 | tf_op jit(solution)/shard_map/while/body/eval_jaxpr/jit(_roll_static)/slice | solution.py:139
  225.9 15.8 %fusion.181 = (f32[36,2,128]{2,1,0:T(2,128)S(1)}, f32[36,20,2,128]{3,2,1,0:T(2,128)S(1)}) fusion(f32[2,128]{1,0:T(2,128)S(1)} %get-tuple-element.609, f32[36,19,2,128]{3,2,1,0:T(2,128)S(1)} %fusion.180, f32[1,20,2,128]{3,2,1,0:T(2,128)S(1)} %get-tuple-element.612, f32[35,20,2,128]{3,2,1,0:T(2,128)S(1)} %get-tuple-element.613, ...), kind=kLoop, calls=%fused_computation.294.clone.1 | loop fusion | flops 4414464 | bytes 6656916 | tf_op jit(solution)/shard_map/while/body/eval_jaxpr/kjrx,sk->srx/reduce_sum | solution.py:150
  243.6 9.1 %fusion.180 = f32[36,19,2,128]{3,2,1,0:T(2,128)S(1)} fusion(f32[36,20,18,130]{3,2,1,0:T(8,128)} %get-tuple-element.668, s32[]{:T(128)S(6)} %add.572, s32[]{:T(128)S(6)} %add.574, f32[2,128]{1,0:T(2,128)S(1)} %get-tuple-element.610, f32[2,128]{1,0:T(2,128)S(1)} %get-tuple-element.611), kind=kLoop, calls=%fused_computation.24.clone.1 | loop fusion | flops 525312 | bytes 2103304 | tf_op jit(solution)/shard_map/while/body/eval_jaxpr/add | solution.py:146
  252.8 9.3 %constant_dynamic-slice_fusion.10 = (f32[35,20,2,128]{3,2,1,0:T(2,128)S(1)}, f32[35,20,2,128]{3,2,1,0:T(2,128)S(1)}) fusion(f32[36,20,18,130]{3,2,1,0:T(8,128)} %get-tuple-element.668, s32[]{:T(128)S(6)} %add.574, s32[]{:T(128)S(6)} %add.572), kind=kLoop, calls=%fused_computation.35.clone.1 | loop fusion | bytes 2867208 | tf_op jit(solution)/shard_map/while/body/eval_jaxpr/jit(_roll_static)/slice | solution.py:139
  263.4 15.5 %fusion.181 = (f32[36,2,128]{2,1,0:T(2,128)S(1)}, f32[36,20,2,128]{3,2,1,0:T(2,128)S(1)}) fusion(f32[2,128]{1,0:T(2,128)S(1)} %get-tuple-element.609, f32[36,19,2,128]{3,2,1,0:T(2,128)S(1)} %fusion.180, f32[1,20,2,128]{3,2,1,0:T(2,128)S(1)} %get-tuple-element.612, f32[35,20,2,128]{3,2,1,0:T(2,128)S(1)} %get-tuple-element.613, ...), kind=kLoop, calls=%fused_computation.294.clone.1 | loop fusion | flops 4414464 | bytes 6656916 | tf_op jit(solution)/shard_map/while/body/eval_jaxpr/kjrx,sk->srx/reduce_sum | solution.py:150
  280.8 9.3 %fusion.180 = f32[36,19,2,128]{3,2,1,0:T(2,128)S(1)} fusion(f32[36,20,18,130]{3,2,1,0:T(8,128)} %get-tuple-element.668, s32[]{:T(128)S(6)} %add.572, s32[]{:T(128)S(6)} %add.574, f32[2,128]{1,0:T(2,128)S(1)} %get-tuple-element.610, f32[2,128]{1,0:T(2,128)S(1)} %get-tuple-element.611), kind=kLoop, calls=%fused_computation.24.clone.1 | loop fusion | flops 525312 | bytes 2103304 | tf_op jit(solution)/shard_map/while/body/eval_jaxpr/add | solution.py:146
  290.1 9.3 %constant_dynamic-slice_fusion.10 = (f32[35,20,2,128]{3,2,1,0:T(2,128)S(1)}, f32[35,20,2,128]{3,2,1,0:T(2,128)S(1)}) fusion(f32[36,20,18,130]{3,2,1,0:T(8,128)} %get-tuple-element.668, s32[]{:T(128)S(6)} %add.574, s32[]{:T(128)S(6)} %add.572), kind=kLoop, calls=%fused_computation.35.clone.1 | loop fusion | bytes 2867208 | tf_op jit(solution)/shard_map/while/body/eval_jaxpr/jit(_roll_static)/slice | solution.py:139
  300.9 16.1 %fusion.181 = (f32[36,2,128]{2,1,0:T(2,128)S(1)}, f32[36,20,2,128]{3,2,1,0:T(2,128)S(1)}) fusion(f32[2,128]{1,0:T(2,128)S(1)} %get-tuple-element.609, f32[36,19,2,128]{3,2,1,0:T(2,128)S(1)} %fusion.180, f32[1,20,2,128]{3,2,1,0:T(2,128)S(1)} %get-tuple-element.612, f32[35,20,2,128]{3,2,1,0:T(2,128)S(1)} %get-tuple-element.613, ...), kind=kLoop, calls=%fused_computation.294.clone.1 | loop fusion | flops 4414464 | bytes 6656916 | tf_op jit(solution)/shard_map/while/body/eval_jaxpr/kjrx,sk->srx/reduce_sum | solution.py:150
  318.8 9.3 %fusion.180 = f32[36,19,2,128]{3,2,1,0:T(2,128)S(1)} fusion(f32[36,20,18,130]{3,2,1,0:T(8,128)} %get-tuple-element.668, s32[]{:T(128)S(6)} %add.572, s32[]{:T(128)S(6)} %add.574, f32[2,128]{1,0:T(2,128)S(1)} %get-tuple-element.610, f32[2,128]{1,0:T(2,128)S(1)} %get-tuple-element.611), kind=kLoop, calls=%fused_computation.24.clone.1 | loop fusion | flops 525312 | bytes 2103304 | tf_op jit(solution)/shard_map/while/body/eval_jaxpr/add | solution.py:146
  328.1 9.3 %constant_dynamic-slice_fusion.10 = (f32[35,20,2,128]{3,2,1,0:T(2,128)S(1)}, f32[35,20,2,128]{3,2,1,0:T(2,128)S(1)}) fusion(f32[36,20,18,130]{3,2,1,0:T(8,128)} %get-tuple-element.668, s32[]{:T(128)S(6)} %add.574, s32[]{:T(128)S(6)} %add.572), kind=kLoop, calls=%fused_computation.35.clone.1 | loop fusion | bytes 2867208 | tf_op jit(solution)/shard_map/while/body/eval_jaxpr/jit(_roll_static)/slice | solution.py:139
  338.8 16.1 %fusion.181 = (f32[36,2,128]{2,1,0:T(2,128)S(1)}, f32[36,20,2,128]{3,2,1,0:T(2,128)S(1)}) fusion(f32[2,128]{1,0:T(2,128)S(1)} %get-tuple-element.609, f32[36,19,2,128]{3,2,1,0:T(2,128)S(1)} %fusion.180, f32[1,20,2,128]{3,2,1,0:T(2,128)S(1)} %get-tuple-element.612, f32[35,20,2,128]{3,2,1,0:T(2,128)S(1)} %get-tuple-element.613, ...), kind=kLoop, calls=%fused_computation.294.clone.1 | loop fusion | flops 4414464 | bytes 6656916 | tf_op jit(solution)/shard_map/while/body/eval_jaxpr/kjrx,sk->srx/reduce_sum | solution.py:150
  356.8 9.3 %fusion.180 = f32[36,19,2,128]{3,2,1,0:T(2,128)S(1)} fusion(f32[36,20,18,130]{3,2,1,0:T(8,128)} %get-tuple-element.668, s32[]{:T(128)S(6)} %add.572, s32[]{:T(128)S(6)} %add.574, f32[2,128]{1,0:T(2,128)S(1)} %get-tuple-element.610, f32[2,128]{1,0:T(2,128)S(1)} %get-tuple-element.611), kind=kLoop, calls=%fused_computation.24.clone.1 | loop fusion | flops 525312 | bytes 2103304 | tf_op jit(solution)/shard_map/while/body/eval_jaxpr/add | solution.py:146
  366.1 9.3 %constant_dynamic-slice_fusion.10 = (f32[35,20,2,128]{3,2,1,0:T(2,128)S(1)}, f32[35,20,2,128]{3,2,1,0:T(2,128)S(1)}) fusion(f32[36,20,18,130]{3,2,1,0:T(8,128)} %get-tuple-element.668, s32[]{:T(128)S(6)} %add.574, s32[]{:T(128)S(6)} %add.572), kind=kLoop, calls=%fused_computation.35.clone.1 | loop fusion | bytes 2867208 | tf_op jit(solution)/shard_map/while/body/eval_jaxpr/jit(_roll_static)/slice | solution.py:139
  376.8 16.1 %fusion.181 = (f32[36,2,128]{2,1,0:T(2,128)S(1)}, f32[36,20,2,128]{3,2,1,0:T(2,128)S(1)}) fusion(f32[2,128]{1,0:T(2,128)S(1)} %get-tuple-element.609, f32[36,19,2,128]{3,2,1,0:T(2,128)S(1)} %fusion.180, f32[1,20,2,128]{3,2,1,0:T(2,128)S(1)} %get-tuple-element.612, f32[35,20,2,128]{3,2,1,0:T(2,128)S(1)} %get-tuple-element.613, ...), kind=kLoop, calls=%fused_computation.294.clone.1 | loop fusion | flops 4414464 | bytes 6656916 | tf_op jit(solution)/shard_map/while/body/eval_jaxpr/kjrx,sk->srx/reduce_sum | solution.py:150
  394.8 9.3 %fusion.180 = f32[36,19,2,128]{3,2,1,0:T(2,128)S(1)} fusion(f32[36,20,18,130]{3,2,1,0:T(8,128)} %get-tuple-element.668, s32[]{:T(128)S(6)} %add.572, s32[]{:T(128)S(6)} %add.574, f32[2,128]{1,0:T(2,128)S(1)} %get-tuple-element.610, f32[2,128]{1,0:T(2,128)S(1)} %get-tuple-element.611), kind=kLoop, calls=%fused_computation.24.clone.1 | loop fusion | flops 525312 | bytes 2103304 | tf_op jit(solution)/shard_map/while/body/eval_jaxpr/add | solution.py:146
  404.1 9.3 %constant_dynamic-slice_fusion.10 = (f32[35,20,2,128]{3,2,1,0:T(2,128)S(1)}, f32[35,20,2,128]{3,2,1,0:T(2,128)S(1)}) fusion(f32[36,20,18,130]{3,2,1,0:T(8,128)} %get-tuple-element.668, s32[]{:T(128)S(6)} %add.574, s32[]{:T(128)S(6)} %add.572), kind=kLoop, calls=%fused_computation.35.clone.1 | loop fusion | bytes 2867208 | tf_op jit(solution)/shard_map/while/body/eval_jaxpr/jit(_roll_static)/slice | solution.py:139
  414.8 15.8 %fusion.181 = (f32[36,2,128]{2,1,0:T(2,128)S(1)}, f32[36,20,2,128]{3,2,1,0:T(2,128)S(1)}) fusion(f32[2,128]{1,0:T(2,128)S(1)} %get-tuple-element.609, f32[36,19,2,128]{3,2,1,0:T(2,128)S(1)} %fusion.180, f32[1,20,2,128]{3,2,1,0:T(2,128)S(1)} %get-tuple-element.612, f32[35,20,2,128]{3,2,1,0:T(2,128)S(1)} %get-tuple-element.613, ...), kind=kLoop, calls=%fused_computation.294.clone.1 | loop fusion | flops 4414464 | bytes 6656916 | tf_op jit(solution)/shard_map/while/body/eval_jaxpr/kjrx,sk->srx/reduce_sum | solution.py:150
  432.5 4.0 all-to-all-start.1
  448.3 3.6 collective-permute-start.10
  452.0 5.6 %collective-permute-start.11 = (f32[3,1,1536]{2,1,0:T(1,128)S(1)}, f32[3,1,1536]{2,1,0:T(1,128)S(1)}, u32[]{:S(2)}, u32[]{:S(2)}) collective-permute-start(f32[3,1,1536]{2,1,0:T(1,128)S(1)} %get-tuple-element.487), channel_id=1, source_target_pairs={{1,0},{2,1},{3,2},{4,3},{5,4},{6,5},{7,6},{8,7},{9,8},{10,9},{11,1... | collective-permute-start | bytes 55304 | tf_op jit(solution)/shard_map/ppermute | solution.py:32
  460.8 8.5 %collective-permute-start.13 = (f32[2,1,1536]{2,1,0:T(1,128)S(1)}, f32[2,1,1536]{2,1,0:T(1,128)S(1)}, u32[]{:S(2)}, u32[]{:S(2)}) collective-permute-start(f32[2,1,1536]{2,1,0:T(1,128)S(1)} %get-tuple-element.496), channel_id=1, source_target_pairs={{1,0},{2,1},{3,2},{4,3},{5,4},{6,5},{7,6},{8,7},{9,8},{10,9},{11,1... | collective-permute-start | bytes 36872 | tf_op jit(solution)/shard_map/ppermute | solution.py:32
  472.4 8.4 %collective-permute-start.15 = (f32[1,1,1536]{2,1,0:T(1,128)S(1)}, f32[1,1,1536]{2,1,0:T(1,128)S(1)}, u32[]{:S(2)}, u32[]{:S(2)}) collective-permute-start(f32[1,1,1536]{2,1,0:T(1,128)S(1)} %get-tuple-element.503), channel_id=1, source_target_pairs={{1,0},{2,1},{3,2},{4,3},{5,4},{6,5},{7,6},{8,7},{9,8},{10,9},{11,1... | collective-permute-start | bytes 18440 | tf_op jit(solution)/shard_map/ppermute | solution.py:32
  483.8 8.4 %collective-permute-start.17 = (f32[2,1,1536]{2,1,0:T(1,128)S(1)}, f32[2,1,1536]{2,1,0:T(1,128)S(1)}, u32[]{:S(2)}, u32[]{:S(2)}) collective-permute-start(f32[2,1,1536]{2,1,0:T(1,128)S(1)} %get-tuple-element.494), channel_id=1, source_target_pairs={{1,0},{2,1},{3,2},{4,3},{5,4},{6,5},{7,6},{8,7},{9,8},{10,9},{11,1... | collective-permute-start | bytes 36872 | tf_op jit(solution)/shard_map/ppermute | solution.py:32
  495.2 8.4 %collective-permute-start.19 = (f32[1,1,1536]{2,1,0:T(1,128)S(1)}, f32[1,1,1536]{2,1,0:T(1,128)S(1)}, u32[]{:S(2)}, u32[]{:S(2)}) collective-permute-start(f32[1,1,1536]{2,1,0:T(1,128)S(1)} %get-tuple-element.501), channel_id=1, source_target_pairs={{1,0},{2,1},{3,2},{4,3},{5,4},{6,5},{7,6},{8,7},{9,8},{10,9},{11,1... | collective-permute-start | bytes 18440 | tf_op jit(solution)/shard_map/ppermute | solution.py:32
  506.6 8.4 %collective-permute-start.21 = (f32[2,1,1536]{2,1,0:T(1,128)S(1)}, f32[2,1,1536]{2,1,0:T(1,128)S(1)}, u32[]{:S(2)}, u32[]{:S(2)}) collective-permute-start(f32[2,1,1536]{2,1,0:T(1,128)S(1)} %get-tuple-element.492), channel_id=1, source_target_pairs={{1,0},{2,1},{3,2},{4,3},{5,4},{6,5},{7,6},{8,7},{9,8},{10,9},{11,1... | collective-permute-start | bytes 36872 | tf_op jit(solution)/shard_map/ppermute | solution.py:32
  518.1 8.4 %collective-permute-start.23 = (f32[1,1,1536]{2,1,0:T(1,128)S(1)}, f32[1,1,1536]{2,1,0:T(1,128)S(1)}, u32[]{:S(2)}, u32[]{:S(2)}) collective-permute-start(f32[1,1,1536]{2,1,0:T(1,128)S(1)} %get-tuple-element.499), channel_id=1, source_target_pairs={{1,0},{2,1},{3,2},{4,3},{5,4},{6,5},{7,6},{8,7},{9,8},{10,9},{11,1... | collective-permute-start | bytes 18440 | tf_op jit(solution)/shard_map/ppermute | solution.py:32
  (191 shorter events, 92.8 us)
Async XLA Ops:
  3.8 17.0 %collective-permute-start = (f32[2,1,1536]{2,1,0:T(1,128)S(1)}, f32[2,1,1536]{2,1,0:T(1,128)S(1)}, u32[]{:S(2)}, u32[]{:S(2)}) collective-permute-start(f32[2,1,1536]{2,1,0:T(1,128)S(1)} %get-tuple-element.490), channel_id=1, source_target_pairs={{0,1},{1,2},{2,3},{3,4},{4,5},{5,6},{6,7},{7,8},{8,9},{9,10},{10,1... | collective-permute-start | bytes 36872 | tf_op jit(solution)/shard_map/ppermute | solution.py:30
  7.5 13.4 %collective-permute-start.1 = (f32[2,1,1536]{2,1,0:T(1,128)S(1)}, f32[2,1,1536]{2,1,0:T(1,128)S(1)}, u32[]{:S(2)}, u32[]{:S(2)}) collective-permute-start(f32[2,1,1536]{2,1,0:T(1,128)S(1)} %get-tuple-element.489), channel_id=1, source_target_pairs={{1,0},{2,1},{3,2},{4,3},{5,4},{6,5},{7,6},{8,7},{9,8},{10,9},{11,1... | collective-permute-start | bytes 36872 | tf_op jit(solution)/shard_map/ppermute | solution.py:32
  10.2 26.6 %collective-permute-start.6 = (f32[2,1,1536]{2,1,0:T(1,128)S(1)}, f32[2,1,1536]{2,1,0:T(1,128)S(1)}, u32[]{:S(2)}, u32[]{:S(2)}) collective-permute-start(f32[2,1,1536]{2,1,0:T(1,128)S(1)} %get-tuple-element.497), channel_id=1, source_target_pairs={{0,1},{1,2},{2,3},{3,4},{4,5},{5,6},{6,7},{7,8},{8,9},{9,10},{10,1... | collective-permute-start | bytes 36872 | tf_op jit(solution)/shard_map/ppermute | solution.py:30
  13.8 23.0 %collective-permute-start.7 = (f32[2,1,1536]{2,1,0:T(1,128)S(1)}, f32[2,1,1536]{2,1,0:T(1,128)S(1)}, u32[]{:S(2)}, u32[]{:S(2)}) collective-permute-start(f32[2,1,1536]{2,1,0:T(1,128)S(1)} %get-tuple-element.498), channel_id=1, source_target_pairs={{1,0},{2,1},{3,2},{4,3},{5,4},{6,5},{7,6},{8,7},{9,8},{10,9},{11,1... | collective-permute-start | bytes 36872 | tf_op jit(solution)/shard_map/ppermute | solution.py:32
  27.6 13.9 %all-to-all-start = ((f32[8,1,768]{2,1,0:T(1,128)}), f32[8,1,768]{2,1,0:T(1,128)S(1)}, u32[]{:S(2)}, u32[]{:S(2)}) async-start(f32[8,1,768]{2,1,0:T(1,128)} %reshape.273), calls=%async_computation | async-start | bytes 49152 | tf_op jit(solution)/shard_map/all_to_all | solution.py:171
  52.4 14.8 %copy-start = (f32[36,20,16,128]{3,2,1,0:T(8,128)}, f32[36,20,16,128]{3,2,1,0:T(8,128)S(1)}, u32[]{:S(2)}) copy-start(f32[36,20,16,128]{3,2,1,0:T(8,128)S(1)} %broadcast_multiply_fusion) | copy-start | bytes 17694724
  52.9 13.4 %collective-permute-start.2 = (f32[36,20,1,128]{3,2,1,0:T(1,128)S(1)}, f32[36,20,1,128]{3,2,1,0:T(1,128)S(1)}, u32[]{:S(2)}, u32[]{:S(2)}) collective-permute-start(f32[36,20,1,128]{3,2,1,0:T(1,128)S(1)} %get-tuple-element.452), channel_id=1, source_target_pairs={{0,8},{8,16},{16,24},{24,32},{32,40},{40,48},{48,56},{56,64},{64,7... | collective-permute-start | bytes 1105928 | tf_op jit(solution)/shard_map/ppermute | solution.py:30
  54.9 12.3 %collective-permute-start.3 = (f32[36,20,1,128]{3,2,1,0:T(1,128)S(1)}, f32[36,20,1,128]{3,2,1,0:T(1,128)S(1)}, u32[]{:S(2)}, u32[]{:S(2)}) collective-permute-start(f32[36,20,1,128]{3,2,1,0:T(1,128)S(1)} %get-tuple-element.453), channel_id=1, source_target_pairs={{8,0},{16,8},{24,16},{32,24},{40,32},{48,40},{56,48},{64,56},{72,6... | collective-permute-start | bytes 1105928 | tf_op jit(solution)/shard_map/ppermute | solution.py:32
  82.1 13.2 %collective-permute-start.4 = (f32[36,20,18,1]{0,3,2,1:T(1,128)S(1)}, f32[36,20,18,1]{0,3,2,1:T(1,128)}, u32[]{:S(2)}, u32[]{:S(2)}) collective-permute-start(f32[36,20,18,1]{0,3,2,1:T(1,128)S(1)} %copy.100), channel_id=1, source_target_pairs={{0,1},{1,2},{2,3},{3,4},{4,5},{5,6},{6,7},{8,9},{9,10},{10,11},{11... | collective-permute-start | bytes 155528 | tf_op jit(solution)/shard_map/ppermute | solution.py:30
  92.4 9.4 %collective-permute-start.5 = (f32[36,20,18,1]{0,3,2,1:T(1,128)}, f32[36,20,18,1]{0,3,2,1:T(1,128)}, u32[]{:S(2)}, u32[]{:S(2)}) collective-permute-start(f32[36,20,18,1]{0,3,2,1:T(1,128)} %copy.101), channel_id=1, source_target_pairs={{1,0},{2,1},{3,2},{4,3},{5,4},{6,5},{7,6},{9,8},{10,9},{11,10},{12... | collective-permute-start | bytes 155528 | tf_op jit(solution)/shard_map/ppermute | solution.py:32
  432.5 9.7 %all-to-all-start.1 = ((f32[3,16,128]{2,0,1:T(4,128)}), f32[3,16,128]{2,0,1:T(4,128)S(1)}, u32[]{:S(2)}, u32[]{:S(2)}) async-start(f32[3,16,128]{2,0,1:T(4,128)} %get-tuple-element.264), calls=%async_computation.1 | async-start | bytes 65536 | tf_op jit(solution)/shard_map/all_to_all | solution.py:206
  436.5 21.1 %collective-permute-start.8 = (f32[1,1,1536]{2,1,0:T(1,128)S(1)}, f32[1,1,1536]{2,1,0:T(1,128)S(1)}, u32[]{:S(2)}, u32[]{:S(2)}) collective-permute-start(f32[1,1,1536]{2,1,0:T(1,128)S(1)} %get-tuple-element.509), channel_id=1, source_target_pairs={{0,1},{1,2},{2,3},{3,4},{4,5},{5,6},{6,7},{7,8},{8,9},{9,10},{10,1... | collective-permute-start | bytes 18440 | tf_op jit(solution)/shard_map/ppermute | solution.py:30
  440.0 17.5 %collective-permute-start.9 = (f32[1,1,1536]{2,1,0:T(1,128)S(1)}, f32[1,1,1536]{2,1,0:T(1,128)S(1)}, u32[]{:S(2)}, u32[]{:S(2)}) collective-permute-start(f32[1,1,1536]{2,1,0:T(1,128)S(1)} %get-tuple-element.508), channel_id=1, source_target_pairs={{1,0},{2,1},{3,2},{4,3},{5,4},{6,5},{7,6},{8,7},{9,8},{10,9},{11,1... | collective-permute-start | bytes 18440 | tf_op jit(solution)/shard_map/ppermute | solution.py:32
  445.7 13.1 %copy-start.1 = (f32[3,1536]{1,0:T(4,128)S(1)}, f32[3,1536]{1,0:T(4,128)}, u32[]{:S(2)}) copy-start(f32[3,1536]{1,0:T(4,128)} %param.9) | copy-start | bytes 55300
  448.3 9.4 %collective-permute-start.10 = (f32[3,1,1536]{2,1,0:T(1,128)S(1)}, f32[3,1,1536]{2,1,0:T(1,128)S(1)}, u32[]{:S(2)}, u32[]{:S(2)}) collective-permute-start(f32[3,1,1536]{2,1,0:T(1,128)S(1)} %get-tuple-element.488), channel_id=1, source_target_pairs={{0,1},{1,2},{2,3},{3,4},{4,5},{5,6},{6,7},{7,8},{8,9},{9,10},{10,1... | collective-permute-start | bytes 55304 | tf_op jit(solution)/shard_map/ppermute | solution.py:30
  452.0 6.4 %collective-permute-start.11 = (f32[3,1,1536]{2,1,0:T(1,128)S(1)}, f32[3,1,1536]{2,1,0:T(1,128)S(1)}, u32[]{:S(2)}, u32[]{:S(2)}) collective-permute-start(f32[3,1,1536]{2,1,0:T(1,128)S(1)} %get-tuple-element.487), channel_id=1, source_target_pairs={{1,0},{2,1},{3,2},{4,3},{5,4},{6,5},{7,6},{8,7},{9,8},{10,9},{11,1... | collective-permute-start | bytes 55304 | tf_op jit(solution)/shard_map/ppermute | solution.py:32
  458.9 10.4 %collective-permute-start.12 = (f32[2,1,1536]{2,1,0:T(1,128)S(1)}, f32[2,1,1536]{2,1,0:T(1,128)S(1)}, u32[]{:S(2)}, u32[]{:S(2)}) collective-permute-start(f32[2,1,1536]{2,1,0:T(1,128)S(1)} %get-tuple-element.495), channel_id=1, source_target_pairs={{0,1},{1,2},{2,3},{3,4},{4,5},{5,6},{6,7},{7,8},{8,9},{9,10},{10,1... | collective-permute-start | bytes 36872 | tf_op jit(solution)/shard_map/ppermute | solution.py:30
  460.8 9.3 %collective-permute-start.13 = (f32[2,1,1536]{2,1,0:T(1,128)S(1)}, f32[2,1,1536]{2,1,0:T(1,128)S(1)}, u32[]{:S(2)}, u32[]{:S(2)}) collective-permute-start(f32[2,1,1536]{2,1,0:T(1,128)S(1)} %get-tuple-element.496), channel_id=1, source_target_pairs={{1,0},{2,1},{3,2},{4,3},{5,4},{6,5},{7,6},{8,7},{9,8},{10,9},{11,1... | collective-permute-start | bytes 36872 | tf_op jit(solution)/shard_map/ppermute | solution.py:32
  470.4 10.4 %collective-permute-start.14 = (f32[1,1,1536]{2,1,0:T(1,128)S(1)}, f32[1,1,1536]{2,1,0:T(1,128)S(1)}, u32[]{:S(2)}, u32[]{:S(2)}) collective-permute-start(f32[1,1,1536]{2,1,0:T(1,128)S(1)} %get-tuple-element.504), channel_id=1, source_target_pairs={{0,1},{1,2},{2,3},{3,4},{4,5},{5,6},{6,7},{7,8},{8,9},{9,10},{10,1... | collective-permute-start | bytes 18440 | tf_op jit(solution)/shard_map/ppermute | solution.py:30
  472.4 9.2 %collective-permute-start.15 = (f32[1,1,1536]{2,1,0:T(1,128)S(1)}, f32[1,1,1536]{2,1,0:T(1,128)S(1)}, u32[]{:S(2)}, u32[]{:S(2)}) collective-permute-start(f32[1,1,1536]{2,1,0:T(1,128)S(1)} %get-tuple-element.503), channel_id=1, source_target_pairs={{1,0},{2,1},{3,2},{4,3},{5,4},{6,5},{7,6},{8,7},{9,8},{10,9},{11,1... | collective-permute-start | bytes 18440 | tf_op jit(solution)/shard_map/ppermute | solution.py:32
  481.9 10.3 %collective-permute-start.16 = (f32[2,1,1536]{2,1,0:T(1,128)S(1)}, f32[2,1,1536]{2,1,0:T(1,128)S(1)}, u32[]{:S(2)}, u32[]{:S(2)}) collective-permute-start(f32[2,1,1536]{2,1,0:T(1,128)S(1)} %get-tuple-element.493), channel_id=1, source_target_pairs={{0,1},{1,2},{2,3},{3,4},{4,5},{5,6},{6,7},{7,8},{8,9},{9,10},{10,1... | collective-permute-start | bytes 36872 | tf_op jit(solution)/shard_map/ppermute | solution.py:30
  483.8 9.2 %collective-permute-start.17 = (f32[2,1,1536]{2,1,0:T(1,128)S(1)}, f32[2,1,1536]{2,1,0:T(1,128)S(1)}, u32[]{:S(2)}, u32[]{:S(2)}) collective-permute-start(f32[2,1,1536]{2,1,0:T(1,128)S(1)} %get-tuple-element.494), channel_id=1, source_target_pairs={{1,0},{2,1},{3,2},{4,3},{5,4},{6,5},{7,6},{8,7},{9,8},{10,9},{11,1... | collective-permute-start | bytes 36872 | tf_op jit(solution)/shard_map/ppermute | solution.py:32
  493.3 10.4 %collective-permute-start.18 = (f32[1,1,1536]{2,1,0:T(1,128)S(1)}, f32[1,1,1536]{2,1,0:T(1,128)S(1)}, u32[]{:S(2)}, u32[]{:S(2)}) collective-permute-start(f32[1,1,1536]{2,1,0:T(1,128)S(1)} %get-tuple-element.502), channel_id=1, source_target_pairs={{0,1},{1,2},{2,3},{3,4},{4,5},{5,6},{6,7},{7,8},{8,9},{9,10},{10,1... | collective-permute-start | bytes 18440 | tf_op jit(solution)/shard_map/ppermute | solution.py:30
  495.2 9.2 %collective-permute-start.19 = (f32[1,1,1536]{2,1,0:T(1,128)S(1)}, f32[1,1,1536]{2,1,0:T(1,128)S(1)}, u32[]{:S(2)}, u32[]{:S(2)}) collective-permute-start(f32[1,1,1536]{2,1,0:T(1,128)S(1)} %get-tuple-element.501), channel_id=1, source_target_pairs={{1,0},{2,1},{3,2},{4,3},{5,4},{6,5},{7,6},{8,7},{9,8},{10,9},{11,1... | collective-permute-start | bytes 18440 | tf_op jit(solution)/shard_map/ppermute | solution.py:32
  504.7 10.3 %collective-permute-start.20 = (f32[2,1,1536]{2,1,0:T(1,128)S(1)}, f32[2,1,1536]{2,1,0:T(1,128)S(1)}, u32[]{:S(2)}, u32[]{:S(2)}) collective-permute-start(f32[2,1,1536]{2,1,0:T(1,128)S(1)} %get-tuple-element.491), channel_id=1, source_target_pairs={{0,1},{1,2},{2,3},{3,4},{4,5},{5,6},{6,7},{7,8},{8,9},{9,10},{10,1... | collective-permute-start | bytes 36872 | tf_op jit(solution)/shard_map/ppermute | solution.py:30
  506.6 9.2 %collective-permute-start.21 = (f32[2,1,1536]{2,1,0:T(1,128)S(1)}, f32[2,1,1536]{2,1,0:T(1,128)S(1)}, u32[]{:S(2)}, u32[]{:S(2)}) collective-permute-start(f32[2,1,1536]{2,1,0:T(1,128)S(1)} %get-tuple-element.492), channel_id=1, source_target_pairs={{1,0},{2,1},{3,2},{4,3},{5,4},{6,5},{7,6},{8,7},{9,8},{10,9},{11,1... | collective-permute-start | bytes 36872 | tf_op jit(solution)/shard_map/ppermute | solution.py:32
  516.2 10.4 %collective-permute-start.22 = (f32[1,1,1536]{2,1,0:T(1,128)S(1)}, f32[1,1,1536]{2,1,0:T(1,128)S(1)}, u32[]{:S(2)}, u32[]{:S(2)}) collective-permute-start(f32[1,1,1536]{2,1,0:T(1,128)S(1)} %get-tuple-element.500), channel_id=1, source_target_pairs={{0,1},{1,2},{2,3},{3,4},{4,5},{5,6},{6,7},{7,8},{8,9},{9,10},{10,1... | collective-permute-start | bytes 18440 | tf_op jit(solution)/shard_map/ppermute | solution.py:30
  518.1 9.2 %collective-permute-start.23 = (f32[1,1,1536]{2,1,0:T(1,128)S(1)}, f32[1,1,1536]{2,1,0:T(1,128)S(1)}, u32[]{:S(2)}, u32[]{:S(2)}) collective-permute-start(f32[1,1,1536]{2,1,0:T(1,128)S(1)} %get-tuple-element.499), channel_id=1, source_target_pairs={{1,0},{2,1},{3,2},{4,3},{5,4},{6,5},{7,6},{8,7},{9,8},{10,9},{11,1... | collective-permute-start | bytes 18440 | tf_op jit(solution)/shard_map/ppermute | solution.py:32
where the time goes:
time: 535 us; the launch traced here: 528 us
  other arithmetic  235 us (44%)
  local copies, waits for them, and re-layouts  149 us (28%)
  starting transfers between devices  120 us (22%)
  waiting for transfers between devices  16.6 us (3%)
  matrix products  5.86 us (1%)
    reduce_sum x8, other arithmetic, wave_update(): jnp.einsum('kjrx,sk->srx', updated, stress_table, precision=lax.Precision...  127 us
    slice x16, local copies, waits for them, and re-layouts, wave_update(): jnp.roll(masked, 1, axis=0)  84 us
    ppermute x12, starting transfers between devices, extended(): lax.ppermute(head, axis, [((i + 1) % count, i) for i in range(ends)])  74.5 us
    add x8, other arithmetic, wave_update(): faces = shift_pos * masked[:, :-1] + shift_neg * masked[:, 1:]  73.7 us
    ppermute x12, starting transfers between devices, extended(): lax.ppermute(tail, axis, [(i, (i + 1) % count) for i in range(ends)])  32 us
    concatenate x12, other arithmetic, extended(): jnp.concatenate([lax.ppermute(tail, axis, [(i, (i + 1) % count) for i in...  22 us
    slice x3, local copies, waits for them, and re-layouts, extended(): lax.slice_in_dim(cells, cells.shape[dim] - width, cells.shape[dim], axis=...  13.8 us
  transfers between devices with their start and end apart: 26, of which 10 were waited for; matrix products, arithmetic and copies ran while one was open for 5% of the time, Pallas kernels for 0%

commit v1 on v0

v1 whole, which is shorter than its diff:
```python
import functools
import math

import jax
import jax.numpy as jnp
from jax import lax
from jax.experimental import pallas as pl
from jax.experimental.pallas import tpu as pltpu
from jax.sharding import PartitionSpec as P

ITERS = 4
GRAVITY_STEP = 0.3
CORIOLIS_STEP = 0.2
STRESS_GAIN = 2.0
TURN_GAIN = 0.2
SPEED_BASE = 0.35
SPEED_RATIO = 0.9

NDIR = 36
NFREQ = 20
ROWS = 16
LANES = 128
CELLS = NDIR * NFREQ * ROWS
PER_DIR = NFREQ * ROWS
QUARTER = NDIR // 4
HALF = NDIR // 2 * NFREQ
PEERS = 8
SLOTS = 16
MARGIN_O = 24
MARGIN_W = 16
SPEEDS = [SPEED_BASE * SPEED_RATIO**j for j in range(NFREQ)]
STEP_ANGLE = 2.0 * math.pi / NDIR
MESH = pl.DeviceIdType.MESH
AROUND = [(1, 0), (-1, 0), (0, 1), (0, -1), (1, 1), (1, -1), (-1, 1), (-1, -1)]


def iota(shape, dim):
    return lax.broadcasted_iota(jnp.int32, shape, dim)


def next_angle(cosine, sine):
    turn_c, turn_s = math.cos(STEP_ANGLE), math.sin(STEP_ANGLE)
    return cosine * turn_c - sine * turn_s, sine * turn_c + cosine * turn_s


def first_angle():
    return jnp.float32(math.cos(0.5 * STEP_ANGLE)), jnp.float32(math.sin(0.5 * STEP_ANGLE))


def exact_dot(values, weights):
    rows = values.shape[0]
    high = values.astype(jnp.bfloat16)
    rest = values - high.astype(jnp.float32)
    middle = rest.astype(jnp.bfloat16)
    low = (rest - middle.astype(jnp.float32)).astype(jnp.bfloat16)
    stacked = jnp.concatenate([high, middle, low], axis=0)
    product = jnp.dot(stacked, weights, preferred_element_type=jnp.float32)
    return product[:rows] + product[rows : 2 * rows] + product[2 * rows :]


def ocean_shift(values, amount):
    return pltpu.roll(values, amount % values.shape[1], 1)


def along_x(values):
    return (ocean_shift(values, -1) - ocean_shift(values, 1)) * 0.5


def along_y(classes):
    above = [classes[1], classes[2], pltpu.roll(classes[0], SLOTS - 1, 0)]
    below = [pltpu.roll(classes[2], 1, 0), classes[0], classes[1]]
    return [(above[c] - below[c]) * 0.5 for c in range(3)]


def coupled_kernel(
    groups_y,
    groups,
    spectrum,
    sea_mask,
    ocean_state,
    depth,
    ocean_out,
    fields_out,
    rows_out,
    cols_out,
    cells,
    raw,
    raw_mask,
    pack,
    window,
    flux,
    flux_cols,
    flux_rows,
    stress,
    result,
    result_send,
    result_land,
    rows_send,
    cols_send,
    load_sem,
    pack_sem,
    band_sem,
    flux_sem,
    stress_sem,
    result_sem,
    halo_sem,
    local_sem,
):
    x = lax.axis_index("gx")
    y = lax.axis_index("sec") * groups_y + lax.axis_index("gy")

    def exists(dy, dx):
        checks = []
        if dy > 0:
            checks.append(y < groups - 1)
        if dy < 0:
            checks.append(y > 0)
        if dx > 0:
            checks.append(x < PEERS - 1)
        if dx < 0:
            checks.append(x > 0)
        answer = checks[0]
        for check in checks[1:]:
            answer = jnp.logical_and(answer, check)
        return answer

    def device(dy, dx):
        row = y + dy
        return (row // groups_y, lax.rem(row, groups_y), x + dx)

    def peer(step):
        return (lax.axis_index("sec"), lax.axis_index("gy"), lax.rem(x + step, PEERS))

    def load(direction):
        span = pl.ds(pl.multiple_of(direction * PER_DIR, PER_DIR), PER_DIR)
        return pltpu.make_async_copy(spectrum.at[span], cells.at[span], load_sem.at[direction])

    def start_load(i, carry):
        for q in range(4):
            load(q * QUARTER + i).start()
        return carry

    lax.fori_loop(0, QUARTER, start_load, 0)

    barrier = pltpu.get_barrier_semaphore()
    for step in range(1, PEERS):
        pl.semaphore_signal(barrier, inc=1, device_id=peer(step), device_id_type=MESH)
    greeted = PEERS - 1
    for dy, dx in AROUND:
        if dy != 0:
            here = exists(dy, dx)

            @pl.when(here)
            def _():
                pl.semaphore_signal(barrier, inc=1, device_id=device(dy, dx), device_id_type=MESH)

            greeted = greeted + here.astype(jnp.int32)

    raw[...] = jnp.zeros_like(raw)
    raw_mask[...] = jnp.zeros_like(raw_mask)
    width = ocean_state.shape[2]
    for f in range(3):
        raw[3 * f : 3 * f + 3, :width] = ocean_state[f]
    raw[9:12, :width] = depth[...]
    raw_mask[12:14, : sea_mask.shape[1]] = sea_mask[...].astype(jnp.float32)
    even = ocean_shift(raw[...], MARGIN_O)
    odd = ocean_shift(raw[...], MARGIN_O - 64)
    mask_rows = ocean_shift(raw_mask[...], MARGIN_W)
    is_ocean = iota((SLOTS, LANES), 0) < 12
    for dest in range(PEERS):
        source = odd if dest % 2 else even
        origin = 384 * (dest // 2) + (128 if dest % 2 else 0)
        for tile in range(2):
            pack[dest, tile] = jnp.where(
                is_ocean,
                source[:, origin + LANES * tile : origin + LANES * (tile + 1)],
                mask_rows[:, LANES * (dest + tile) : LANES * (dest + tile + 1)],
            )

    slab = jnp.zeros((2, 2 * SLOTS, LANES), jnp.float32)
    window[:, 11 * SLOTS : 13 * SLOTS, :] = slab
    edge = jnp.zeros((2, 3 * SLOTS, LANES), jnp.float32)

    @pl.when(y == 0)
    def _():
        window[:, 13 * SLOTS : 16 * SLOTS, :] = edge
        flux_rows[0] = jnp.zeros((3, 8, LANES), jnp.float32)
        stress[:, :, 24:32, :] = jnp.zeros((3, 3, 8, LANES), jnp.float32)

    @pl.when(y == groups - 1)
    def _():
        window[:, 8 * SLOTS : 11 * SLOTS, :] = edge
        flux_rows[1] = jnp.zeros((3, 8, LANES), jnp.float32)
        stress[:, :, 16:24, :] = jnp.zeros((3, 3, 8, LANES), jnp.float32)

    @pl.when(x == 0)
    def _():
        flux_cols[0] = jnp.zeros((3, ROWS, LANES), jnp.float32)
        stress[2] = jnp.zeros((3, 32, LANES), jnp.float32)

    @pl.when(x == PEERS - 1)
    def _():
        flux_cols[1] = jnp.zeros((3, ROWS, LANES), jnp.float32)
        stress[1] = jnp.zeros((3, 32, LANES), jnp.float32)

    mine = pl.ds(pl.multiple_of(x * SLOTS, SLOTS), SLOTS)

    def pack_copy(step):
        dest = peer(step)
        return pltpu.make_async_remote_copy(
            src_ref=pack.at[dest[2]],
            dst_ref=window.at[:, mine, :],
            send_sem=pack_sem.at[0, step],
            recv_sem=pack_sem.at[1, step],
            device_id=dest,
            device_id_type=MESH,
        )

    pl.semaphore_wait(barrier, greeted)
    for step in range(1, PEERS):
        pack_copy(step).start()
    window[:, mine, :] = pack[x]

    def sums(direction):
        base = direction * PER_DIR
        total = weighted = None
        for j in range(NFREQ):
            value = cells[pl.ds(pl.multiple_of(base + j * ROWS, ROWS), ROWS), :]
            total = value if j == 0 else total + value
            scaled = value * SPEEDS[j]
            weighted = scaled if j == 0 else weighted + scaled
        return total, weighted

    def gather(i, carry):
        (cosine, sine), plain, fluxes = carry
        for q in range(4):
            load(q * QUARTER + i).wait()
        scale = 0.5 / (NDIR * NFREQ)
        cc, cs, ss = cosine * cosine * scale, cosine * sine * scale, sine * sine * scale
        totals, weighted = zip(*[sums(q * QUARTER + i) for q in range(4)])
        pair = (totals[0] + totals[2]) - (totals[1] + totals[3])
        plain = (
            plain[0] + ((totals[0] + totals[2]) + (totals[1] + totals[3])),
            plain[1] + (cc - ss) * pair,
            plain[2] + (2.0 * cs) * pair,
        )
        straight, crossed = (cc, cs, ss), (ss, -cs, cc)
        west, east, south, north = fluxes
        west = tuple(
            west[s] + (cosine * straight[s]) * weighted[0] + (sine * crossed[s]) * weighted[3] for s in range(3)
        )
        east = tuple(
            east[s] + (cosine * straight[s]) * weighted[2] + (sine * crossed[s]) * weighted[1] for s in range(3)
        )
        south = tuple(
            south[s] + (sine * straight[s]) * weighted[0] + (cosine * crossed[s]) * weighted[1] for s in range(3)
        )
        north = tuple(
            north[s] + (sine * straight[s]) * weighted[2] + (cosine * crossed[s]) * weighted[3] for s in range(3)
        )
        return next_angle(cosine, sine), plain, (west, east, south, north)

    zero = jnp.zeros((ROWS, LANES), jnp.float32)
    triple = (zero, zero, zero)
    state = (first_angle(), triple, (triple, triple, triple, triple))
    state = lax.fori_loop(0, QUARTER // 2, gather, state)

    for step in range(1, PEERS):
        pack_copy(step).wait_recv()

    def band_copy(n):
        dy = 1 if n == 0 else -1
        source = pl.ds((5 if n == 0 else 0) * SLOTS, 3 * SLOTS)
        target = pl.ds((13 if n == 0 else 8) * SLOTS, 3 * SLOTS)
        return pltpu.make_async_remote_copy(
            src_ref=window.at[:, source, :],
            dst_ref=window.at[:, target, :],
            send_sem=band_sem.at[0, n],
            recv_sem=band_sem.at[1, n],
            device_id=device(dy, 0),
            device_id_type=MESH,
        )

    vertical = (exists(1, 0), exists(-1, 0))
    from_side = (exists(-1, 0), exists(1, 0))
    for n in range(2):

        @pl.when(vertical[n])
        def _():
            band_copy(n).start()

    _, plain, fluxes = lax.fori_loop(QUARTER // 2, QUARTER, gather, state)
    for side in range(4):
        for s in range(3):
            flux[side, s] = fluxes[side][s]

    def flux_copy(n):
        if n < 2:
            source, target, dest = flux.at[n], flux_cols.at[n], device(0, 1 if n == 0 else -1)
        else:
            span = pl.ds(8 if n == 2 else 0, 8)
            source, target, dest = flux.at[n, :, span, :], flux_rows.at[n - 2], device(1 if n == 2 else -1, 0)
        return pltpu.make_async_remote_copy(
            src_ref=source,
            dst_ref=target,
            send_sem=flux_sem.at[0, n],
            recv_sem=flux_sem.at[1, n],
            device_id=dest,
            device_id_type=MESH,
        )

    sends = (exists(0, 1), exists(0, -1), exists(1, 0), exists(-1, 0))
    receives = (exists(0, -1), exists(0, 1), exists(-1, 0), exists(1, 0))
    for n in range(4):

        @pl.when(sends[n])
        def _():
            flux_copy(n).start()

    lane = iota((ROWS, LANES), 1)

    def pack_rows(n, carry):
        span = pl.ds(pl.multiple_of(n * 8, 8), 8)
        rows_send[0, span, :] = cells[pl.ds(n * (8 * ROWS) + (ROWS - 1), 8, stride=ROWS), :]
        rows_send[1, span, :] = cells[pl.ds(n * (8 * ROWS) + HALF * ROWS, 8, stride=ROWS), :]
        return carry

    lax.fori_loop(0, HALF // 8, pack_rows, 0)

    def edge_lanes(direction, last):
        base = direction * PER_DIR
        tile = zero
        for j in range(NFREQ):
            value = cells[pl.ds(pl.multiple_of(base + j * ROWS, ROWS), ROWS), :]
            tile = jnp.where(lane == j, pltpu.roll(value, (j + 1 if last else j) % LANES, 1) if (last or j) else value, tile)
        return tile

    def pack_cols(n, carry):
        group, part = n // 6, lax.rem(n, 6)
        eastward = jnp.where(n < QUARTER, n, n + 2 * QUARTER)
        shift = part * NFREQ
        keep = part > 0
        cols_send[0, group] = jnp.where(keep, cols_send[0, group], zero) + pltpu.roll(edge_lanes(eastward, True), shift, 1)
        cols_send[1, group] = jnp.where(keep, cols_send[1, group], zero) + pltpu.roll(
            edge_lanes(n + QUARTER, False), shift, 1
        )
        return carry

    cols_send[...] = jnp.zeros_like(cols_send)
    lax.fori_loop(0, 2 * QUARTER, pack_cols, 0)

    def halo_copy(n):
        source = cols_send.at[n] if n < 2 else rows_send.at[n - 2]
        target = cols_out.at[n] if n < 2 else rows_out.at[n - 2]
        dest = (device(0, 1), device(0, -1), device(1, 0), device(-1, 0))[n]
        return pltpu.make_async_remote_copy(
            src_ref=source,
            dst_ref=target,
            send_sem=halo_sem.at[0, n],
            recv_sem=halo_sem.at[1, n],
            device_id=dest,
            device_id_type=MESH,
        )

    def halo_fill(n):
        source = cols_send.at[n] if n < 2 else rows_send.at[n - 2]
        target = cols_out.at[n] if n < 2 else rows_out.at[n - 2]
        return pltpu.make_async_copy(source, target, local_sem.at[n])

    for n in range(4):

        @pl.when(sends[n])
        def _():
            halo_copy(n).start()

        @pl.when(jnp.logical_not(receives[n]))
        def _():
            halo_fill(n).start()

    for n in range(2):

        @pl.when(from_side[n])
        def _():
            band_copy(n).wait_recv()

    def window_rows(first):
        return jnp.concatenate([window[t, pl.ds(first, SLOTS, stride=SLOTS), :] for t in range(2)], axis=1)

    wide = (2 * LANES, 2 * LANES)
    wave_masks = [window_rows(12), window_rows(13)]
    spread = (iota(wide, 0) == (2 * iota(wide, 1)) // 3).astype(jnp.bfloat16)
    masks = jnp.dot(
        jnp.concatenate(wave_masks, axis=0).astype(jnp.bfloat16), spread, preferred_element_type=jnp.float32
    )
    ocean_mask = [masks[:SLOTS], masks[:SLOTS], masks[SLOTS:]]
    surface = [window_rows(c) * ocean_mask[c] for c in range(3)]
    eastward = [window_rows(3 + c) * ocean_mask[c] for c in range(3)]
    northward = [window_rows(6 + c) * ocean_mask[c] for c in range(3)]
    bottom = [window_rows(9 + c) for c in range(3)]

    east_y, north_y = along_y(eastward), along_y(northward)
    vorticity = [along_x(northward[c]) - east_y[c] for c in range(3)]
    divergence = [along_x(eastward[c]) + north_y[c] for c in range(3)]
    coarse = []
    for field in (vorticity, divergence):
        coarse.append((2.0 * field[0] + field[1])[:8])
        coarse.append((field[1] + 2.0 * field[2])[:8])
    narrow = (2 * LANES, LANES)
    fine, wave = iota(narrow, 0), iota(narrow, 1) + MARGIN_W
    group = 3 * (wave // 2)
    ends = jnp.where(wave % 2 == 0, group, group + 2)
    weights = jnp.where(fine == ends, 2.0, jnp.where(fine == group + 1, 1.0, 0.0)).astype(jnp.bfloat16)
    coarse = exact_dot(jnp.concatenate(coarse, axis=0), weights) * (1.0 / 9.0)
    for n in range(2):
        for c in range(2):
            place = pl.ds(ROWS * n + c, 8, stride=2)
            fields_out[place, :] = TURN_GAIN * jnp.tanh(coarse[16 * n + 8 * c : 16 * n + 8 * c + 8])

    center = [ocean_shift(wave_masks[c], -MARGIN_W)[:, :LANES] for c in range(2)]
    west_mask = [ocean_shift(wave_masks[c], 1 - MARGIN_W)[:, :LANES] for c in range(2)]
    east_mask = [ocean_shift(wave_masks[c], -1 - MARGIN_W)[:, :LANES] for c in range(2)]
    south_mask = [pltpu.roll(center[1], 1, 0), center[0]]
    north_mask = [center[1], pltpu.roll(center[0], SLOTS - 1, 0)]
    for c in range(2):
        fields_out[pl.ds(2 * ROWS + c, 8, stride=2), :] = center[c][:8]
        for n, other in enumerate((west_mask, east_mask, south_mask, north_mask)):
            fields_out[pl.ds((3 + n) * ROWS + c, 8, stride=2), :] = (center[c] * other[c])[:8]

    def field(n):
        return fields_out[ROWS * n : ROWS * (n + 1), :]

    turning = field(0)
    turn_abs = jnp.abs(turning)
    wave_mask = field(2)
    scale = 0.25 / (NDIR * NFREQ)
    base, along, across = plain[0] * scale, plain[1] * 0.5, plain[2] * 0.5
    turn_c, turn_s = math.cos(2.0 * STEP_ANGLE), math.sin(2.0 * STEP_ANGLE)
    signed = jnp.where(turning > 0.0, turn_s, -turn_s)
    along_turn = along * turn_c - across * signed
    across_turn = across * turn_c + along * signed
    stay = 1.0 - turn_abs
    along = stay * along + turn_abs * along_turn
    across = stay * across + turn_abs * across_turn
    local = [base + along, across, base - along]
    local = [local[s] - ((fluxes[0][s] + fluxes[1][s]) + (fluxes[2][s] + fluxes[3][s])) for s in range(3)]

    for n in range(4):

        @pl.when(receives[n])
        def _():
            flux_copy(n).wait_recv()

    row = iota((ROWS, LANES), 0)
    for s in range(3):
        from_west = jnp.where(lane == 0, pltpu.roll(flux_cols[0, s], 1, 1), pltpu.roll(fluxes[0][s], 1, 1))
        from_east = jnp.where(
            lane == LANES - 1, pltpu.roll(flux_cols[1, s], LANES - 1, 1), pltpu.roll(fluxes[1][s], LANES - 1, 1)
        )
        from_south = jnp.where(row == 0, flux_rows[0, s, 7:8, :], pltpu.roll(fluxes[2][s], 1, 0))
        from_north = jnp.where(row == ROWS - 1, flux_rows[1, s, 0:1, :], pltpu.roll(fluxes[3][s], ROWS - 1, 0))
        stress[0, s, 0:ROWS, :] = (
            wave_mask * local[s]
            + field(3) * from_west
            + field(4) * from_east
            + field(5) * from_south
            + field(6) * from_north
        )

    def stress_copy(n):
        dy, dx = AROUND[n]
        source = pl.ds({0: 0, 1: 8, -1: 0}[dy], 16 if dy == 0 else 8)
        target = pl.ds({0: 0, 1: 24, -1: 16}[dy], 16 if dy == 0 else 8)
        return pltpu.make_async_remote_copy(
            src_ref=stress.at[0, :, source, :],
            dst_ref=stress.at[{0: 0, 1: 2, -1: 1}[dx], :, target, :],
            send_sem=stress_sem.at[0, n],
            recv_sem=stress_sem.at[1, n],
            device_id=device(dy, dx),
            device_id_type=MESH,
        )

    for n, (dy, dx) in enumerate(AROUND):

        @pl.when(exists(dy, dx))
        def _():
            stress_copy(n).start()

    safe = [jnp.where(bottom[c] > 0.0, bottom[c], 1.0) for c in range(3)]
    inverse = [-STRESS_GAIN / safe[c] for c in range(3)]

    def raise_surface(surface, eastward, northward):
        flow_y = along_y([bottom[c] * northward[c] for c in range(3)])
        return [
            (surface[c] - GRAVITY_STEP * (along_x(bottom[c] * eastward[c]) + flow_y[c])) * ocean_mask[c]
            for c in range(3)
        ]

    def push(surface, eastward, northward):
        slope = along_y(surface)
        new_east = [
            eastward[c] + GRAVITY_STEP * (CORIOLIS_STEP * northward[c] - along_x(surface[c])) for c in range(3)
        ]
        new_north = [northward[c] + GRAVITY_STEP * (-CORIOLIS_STEP * eastward[c] - slope[c]) for c in range(3)]
        return new_east, new_north

    surface = raise_surface(surface, eastward, northward)
    pushed = push(surface, eastward, northward)
    wave_lane, fine = iota(wide, 0), iota(wide, 1)
    wave_lane = jnp.where(
        wave_lane < LANES,
        wave_lane + MARGIN_W,
        jnp.where(wave_lane < LANES + 64, wave_lane + MARGIN_W, wave_lane - 2 * LANES + MARGIN_W),
    )
    first = 2 * (fine // 3)
    part = fine % 3
    hits = jnp.where(wave_lane == first, 1.0, 0.0) * jnp.where(part == 0, 1.0, jnp.where(part == 1, 0.5, 0.0)) + jnp.where(
        wave_lane == first + 1, 1.0, 0.0
    ) * jnp.where(part == 2, 1.0, jnp.where(part == 1, 0.5, 0.0))
    prolong = hits.astype(jnp.bfloat16)

    for n, (dy, dx) in enumerate(AROUND):

        @pl.when(exists(-dy, -dx))
        def _():
            stress_copy(n).wait_recv()

    side_lane = iota((SLOTS, LANES), 1)
    pieces = []
    for s in range(3):
        for c in range(2):
            own, right, left = [stress[n, s, pl.ds(c, SLOTS, stride=2), :] for n in range(3)]
            pieces.append(jnp.concatenate([own, jnp.where(side_lane < 64, right, left)], axis=1))
    spread_stress = exact_dot(jnp.concatenate(pieces, axis=0), prolong)
    tensor = []
    for s in range(3):
        low = spread_stress[2 * SLOTS * s : 2 * SLOTS * s + SLOTS]
        high = spread_stress[2 * SLOTS * s + SLOTS : 2 * SLOTS * (s + 1)]
        tensor.append([low, 0.5 * low + 0.5 * high, high])
    cross_y, normal_y = along_y(tensor[1]), along_y(tensor[2])
    force_x = [inverse[c] * (along_x(tensor[0][c]) + cross_y[c]) for c in range(3)]
    force_y = [inverse[c] * (along_x(tensor[1][c]) + normal_y[c]) for c in range(3)]

    for step in range(ITERS):
        if step > 0:
            surface = raise_surface(surface, eastward, northward)
            pushed = push(surface, eastward, northward)
        eastward = [(pushed[0][c] + force_x[c]) * ocean_mask[c] for c in range(3)]
        northward = [(pushed[1][c] + force_y[c]) * ocean_mask[c] for c in range(3)]

    is_even = lax.rem(x, 2) == 0
    for f, values in enumerate((surface, eastward, northward)):
        for c in range(3):
            own = values[c][:8]
            placed = jnp.where(is_even, ocean_shift(own, -MARGIN_O), ocean_shift(own, 64 - MARGIN_O))
            for t in range(2):
                result[t, 8 * (3 * f + c) : 8 * (3 * f + c) + 8, :] = placed[:, LANES * t : LANES * (t + 1)]
    for dest in range(PEERS):
        for t in range(2):
            result_send[dest, t, 0:8, :] = result[t, pl.ds(dest, 8, stride=8), :]
            result_send[dest, t, 8:9, :] = result[t, 64 + dest : 65 + dest, :]

    def result_copy(step):
        dest = peer(step)
        return pltpu.make_async_remote_copy(
            src_ref=result_send.at[dest[2]],
            dst_ref=result_land.at[x],
            send_sem=result_sem.at[0, step],
            recv_sem=result_sem.at[1, step],
            device_id=dest,
            device_id_type=MESH,
        )

    for step in range(1, PEERS):
        result_copy(step).start()
    result_land[x] = result_send[x]
    for step in range(1, PEERS):
        result_copy(step).wait_recv()
    low_half = iota((SLOTS, LANES), 1) < 64
    for q in range(PEERS // 2):
        left, right = 2 * q, 2 * q + 1
        tiles = (
            result_land[left, 0],
            jnp.where(low_half, result_land[left, 1], result_land[right, 0]),
            result_land[right, 1],
        )
        for t in range(3):
            lanes = pl.ds((3 * q + t) * LANES, LANES)
            for f in range(3):
                ocean_out[f, :, lanes] = tiles[t][3 * f : 3 * f + 3]

    for step in range(1, PEERS):
        pack_copy(step).wait_send()
        result_copy(step).wait_send()
    for n in range(2):

        @pl.when(vertical[n])
        def _():
            band_copy(n).wait_send()

    for n, (dy, dx) in enumerate(AROUND):

        @pl.when(exists(dy, dx))
        def _():
            stress_copy(n).wait_send()

    for n in range(4):

        @pl.when(sends[n])
        def _():
            flux_copy(n).wait_send()
            halo_copy(n).wait_send()

        @pl.when(receives[n])
        def _():
            halo_copy(n).wait_recv()

        @pl.when(jnp.logical_not(receives[n]))
        def _():
            halo_fill(n).wait()


def wave_kernel(spectrum, fields, rows_in, cols_in, out, cells, updated, rows, cols, load_sem, store_sem, halo_sem):
    def span_of(direction):
        return pl.ds(pl.multiple_of(direction * PER_DIR, PER_DIR), PER_DIR)

    def load(direction):
        span = span_of(direction)
        return pltpu.make_async_copy(spectrum.at[span], cells.at[span], load_sem.at[direction])

    def store(direction):
        span = span_of(direction)
        return pltpu.make_async_copy(updated.at[span], out.at[span], store_sem.at[direction])

    halos = [pltpu.make_async_copy(rows_in, rows, halo_sem.at[0]), pltpu.make_async_copy(cols_in, cols, halo_sem.at[1])]
    for q in range(4):
        load(q * QUARTER + QUARTER - 1).start()
    for q in range(4):
        load(q * QUARTER).start()
    for copy in halos:
        copy.start()

    def start_load(i, carry):
        for q in range(4):
            load(q * QUARTER + i).start()
        return carry

    lax.fori_loop(1, QUARTER - 1, start_load, 0)

    def field(n):
        return fields[ROWS * n : ROWS * (n + 1), :]

    turning, shifting, mask = field(0), field(1), field(2)
    turn_left = turning > 0.0
    shift_up = shifting > 0.0
    turn_part = mask * jnp.abs(turning)
    stay = mask - turn_part
    shift_part = mask * shifting
    sides = [field(3), field(4), field(5), field(6)]
    lane = iota((ROWS, LANES), 1)
    row = iota((ROWS, LANES), 0)

    for q in range(4):
        load(q * QUARTER + QUARTER - 1).wait()
    for q in range(4):
        load(q * QUARTER).wait()
    for copy in halos:
        copy.wait()

    def cell(direction, j):
        return cells[pl.ds(pl.multiple_of(direction * PER_DIR + j * ROWS, ROWS), ROWS), :]

    def one_direction(i, q, cosine, sine):
        direction = q * QUARTER + i
        before = jnp.where(direction == 0, NDIR - 1, direction - 1)
        after = jnp.where(direction == NDIR - 1, 0, direction + 1)
        from_west, from_south = q in (0, 3), q in (0, 1)
        speed_x, speed_y = (cosine, sine) if q % 2 == 0 else (sine, cosine)
        coefficient_x = sides[0 if from_west else 1] * speed_x
        coefficient_y = sides[2 if from_south else 3] * speed_y
        leave = mask * (speed_x + speed_y)
        place = (i if q == 0 else QUARTER + i) if from_west else (i if q == 1 else QUARTER + i)
        side = 0 if from_west else 1
        columns = pltpu.roll(cols[side, place // 6], lax.rem(LANES - lax.rem(place, 6) * NFREQ, LANES), 1)
        first_row = (direction if from_south else direction - 2 * QUARTER) * NFREQ
        value = cell(direction, 0)
        last_face = None
        for j in range(NFREQ):
            if from_west:
                beside = pltpu.roll(value, 1, 1)
                rim = pltpu.roll(columns, LANES - j, 1) if j else columns
                beside = jnp.where(lane == 0, rim, beside)
            else:
                beside = pltpu.roll(value, LANES - 1, 1)
                rim = pltpu.roll(columns, LANES - 1 - j, 1)
                beside = jnp.where(lane == LANES - 1, rim, beside)
            rim_row = rows[0 if from_south else 1, pl.ds(first_row + j, 1), :]
            if from_south:
                along = jnp.where(row == 0, rim_row, pltpu.roll(value, 1, 0))
            else:
                along = jnp.where(row == ROWS - 1, rim_row, pltpu.roll(value, ROWS - 1, 0))
            moved = coefficient_x * beside + coefficient_y * along - leave * value
            total = stay * value + SPEEDS[j] * moved
            total = total + turn_part * jnp.where(turn_left, cell(before, j), cell(after, j))
            if last_face is not None:
                total = total + last_face
            if j < NFREQ - 1:
                following = cell(direction, j + 1)
                last_face = shift_part * jnp.where(shift_up, value, following)
                total = total - last_face
                value = following
            updated[pl.ds(pl.multiple_of(direction * PER_DIR + j * ROWS, ROWS), ROWS), :] = total

    def one_step(i, angle):
        @pl.when(i < QUARTER - 2)
        def _():
            for q in range(4):
                load(q * QUARTER + i + 1).wait()

        for q in range(4):
            one_direction(i, q, *angle)
            store(q * QUARTER + i).start()
        return next_angle(*angle)

    lax.fori_loop(0, QUARTER, one_step, first_angle())

    def finish(direction, carry):
        store(direction).wait()
        return carry

    lax.fori_loop(0, NDIR, finish, 0)


def shards(mesh_shape, spectrum, sea_mask, ocean_state, depth):
    groups_y = mesh_shape["gy"]
    groups = groups_y * mesh_shape["sec"]
    cells = spectrum.reshape(CELLS, LANES)
    vmem = pl.BlockSpec(memory_space=pltpu.VMEM)
    anywhere = pl.BlockSpec(memory_space=pl.ANY)
    f32 = jnp.float32
    dma = pltpu.SemaphoreType.DMA
    ocean_out, fields, rows, cols = pl.pallas_call(
        functools.partial(coupled_kernel, groups_y, groups),
        out_shape=(
            jax.ShapeDtypeStruct(ocean_state.shape, f32),
            jax.ShapeDtypeStruct((7 * ROWS, LANES), f32),
            jax.ShapeDtypeStruct((2, HALF, LANES), f32),
            jax.ShapeDtypeStruct((2, 3, ROWS, LANES), f32),
        ),
        in_specs=[anywhere, vmem, vmem, vmem],
        out_specs=(vmem, vmem, anywhere, anywhere),
        scratch_shapes=[
            pltpu.VMEM((CELLS, LANES), f32),
            pltpu.VMEM((SLOTS, 1792), f32),
            pltpu.VMEM((SLOTS, 1280), f32),
            pltpu.VMEM((PEERS, 2, SLOTS, LANES), f32),
            pltpu.VMEM((2, SLOTS * SLOTS, LANES), f32),
            pltpu.VMEM((4, 3, ROWS, LANES), f32),
            pltpu.VMEM((2, 3, ROWS, LANES), f32),
            pltpu.VMEM((2, 3, 8, LANES), f32),
            pltpu.VMEM((3, 3, 32, LANES), f32),
            pltpu.VMEM((2, 72, LANES), f32),
            pltpu.VMEM((PEERS, 2, SLOTS, LANES), f32),
            pltpu.VMEM((PEERS, 2, SLOTS, LANES), f32),
            pltpu.VMEM((2, HALF, LANES), f32),
            pltpu.VMEM((2, 3, ROWS, LANES), f32),
            dma((NDIR,)),
            dma((2, PEERS)),
            dma((2, 2)),
            dma((2, 4)),
            dma((2, 8)),
            dma((2, PEERS)),
            dma((2, 4)),
            dma((4,)),
        ],
        compiler_params=pltpu.CompilerParams(
            collective_id=0, has_side_effects=True, vmem_limit_bytes=32 * 1024 * 1024
        ),
        name="coupled",
    )(cells, sea_mask, ocean_state, depth)
    spectrum_out = pl.pallas_call(
        wave_kernel,
        out_shape=jax.ShapeDtypeStruct((CELLS, LANES), f32),
        in_specs=[anywhere, vmem, anywhere, anywhere],
        out_specs=anywhere,
        scratch_shapes=[
            pltpu.VMEM((CELLS, LANES), f32),
            pltpu.VMEM((CELLS, LANES), f32),
            pltpu.VMEM((2, HALF, LANES), f32),
            pltpu.VMEM((2, 3, ROWS, LANES), f32),
            dma((NDIR,)),
            dma((NDIR,)),
            dma((2,)),
        ],
        compiler_params=pltpu.CompilerParams(vmem_limit_bytes=32 * 1024 * 1024),
        name="wave",
    )(cells, fields, rows, cols)
    return (spectrum_out.reshape(spectrum.shape), ocean_out)


def solution(mesh):
    return jax.shard_map(
        functools.partial(shards, dict(mesh.shape)),
        mesh=mesh,
        in_specs=(
            P(None, None, ("sec", "gy"), "gx"),
            P(("sec", "gy", "gx"), None),
            P(None, ("sec", "gy", "gx"), None),
            P(("sec", "gy", "gx"), None),
        ),
        out_specs=(P(None, None, ("sec", "gy"), "gx"), P(None, ("sec", "gy", "gx"), None)),
        check_vma=False,
    )
```

time: 535 us -> 59.2 us (0.11); the launches traced: 528 us -> 59 us
  other arithmetic: 235 us -> 0 us
  local copies, waits for them, and re-layouts: 149 us -> 5.62 us
  starting transfers between devices: 120 us -> 0 us
  Pallas kernels: 0 us -> 52.7 us
  waiting for transfers between devices: 16.6 us -> 0 us
  matrix products: 5.86 us -> 0 us
    reduce_sum x8 -> x0, other arithmetic: 127 us -> none  [wave_update(): jnp.einsum('kjrx,sk->srx', updated, stress_table, precision=lax.Precision...]
    slice x38 -> x0, local copies, waits for them, and re-layouts: 111 us -> none  [the longest x16 84 us: wave_update(): jnp.roll(masked, 1, axis=0)]
    ppermute x24 -> x0, starting transfers between devices: 106 us -> none  [the longest x12 74.5 us: extended(): lax.ppermute(head, axis, [((i + 1) % count, i) for i in range(ends)])]
    add x11 -> x0, other arithmetic: 73.8 us -> none  [the longest x8 73.7 us: wave_update(): faces = shift_pos * masked[:, :-1] + shift_neg * masked[:, 1:]]
    pallas_call x0 -> x2, Pallas kernels: none -> 52.7 us  [the longest x1 37.6 us: shards(): pl.pallas_call(functools.partial(coupled_kernel, groups_y, groups), out_s...]
    concatenate x12 -> x0, other arithmetic: 22 us -> none  [extended(): jnp.concatenate([lax.ppermute(tail, axis, [(i, (i + 1) % count) for i in...]
    all_to_all x2 -> x0, starting transfers between devices: 13.2 us -> none  [the longest x1 9.19 us: shards(): lax.all_to_all(outgoing, 'gx', split_axis=2, concat_axis=1, tiled=True)]
    ppermute x2 -> x0, local copies, waits for them, and re-layouts: 12.9 us -> none  [the longest x1 6.52 us: extended(): lax.ppermute(tail, axis, [(i, (i + 1) % count) for i in range(ends)])]
  transfers between devices with their start and end apart: 26 -> 0, of which waited for: 10 -> 0; matrix products, arithmetic and copies ran while one was open for 5% -> 0% of each run, Pallas kernels for 0% -> 0%
where the time goes in v1:
time: 59.2 us; the launch traced here: 59 us
  Pallas kernels  52.7 us (89%)
  local copies, waits for them, and re-layouts  5.62 us (9%)
  between operations  0.66 us (1%)
    pallas_call x1, Pallas kernels, shards(): pl.pallas_call(functools.partial(coupled_kernel, groups_y, groups), out_s...  37.6 us
    pallas_call x1, Pallas kernels, shards(): pl.pallas_call(wave_kernel, out_shape=jax.ShapeDtypeStruct((CELLS, LANES)...  15.1 us
    unnamed x9, local copies, waits for them, and re-layouts  5.62 us

profile of v1, /device:TPU:25, one launch (start us, length us, event | category | flops | bytes accessed | tf_op | source)
XLA Modules:
  0.0 59.0 jit_solution(3466966826846944690)
XLA Ops:
  0.6 0.0 copy-start
  0.6 2.7 %copy-done = f32[36,20,16,128]{3,2,1,0:T(8,128)S(1)} copy-done((f32[36,20,16,128]{3,2,1,0:T(8,128)S(1)}, f32[36,20,16,128]{3,2,1,0:T(8,128)}, u32[]{:S(2)}) %copy-start) | copy-done | bytes 5898264
  3.3 0.0 copy-start.1
  3.3 0.9 %copy-done.1 = f32[3,3,1536]{2,1,0:T(4,128)S(1)} copy-done((f32[3,3,1536]{2,1,0:T(4,128)S(1)}, f32[3,3,1536]{2,1,0:T(4,128)}, u32[]{:S(2)}) %copy-start.1) | copy-done | bytes 55320
  4.2 0.0 copy-start.2
  4.2 0.7 %copy-done.2 = f32[3,1536]{1,0:T(4,128)S(1)} copy-done((f32[3,1536]{1,0:T(4,128)S(1)}, f32[3,1536]{1,0:T(4,128)}, u32[]{:S(2)}) %copy-start.2) | copy-done | bytes 18456
  4.9 0.0 copy-start.3
  4.9 0.7 %copy-done.3 = s32[2,1024]{1,0:T(2,128)S(1)} copy-done((s32[2,1024]{1,0:T(2,128)S(1)}, s32[2,1024]{1,0:T(2,128)}, u32[]{:S(2)}) %copy-start.3) | copy-done | bytes 8216
  5.6 37.6 %coupled.1 = (f32[3,3,1536]{2,1,0:T(4,128)S(1)}, f32[112,128]{1,0:T(8,128)S(1)}, f32[2,360,128]{2,1,0:T(8,128)S(1)}, f32[2,3,16,128]{3,2,1,0:T(8,128)S(1)}) custom-call(f32[11520,128]{1,0:T(8,128)S(1)} %bitcast.2, s32[2,1024]{1,0:T(2,128)S(1)} %copy-done.3, f32[3,3,1536]{2,1,0:T(4,128)S(1)} %copy-done.1, f32[3,1536]{1,0:T(4,128)S(1)} %copy-done.2), custom_call_target="tpu_custom_call" | custom-call | tf_op jit(solution)/shard_map/coupled/pallas_call | solution.py:741
  43.2 15.1 %wave.1 = f32[11520,128]{1,0:T(8,128)} custom-call(f32[11520,128]{1,0:T(8,128)S(1)} %bitcast.3, f32[112,128]{1,0:T(8,128)S(1)} %get-tuple-element.6.fields, f32[2,360,128]{2,1,0:T(8,128)S(1)} %get-tuple-element.7.rows_in, f32[2,3,16,128]{3,2,1,0:T(8,128)S(1)} %get-tuple-element.8.cols_in), custom_call_target="tpu_custom_call" | custom-call | tf_op jit(solution)/shard_map/wave/pallas_call | solution.py:780
  58.3 0.6 %copy.7 = f32[3,3,1536]{2,1,0:T(4,128)} copy(f32[3,3,1536]{2,1,0:T(4,128)S(1)} %get-tuple-element.13) | data formatting | bytes 110592
Async XLA Ops:
  0.6 2.7 %copy-start = (f32[36,20,16,128]{3,2,1,0:T(8,128)S(1)}, f32[36,20,16,128]{3,2,1,0:T(8,128)}, u32[]{:S(2)}) copy-start(f32[36,20,16,128]{3,2,1,0:T(8,128)} %param.4) | copy-start | bytes 17694724
  3.3 0.9 %copy-start.1 = (f32[3,3,1536]{2,1,0:T(4,128)S(1)}, f32[3,3,1536]{2,1,0:T(4,128)}, u32[]{:S(2)}) copy-start(f32[3,3,1536]{2,1,0:T(4,128)} %ocean_state.1) | copy-start | bytes 165892
  4.2 0.7 %copy-start.2 = (f32[3,1536]{1,0:T(4,128)S(1)}, f32[3,1536]{1,0:T(4,128)}, u32[]{:S(2)}) copy-start(f32[3,1536]{1,0:T(4,128)} %depth.1) | copy-start | bytes 55300
  4.9 0.7 %copy-start.3 = (s32[2,1024]{1,0:T(2,128)S(1)}, s32[2,1024]{1,0:T(2,128)}, u32[]{:S(2)}) copy-start(s32[2,1024]{1,0:T(2,128)} %sea_mask.1) | copy-start | bytes 24580

commit v2 on v1

--- a/solution.py
+++ b/solution.py
@@ -23,6 +23,8 @@
 CELLS = NDIR * NFREQ * ROWS
 PER_DIR = NFREQ * ROWS
 QUARTER = NDIR // 4
+PITCH = 24
+VMEM_LIMIT = 60 * 1024 * 1024
 HALF = NDIR // 2 * NFREQ
 PEERS = 8
 SLOTS = 16
@@ -332,17 +334,17 @@
         tile = zero
         for j in range(NFREQ):
             value = cells[pl.ds(pl.multiple_of(base + j * ROWS, ROWS), ROWS), :]
-            tile = jnp.where(lane == j, pltpu.roll(value, (j + 1 if last else j) % LANES, 1) if (last or j) else value, tile)
+            tile = jnp.where(lane == 2 * j + last, pltpu.roll(value, 2 * j + 2 * last, 1) if (last or j) else value, tile)
         return tile
 
     def pack_cols(n, carry):
-        group, part = n // 6, lax.rem(n, 6)
+        group, part = n // 3, lax.rem(n, 3)
         eastward = jnp.where(n < QUARTER, n, n + 2 * QUARTER)
-        shift = part * NFREQ
+        shift = part * (2 * NFREQ)
         keep = part > 0
-        cols_send[0, group] = jnp.where(keep, cols_send[0, group], zero) + pltpu.roll(edge_lanes(eastward, True), shift, 1)
+        cols_send[0, group] = jnp.where(keep, cols_send[0, group], zero) + pltpu.roll(edge_lanes(eastward, 1), shift, 1)
         cols_send[1, group] = jnp.where(keep, cols_send[1, group], zero) + pltpu.roll(
-            edge_lanes(n + QUARTER, False), shift, 1
+            edge_lanes(n + QUARTER, 0), shift, 1
         )
         return carry
 
@@ -619,25 +621,25 @@
             halo_fill(n).wait()
 
 
-def wave_kernel(spectrum, fields, rows_in, cols_in, out, cells, updated, rows, cols, load_sem, store_sem, halo_sem):
-    def span_of(direction):
-        return pl.ds(pl.multiple_of(direction * PER_DIR, PER_DIR), PER_DIR)
-
+def wave_kernel(spectrum, fields, rows_in, cols_in, out, cells, updated, beside, rows, cols, load_sem, store_sem, halo_sem):
     def load(direction):
-        span = span_of(direction)
-        return pltpu.make_async_copy(spectrum.at[span], cells.at[span], load_sem.at[direction])
+        return pltpu.make_async_copy(
+            spectrum.at[pl.ds(direction * NFREQ, NFREQ)],
+            cells.at[pl.ds(direction * NFREQ, NFREQ), pl.ds(8, ROWS), :],
+            load_sem.at[direction],
+        )
 
     def store(direction):
-        span = span_of(direction)
+        span = pl.ds(direction * NFREQ, NFREQ)
         return pltpu.make_async_copy(updated.at[span], out.at[span], store_sem.at[direction])
 
     halos = [pltpu.make_async_copy(rows_in, rows, halo_sem.at[0]), pltpu.make_async_copy(cols_in, cols, halo_sem.at[1])]
+    for copy in halos:
+        copy.start()
     for q in range(4):
         load(q * QUARTER + QUARTER - 1).start()
     for q in range(4):
         load(q * QUARTER).start()
-    for copy in halos:
-        copy.start()
 
     def start_load(i, carry):
         for q in range(4):
@@ -645,70 +647,98 @@
         return carry
 
     lax.fori_loop(1, QUARTER - 1, start_load, 0)
-
-    def field(n):
-        return fields[ROWS * n : ROWS * (n + 1), :]
-
-    turning, shifting, mask = field(0), field(1), field(2)
-    turn_left = turning > 0.0
-    shift_up = shifting > 0.0
-    turn_part = mask * jnp.abs(turning)
-    stay = mask - turn_part
-    shift_part = mask * shifting
-    sides = [field(3), field(4), field(5), field(6)]
-    lane = iota((ROWS, LANES), 1)
-    row = iota((ROWS, LANES), 0)
+    flat = cells.reshape((NDIR * NFREQ + 1) * PITCH, LANES)
+
+    def half(n, h):
+        return fields[ROWS * n + 8 * h : ROWS * n + 8 * h + 8, :]
+
+    def turn_part(h):
+        return half(2, h) * jnp.abs(half(0, h))
+
+    lane = iota((8, LANES), 1)
+    for copy in halos:
+        copy.wait()
+
+    def place_rows(n, carry):
+        span = pl.ds(pl.multiple_of(n * 8, 8), 8)
+        flat[pl.ds(n * (8 * PITCH) + 7, 8, stride=PITCH), :] = rows[0, span, :]
+        flat[pl.ds(n * (8 * PITCH) + (HALF + 1) * PITCH, 8, stride=PITCH), :] = rows[1, span, :]
+        return carry
+
+    lax.fori_loop(0, HALF // 8, place_rows, 0)
+
+    def cell(direction, j, offset):
+        return flat[pl.ds(direction * (NFREQ * PITCH) + (j * PITCH + 8 + offset), 8), :]
+
+    odd = lax.rem(lane, 2) == 1
+
+    def rims(i, h):
+        columns = []
+        for place in (i, QUARTER + i):
+            group, part = place // 3, lax.rem(place, 3)
+            span = slice(8 * h, 8 * h + 8)
+            merged = jnp.where(odd, cols[0, group, span, :], cols[1, group, span, :])
+            columns.append(pltpu.roll(merged, lax.rem(LANES - part * (2 * NFREQ), LANES), 1))
+        return columns
+
+    def prepare(i, h, j, columns):
+        rim = [pltpu.roll(column, LANES - 1 - 2 * j, 1) for column in columns]
+        for q in range(4):
+            value = cell(q * QUARTER + i, j, 8 * h)
+            if q in (0, 3):
+                moved = jnp.where(lane == 0, rim[q // 2], pltpu.roll(value, 1, 1))
+            else:
+                moved = jnp.where(lane == LANES - 1, rim[q // 2], pltpu.roll(value, LANES - 1, 1))
+            beside[q * NFREQ + j, 8 * h : 8 * h + 8, :] = moved
+
+    def update(i, cosine, sine):
+        following_step = jnp.minimum(i + 1, QUARTER - 1)
+        for h in range(2):
+            columns = rims(following_step, h)
+            turn_left = half(0, h) > 0.0
+            shift_up = half(1, h) > 0.0
+            mask = half(2, h)
+            turned = turn_part(h)
+            stay = mask - turned
+            shifted = mask * half(1, h)
+            leave = mask * (cosine + sine)
+            factors = []
+            for q in range(4):
+                speed_x, speed_y = (cosine, sine) if q % 2 == 0 else (sine, cosine)
+                factors.append((half(3 if q in (0, 3) else 4, h) * speed_x, half(5 if q in (0, 1) else 6, h) * speed_y))
+            values = [cell(q * QUARTER + i, 0, 8 * h) for q in range(4)]
+            faces = [None] * 4
+            for j in range(NFREQ):
+                keep = stay - SPEEDS[j] * leave
+                for q in range(4):
+                    direction = q * QUARTER + i
+                    before, after = direction - 1, direction + 1
+                    if q == 0:
+                        before = jnp.where(i == 0, NDIR - 1, before)
+                    if q == 3:
+                        after = jnp.where(i == QUARTER - 1, 0, after)
+                    along = cell(direction, j, 8 * h + (-1 if q in (0, 1) else 1))
+                    moved = factors[q][0] * beside[q * NFREQ + j, 8 * h : 8 * h + 8, :] + factors[q][1] * along
+                    total = keep * values[q] + SPEEDS[j] * moved
+                    total = total + turned * jnp.where(turn_left, cell(before, j, 8 * h), cell(after, j, 8 * h))
+                    if j > 0:
+                        total = total + faces[q]
+                    if j < NFREQ - 1:
+                        following = cell(direction, j + 1, 8 * h)
+                        faces[q] = shifted * jnp.where(shift_up, values[q], following)
+                        total = total - faces[q]
+                        values[q] = following
+                    updated[direction * NFREQ + j, 8 * h : 8 * h + 8, :] = total
+                prepare(following_step, h, j, columns)
 
     for q in range(4):
         load(q * QUARTER + QUARTER - 1).wait()
     for q in range(4):
         load(q * QUARTER).wait()
-    for copy in halos:
-        copy.wait()
-
-    def cell(direction, j):
-        return cells[pl.ds(pl.multiple_of(direction * PER_DIR + j * ROWS, ROWS), ROWS), :]
-
-    def one_direction(i, q, cosine, sine):
-        direction = q * QUARTER + i
-        before = jnp.where(direction == 0, NDIR - 1, direction - 1)
-        after = jnp.where(direction == NDIR - 1, 0, direction + 1)
-        from_west, from_south = q in (0, 3), q in (0, 1)
-        speed_x, speed_y = (cosine, sine) if q % 2 == 0 else (sine, cosine)
-        coefficient_x = sides[0 if from_west else 1] * speed_x
-        coefficient_y = sides[2 if from_south else 3] * speed_y
-        leave = mask * (speed_x + speed_y)
-        place = (i if q == 0 else QUARTER + i) if from_west else (i if q == 1 else QUARTER + i)
-        side = 0 if from_west else 1
-        columns = pltpu.roll(cols[side, place // 6], lax.rem(LANES - lax.rem(place, 6) * NFREQ, LANES), 1)
-        first_row = (direction if from_south else direction - 2 * QUARTER) * NFREQ
-        value = cell(direction, 0)
-        last_face = None
+    for h in range(2):
+        first_columns = rims(0, h)
         for j in range(NFREQ):
-            if from_west:
-                beside = pltpu.roll(value, 1, 1)
-                rim = pltpu.roll(columns, LANES - j, 1) if j else columns
-                beside = jnp.where(lane == 0, rim, beside)
-            else:
-                beside = pltpu.roll(value, LANES - 1, 1)
-                rim = pltpu.roll(columns, LANES - 1 - j, 1)
-                beside = jnp.where(lane == LANES - 1, rim, beside)
-            rim_row = rows[0 if from_south else 1, pl.ds(first_row + j, 1), :]
-            if from_south:
-                along = jnp.where(row == 0, rim_row, pltpu.roll(value, 1, 0))
-            else:
-                along = jnp.where(row == ROWS - 1, rim_row, pltpu.roll(value, ROWS - 1, 0))
-            moved = coefficient_x * beside + coefficient_y * along - leave * value
-            total = stay * value + SPEEDS[j] * moved
-            total = total + turn_part * jnp.where(turn_left, cell(before, j), cell(after, j))
-            if last_face is not None:
-                total = total + last_face
-            if j < NFREQ - 1:
-                following = cell(direction, j + 1)
-                last_face = shift_part * jnp.where(shift_up, value, following)
-                total = total - last_face
-                value = following
-            updated[pl.ds(pl.multiple_of(direction * PER_DIR + j * ROWS, ROWS), ROWS), :] = total
+            prepare(0, h, j, first_columns)
 
     def one_step(i, angle):
         @pl.when(i < QUARTER - 2)
@@ -716,8 +746,8 @@
             for q in range(4):
                 load(q * QUARTER + i + 1).wait()
 
+        update(i, *angle)
         for q in range(4):
-            one_direction(i, q, *angle)
             store(q * QUARTER + i).start()
         return next_angle(*angle)
 
@@ -744,7 +774,7 @@
             jax.ShapeDtypeStruct(ocean_state.shape, f32),
             jax.ShapeDtypeStruct((7 * ROWS, LANES), f32),
             jax.ShapeDtypeStruct((2, HALF, LANES), f32),
-            jax.ShapeDtypeStruct((2, 3, ROWS, LANES), f32),
+            jax.ShapeDtypeStruct((2, 6, ROWS, LANES), f32),
         ),
         in_specs=[anywhere, vmem, vmem, vmem],
         out_specs=(vmem, vmem, anywhere, anywhere),
@@ -762,7 +792,7 @@
             pltpu.VMEM((PEERS, 2, SLOTS, LANES), f32),
             pltpu.VMEM((PEERS, 2, SLOTS, LANES), f32),
             pltpu.VMEM((2, HALF, LANES), f32),
-            pltpu.VMEM((2, 3, ROWS, LANES), f32),
+            pltpu.VMEM((2, 6, ROWS, LANES), f32),
             dma((NDIR,)),
             dma((2, PEERS)),
             dma((2, 2)),
@@ -773,27 +803,28 @@
             dma((4,)),
         ],
         compiler_params=pltpu.CompilerParams(
-            collective_id=0, has_side_effects=True, vmem_limit_bytes=32 * 1024 * 1024
+            collective_id=0, has_side_effects=True, vmem_limit_bytes=VMEM_LIMIT
         ),
         name="coupled",
     )(cells, sea_mask, ocean_state, depth)
     spectrum_out = pl.pallas_call(
         wave_kernel,
-        out_shape=jax.ShapeDtypeStruct((CELLS, LANES), f32),
+        out_shape=jax.ShapeDtypeStruct((NDIR * NFREQ, ROWS, LANES), f32),
         in_specs=[anywhere, vmem, anywhere, anywhere],
         out_specs=anywhere,
         scratch_shapes=[
-            pltpu.VMEM((CELLS, LANES), f32),
-            pltpu.VMEM((CELLS, LANES), f32),
+            pltpu.VMEM((NDIR * NFREQ + 1, PITCH, LANES), f32),
+            pltpu.VMEM((NDIR * NFREQ, ROWS, LANES), f32),
+            pltpu.VMEM((4 * NFREQ, ROWS, LANES), f32),
             pltpu.VMEM((2, HALF, LANES), f32),
-            pltpu.VMEM((2, 3, ROWS, LANES), f32),
+            pltpu.VMEM((2, 6, ROWS, LANES), f32),
             dma((NDIR,)),
             dma((NDIR,)),
             dma((2,)),
         ],
-        compiler_params=pltpu.CompilerParams(vmem_limit_bytes=32 * 1024 * 1024),
+        compiler_params=pltpu.CompilerParams(vmem_limit_bytes=VMEM_LIMIT),
         name="wave",
-    )(cells, fields, rows, cols)
+    )(spectrum.reshape(NDIR * NFREQ, ROWS, LANES), fields, rows, cols)
     return (spectrum_out.reshape(spectrum.shape), ocean_out)
 
 

time: 59.2 us -> 41.4 us (0.70)
  Pallas kernels: 52.7 us -> 40 us
  local copies, waits for them, and re-layouts: 5.62 us -> 0.64 us
    pallas_call x1, Pallas kernels: 15.1 us -> 8.25 us  [shards(): pl.pallas_call(wave_kernel, out_shape=jax.ShapeDtypeStruct((NDIR * NFREQ,...]
    pallas_call x1, Pallas kernels: 37.6 us -> 31.7 us  [shards(): pl.pallas_call(functools.partial(coupled_kernel, groups_y, groups), out_s...]
    unnamed x9 -> x3, local copies, waits for them, and re-layouts: 5.62 us -> 0.64 us
where the time goes in v2:
time: 41.4 us; the launch traced here: 41.3 us
  Pallas kernels  40 us (97%)
  between operations  0.66 us (2%)
  local copies, waits for them, and re-layouts  0.64 us (2%)
    pallas_call x1, Pallas kernels, shards(): pl.pallas_call(functools.partial(coupled_kernel, groups_y, groups), out_s...  31.7 us
    pallas_call x1, Pallas kernels, shards(): pl.pallas_call(wave_kernel, out_shape=jax.ShapeDtypeStruct((NDIR * NFREQ,...  8.25 us

profile of v2, /device:TPU:25, one launch (start us, length us, event | category | flops | bytes accessed | tf_op | source)
XLA Modules:
  0.0 41.3 jit_solution(11250772721005460630)
XLA Ops:
  0.6 31.7 %coupled.1 = (f32[3,3,1536]{2,1,0:T(4,128)}, f32[112,128]{1,0:T(8,128)}, f32[2,360,128]{2,1,0:T(8,128)}, f32[2,6,16,128]{3,2,1,0:T(8,128)}) custom-call(f32[11520,128]{1,0:T(8,128)} %bitcast.3, s32[2,1024]{1,0:T(2,128)} %sea_mask.1, f32[3,3,1536]{2,1,0:T(4,128)} %ocean_state.1, f32[3,1536]{1,0:T(4,128)} %depth.1), custom_call_target="tpu_custom_call" | custom-call | tf_op jit(solution)/shard_map/coupled/pallas_call | solution.py:771
  32.4 0.0 copy-start
  32.4 8.3 %wave.1 = f32[720,16,128]{2,1,0:T(8,128)} custom-call(f32[720,16,128]{2,1,0:T(8,128)} %bitcast.4, f32[112,128]{1,0:T(8,128)} %get-tuple-element.6.fields, f32[2,360,128]{2,1,0:T(8,128)} %get-tuple-element.7.rows_in, f32[2,6,16,128]{3,2,1,0:T(8,128)} %get-tuple-element.8.cols_in), custom_call_target="tpu_custom_call" | custom-call | tf_op jit(solution)/shard_map/wave/pallas_call | solution.py:810
  40.6 0.0 copy-done
  40.6 0.6 %copy.7 = f32[3,3,1536]{2,1,0:T(4,128)} copy(f32[3,3,1536]{2,1,0:T(4,128)S(1)} %copy-done) | data formatting | bytes 110592
Async XLA Ops:
  32.4 8.3 %copy-start = (f32[3,3,1536]{2,1,0:T(4,128)S(1)}, f32[3,3,1536]{2,1,0:T(4,128)}, u32[]{:S(2)}) copy-start(f32[3,3,1536]{2,1,0:T(4,128)} %get-tuple-element.13) | copy-start | bytes 165892

commit v3 on v2

--- a/solution.py
+++ b/solution.py
@@ -86,23 +86,28 @@
     rows_out,
     cols_out,
     cells,
+    state_in,
+    depth_in,
+    mask_in,
     raw,
     raw_mask,
     pack,
     window,
-    flux,
-    flux_cols,
-    flux_rows,
+    mask_window,
+    beside_send,
+    across_send,
+    beside_land,
+    across_land,
     stress,
     result,
     result_send,
     result_land,
     rows_send,
     cols_send,
+    input_sem,
     load_sem,
     pack_sem,
-    band_sem,
-    flux_sem,
+    far_sem,
     stress_sem,
     result_sem,
     halo_sem,
@@ -126,12 +131,36 @@
             answer = jnp.logical_and(answer, check)
         return answer
 
+    def device_at(row, column):
+        return (row // groups_y, lax.rem(row, groups_y), column)
+
     def device(dy, dx):
-        row = y + dy
-        return (row // groups_y, lax.rem(row, groups_y), x + dx)
+        return device_at(y + dy, x + dx)
 
     def peer(step):
         return (lax.axis_index("sec"), lax.axis_index("gy"), lax.rem(x + step, PEERS))
+
+    inputs = [
+        pltpu.make_async_copy(ocean_state, state_in, input_sem.at[0]),
+        pltpu.make_async_copy(depth, depth_in, input_sem.at[1]),
+        pltpu.make_async_copy(sea_mask, mask_in, input_sem.at[2]),
+    ]
+    for copy in inputs:
+        copy.start()
+
+    barrier = pltpu.get_barrier_semaphore()
+    for step in range(1, PEERS):
+        pl.semaphore_signal(barrier, inc=1, device_id=peer(step), device_id_type=MESH)
+    greeted = PEERS - 1
+    for dy in (1, -1):
+        here = exists(dy, 0)
+
+        @pl.when(here)
+        def _():
+            for column in range(PEERS):
+                pl.semaphore_signal(barrier, inc=1, device_id=device_at(y + dy, column), device_id_type=MESH)
+
+        greeted = greeted + here.astype(jnp.int32) * PEERS
 
     def load(direction):
         span = pl.ds(pl.multiple_of(direction * PER_DIR, PER_DIR), PER_DIR)
@@ -144,27 +173,38 @@
 
     lax.fori_loop(0, QUARTER, start_load, 0)
 
-    barrier = pltpu.get_barrier_semaphore()
-    for step in range(1, PEERS):
-        pl.semaphore_signal(barrier, inc=1, device_id=peer(step), device_id_type=MESH)
-    greeted = PEERS - 1
-    for dy, dx in AROUND:
-        if dy != 0:
-            here = exists(dy, dx)
-
-            @pl.when(here)
-            def _():
-                pl.semaphore_signal(barrier, inc=1, device_id=device(dy, dx), device_id_type=MESH)
-
-            greeted = greeted + here.astype(jnp.int32)
+    window[:, 11 * SLOTS : 13 * SLOTS, :] = jnp.zeros((2, 2 * SLOTS, LANES), jnp.float32)
+    edge = jnp.zeros((2, 3 * SLOTS, LANES), jnp.float32)
+
+    @pl.when(y == 0)
+    def _():
+        window[:, 13 * SLOTS : 16 * SLOTS, :] = edge
+        across_land[:, 1] = jnp.zeros((3, 4, 8, LANES), jnp.float32)
+
+    @pl.when(y == groups - 1)
+    def _():
+        window[:, 8 * SLOTS : 11 * SLOTS, :] = edge
+        across_land[:, 0] = jnp.zeros((3, 4, 8, LANES), jnp.float32)
+
+    @pl.when(x == 0)
+    def _():
+        beside_land[1] = jnp.zeros((5, ROWS, LANES), jnp.float32)
+        across_land[2] = jnp.zeros((2, 4, 8, LANES), jnp.float32)
+
+    @pl.when(x == PEERS - 1)
+    def _():
+        beside_land[0] = jnp.zeros((5, ROWS, LANES), jnp.float32)
+        across_land[1] = jnp.zeros((2, 4, 8, LANES), jnp.float32)
 
     raw[...] = jnp.zeros_like(raw)
     raw_mask[...] = jnp.zeros_like(raw_mask)
-    width = ocean_state.shape[2]
+    width = state_in.shape[2]
+    for copy in inputs:
+        copy.wait()
     for f in range(3):
-        raw[3 * f : 3 * f + 3, :width] = ocean_state[f]
-    raw[9:12, :width] = depth[...]
-    raw_mask[12:14, : sea_mask.shape[1]] = sea_mask[...].astype(jnp.float32)
+        raw[3 * f : 3 * f + 3, :width] = state_in[f]
+    raw[9:12, :width] = depth_in[...]
+    raw_mask[12:14, : mask_in.shape[1]] = mask_in[...].astype(jnp.float32)
     even = ocean_shift(raw[...], MARGIN_O)
     odd = ocean_shift(raw[...], MARGIN_O - 64)
     mask_rows = ocean_shift(raw_mask[...], MARGIN_W)
@@ -179,67 +219,83 @@
                 mask_rows[:, LANES * (dest + tile) : LANES * (dest + tile + 1)],
             )
 
-    slab = jnp.zeros((2, 2 * SLOTS, LANES), jnp.float32)
-    window[:, 11 * SLOTS : 13 * SLOTS, :] = slab
-    edge = jnp.zeros((2, 3 * SLOTS, LANES), jnp.float32)
-
-    @pl.when(y == 0)
-    def _():
-        window[:, 13 * SLOTS : 16 * SLOTS, :] = edge
-        flux_rows[0] = jnp.zeros((3, 8, LANES), jnp.float32)
-        stress[:, :, 24:32, :] = jnp.zeros((3, 3, 8, LANES), jnp.float32)
-
-    @pl.when(y == groups - 1)
-    def _():
-        window[:, 8 * SLOTS : 11 * SLOTS, :] = edge
-        flux_rows[1] = jnp.zeros((3, 8, LANES), jnp.float32)
-        stress[:, :, 16:24, :] = jnp.zeros((3, 3, 8, LANES), jnp.float32)
-
-    @pl.when(x == 0)
-    def _():
-        flux_cols[0] = jnp.zeros((3, ROWS, LANES), jnp.float32)
-        stress[2] = jnp.zeros((3, 32, LANES), jnp.float32)
-
-    @pl.when(x == PEERS - 1)
-    def _():
-        flux_cols[1] = jnp.zeros((3, ROWS, LANES), jnp.float32)
-        stress[1] = jnp.zeros((3, 32, LANES), jnp.float32)
-
-    mine = pl.ds(pl.multiple_of(x * SLOTS, SLOTS), SLOTS)
+    def slot(n):
+        return pl.ds(pl.multiple_of(n * SLOTS, SLOTS), SLOTS)
 
     def pack_copy(step):
         dest = peer(step)
         return pltpu.make_async_remote_copy(
             src_ref=pack.at[dest[2]],
-            dst_ref=window.at[:, mine, :],
+            dst_ref=window.at[:, slot(x), :],
             send_sem=pack_sem.at[0, step],
             recv_sem=pack_sem.at[1, step],
             device_id=dest,
             device_id_type=MESH,
         )
 
+    upward = x >= PEERS - 3
+    far = jnp.logical_or(jnp.logical_and(upward, y < groups - 1), jnp.logical_and(x <= 2, y > 0))
+    far_row = jnp.where(upward, y + 1, y - 1)
+
+    def far_copy(column):
+        return pltpu.make_async_remote_copy(
+            src_ref=pack.at[column],
+            dst_ref=window.at[:, slot(x + PEERS), :],
+            send_sem=far_sem.at[0, column],
+            recv_sem=far_sem.at[1, x],
+            device_id=device_at(far_row, column),
+            device_id_type=MESH,
+        )
+
+    def far_arrival(column):
+        return pltpu.make_async_remote_copy(
+            src_ref=pack.at[column],
+            dst_ref=window.at[:, slot(column + PEERS), :],
+            send_sem=far_sem.at[0, column],
+            recv_sem=far_sem.at[1, column],
+            device_id=peer(1),
+            device_id_type=MESH,
+        )
+
     pl.semaphore_wait(barrier, greeted)
+
+    @pl.when(far)
+    def _():
+        for column in range(PEERS):
+            far_copy(column).start()
+
     for step in range(1, PEERS):
         pack_copy(step).start()
-    window[:, mine, :] = pack[x]
-
-    def sums(direction):
-        base = direction * PER_DIR
-        total = weighted = None
-        for j in range(NFREQ):
-            value = cells[pl.ds(pl.multiple_of(base + j * ROWS, ROWS), ROWS), :]
-            total = value if j == 0 else total + value
-            scaled = value * SPEEDS[j]
-            weighted = scaled if j == 0 else weighted + scaled
-        return total, weighted
+    window[:, slot(x), :] = pack[x]
+
+    lane = iota((ROWS, LANES), 1)
+    row = iota((ROWS, LANES), 0)
+    zero = jnp.zeros((ROWS, LANES), jnp.float32)
 
     def gather(i, carry):
         (cosine, sine), plain, fluxes = carry
         for q in range(4):
             load(q * QUARTER + i).wait()
+        totals, weighted, rims = [None] * 4, [None] * 4, [zero, zero]
+        for j in range(NFREQ):
+            values = []
+            for q in range(4):
+                base = (q * QUARTER + i) * PER_DIR
+                values.append(cells[pl.ds(pl.multiple_of(base + j * ROWS, ROWS), ROWS), :])
+                scaled = values[q] * SPEEDS[j]
+                totals[q] = values[q] if j == 0 else totals[q] + values[q]
+                weighted[q] = scaled if j == 0 else weighted[q] + scaled
+            here = jnp.logical_or(lane == 2 * j + 1, lane == 2 * j + 2)
+            for n, (east, west) in enumerate(((0, 1), (3, 2))):
+                both = jnp.where(lane == LANES - 1, values[east], values[west])
+                rims[n] = jnp.where(here, pltpu.roll(both, 2 * j + 2, 1), rims[n])
+        for n in range(2):
+            place = i + n * QUARTER
+            group, part = place // 3, lax.rem(place, 3)
+            earlier = jnp.where(part > 0, cols_send[group], zero)
+            cols_send[group] = earlier + pltpu.roll(rims[n], part * (2 * NFREQ), 1)
         scale = 0.5 / (NDIR * NFREQ)
         cc, cs, ss = cosine * cosine * scale, cosine * sine * scale, sine * sine * scale
-        totals, weighted = zip(*[sums(q * QUARTER + i) for q in range(4)])
         pair = (totals[0] + totals[2]) - (totals[1] + totals[3])
         plain = (
             plain[0] + ((totals[0] + totals[2]) + (totals[1] + totals[3])),
@@ -262,128 +318,33 @@
         )
         return next_angle(cosine, sine), plain, (west, east, south, north)
 
-    zero = jnp.zeros((ROWS, LANES), jnp.float32)
+    cols_send[...] = jnp.zeros_like(cols_send)
     triple = (zero, zero, zero)
-    state = (first_angle(), triple, (triple, triple, triple, triple))
-    state = lax.fori_loop(0, QUARTER // 2, gather, state)
+    carry = (first_angle(), triple, (triple, triple, triple, triple))
+    _, plain, fluxes = lax.fori_loop(0, QUARTER, gather, carry)
+
+    def pack_rows(n, carry):
+        for m in range(5):
+            start = n * 40 + m * 8
+            span = pl.ds(pl.multiple_of(start, 8), 8)
+            rows_send[0, span, :] = cells[pl.ds(start * ROWS + (ROWS - 1), 8, stride=ROWS), :]
+            rows_send[1, span, :] = cells[pl.ds(start * ROWS + HALF * ROWS, 8, stride=ROWS), :]
+        return carry
+
+    lax.fori_loop(0, HALF // 40, pack_rows, 0)
 
     for step in range(1, PEERS):
         pack_copy(step).wait_recv()
 
-    def band_copy(n):
-        dy = 1 if n == 0 else -1
-        source = pl.ds((5 if n == 0 else 0) * SLOTS, 3 * SLOTS)
-        target = pl.ds((13 if n == 0 else 8) * SLOTS, 3 * SLOTS)
-        return pltpu.make_async_remote_copy(
-            src_ref=window.at[:, source, :],
-            dst_ref=window.at[:, target, :],
-            send_sem=band_sem.at[0, n],
-            recv_sem=band_sem.at[1, n],
-            device_id=device(dy, 0),
-            device_id_type=MESH,
-        )
-
-    vertical = (exists(1, 0), exists(-1, 0))
-    from_side = (exists(-1, 0), exists(1, 0))
-    for n in range(2):
-
-        @pl.when(vertical[n])
-        def _():
-            band_copy(n).start()
-
-    _, plain, fluxes = lax.fori_loop(QUARTER // 2, QUARTER, gather, state)
-    for side in range(4):
-        for s in range(3):
-            flux[side, s] = fluxes[side][s]
-
-    def flux_copy(n):
-        if n < 2:
-            source, target, dest = flux.at[n], flux_cols.at[n], device(0, 1 if n == 0 else -1)
-        else:
-            span = pl.ds(8 if n == 2 else 0, 8)
-            source, target, dest = flux.at[n, :, span, :], flux_rows.at[n - 2], device(1 if n == 2 else -1, 0)
-        return pltpu.make_async_remote_copy(
-            src_ref=source,
-            dst_ref=target,
-            send_sem=flux_sem.at[0, n],
-            recv_sem=flux_sem.at[1, n],
-            device_id=dest,
-            device_id_type=MESH,
-        )
-
-    sends = (exists(0, 1), exists(0, -1), exists(1, 0), exists(-1, 0))
-    receives = (exists(0, -1), exists(0, 1), exists(-1, 0), exists(1, 0))
-    for n in range(4):
-
-        @pl.when(sends[n])
-        def _():
-            flux_copy(n).start()
-
-    lane = iota((ROWS, LANES), 1)
-
-    def pack_rows(n, carry):
-        span = pl.ds(pl.multiple_of(n * 8, 8), 8)
-        rows_send[0, span, :] = cells[pl.ds(n * (8 * ROWS) + (ROWS - 1), 8, stride=ROWS), :]
-        rows_send[1, span, :] = cells[pl.ds(n * (8 * ROWS) + HALF * ROWS, 8, stride=ROWS), :]
-        return carry
-
-    lax.fori_loop(0, HALF // 8, pack_rows, 0)
-
-    def edge_lanes(direction, last):
-        base = direction * PER_DIR
-        tile = zero
-        for j in range(NFREQ):
-            value = cells[pl.ds(pl.multiple_of(base + j * ROWS, ROWS), ROWS), :]
-            tile = jnp.where(lane == 2 * j + last, pltpu.roll(value, 2 * j + 2 * last, 1) if (last or j) else value, tile)
-        return tile
-
-    def pack_cols(n, carry):
-        group, part = n // 3, lax.rem(n, 3)
-        eastward = jnp.where(n < QUARTER, n, n + 2 * QUARTER)
-        shift = part * (2 * NFREQ)
-        keep = part > 0
-        cols_send[0, group] = jnp.where(keep, cols_send[0, group], zero) + pltpu.roll(edge_lanes(eastward, 1), shift, 1)
-        cols_send[1, group] = jnp.where(keep, cols_send[1, group], zero) + pltpu.roll(
-            edge_lanes(n + QUARTER, 0), shift, 1
-        )
-        return carry
-
-    cols_send[...] = jnp.zeros_like(cols_send)
-    lax.fori_loop(0, 2 * QUARTER, pack_cols, 0)
-
-    def halo_copy(n):
-        source = cols_send.at[n] if n < 2 else rows_send.at[n - 2]
-        target = cols_out.at[n] if n < 2 else rows_out.at[n - 2]
-        dest = (device(0, 1), device(0, -1), device(1, 0), device(-1, 0))[n]
-        return pltpu.make_async_remote_copy(
-            src_ref=source,
-            dst_ref=target,
-            send_sem=halo_sem.at[0, n],
-            recv_sem=halo_sem.at[1, n],
-            device_id=dest,
-            device_id_type=MESH,
-        )
-
-    def halo_fill(n):
-        source = cols_send.at[n] if n < 2 else rows_send.at[n - 2]
-        target = cols_out.at[n] if n < 2 else rows_out.at[n - 2]
-        return pltpu.make_async_copy(source, target, local_sem.at[n])
-
-    for n in range(4):
-
-        @pl.when(sends[n])
-        def _():
-            halo_copy(n).start()
-
-        @pl.when(jnp.logical_not(receives[n]))
-        def _():
-            halo_fill(n).start()
-
-    for n in range(2):
-
-        @pl.when(from_side[n])
-        def _():
-            band_copy(n).wait_recv()
+    @pl.when(y < groups - 1)
+    def _():
+        for column in range(3):
+            far_arrival(column).wait_recv()
+
+    @pl.when(y > 0)
+    def _():
+        for column in range(PEERS - 3, PEERS):
+            far_arrival(column).wait_recv()
 
     def window_rows(first):
         return jnp.concatenate([window[t, pl.ds(first, SLOTS, stride=SLOTS), :] for t in range(2)], axis=1)
@@ -418,22 +379,23 @@
             place = pl.ds(ROWS * n + c, 8, stride=2)
             fields_out[place, :] = TURN_GAIN * jnp.tanh(coarse[16 * n + 8 * c : 16 * n + 8 * c + 8])
 
-    center = [ocean_shift(wave_masks[c], -MARGIN_W)[:, :LANES] for c in range(2)]
-    west_mask = [ocean_shift(wave_masks[c], 1 - MARGIN_W)[:, :LANES] for c in range(2)]
-    east_mask = [ocean_shift(wave_masks[c], -1 - MARGIN_W)[:, :LANES] for c in range(2)]
-    south_mask = [pltpu.roll(center[1], 1, 0), center[0]]
-    north_mask = [center[1], pltpu.roll(center[0], SLOTS - 1, 0)]
     for c in range(2):
-        fields_out[pl.ds(2 * ROWS + c, 8, stride=2), :] = center[c][:8]
-        for n, other in enumerate((west_mask, east_mask, south_mask, north_mask)):
-            fields_out[pl.ds((3 + n) * ROWS + c, 8, stride=2), :] = (center[c] * other[c])[:8]
+        placed = ocean_shift(wave_masks[c], -MARGIN_W)
+        for t in range(2):
+            mask_window[t, pl.ds(c, SLOTS, stride=2), :] = placed[:, LANES * t : LANES * (t + 1)]
+    around = jnp.concatenate([mask_window[0], mask_window[1]], axis=1)
+    west_mask = around * pltpu.roll(around, 1, 1)
+    east_mask = around * pltpu.roll(around, 2 * LANES - 1, 1)
+    south_mask = around * pltpu.roll(around, 1, 0)
+    north_mask = around * pltpu.roll(around, 2 * ROWS - 1, 0)
+    for n, values in enumerate((around, west_mask, east_mask, south_mask, north_mask)):
+        fields_out[(2 + n) * ROWS : (3 + n) * ROWS, :] = values[:ROWS, :LANES]
 
     def field(n):
         return fields_out[ROWS * n : ROWS * (n + 1), :]
 
     turning = field(0)
     turn_abs = jnp.abs(turning)
-    wave_mask = field(2)
     scale = 0.25 / (NDIR * NFREQ)
     base, along, across = plain[0] * scale, plain[1] * 0.5, plain[2] * 0.5
     turn_c, turn_s = math.cos(2.0 * STEP_ANGLE), math.sin(2.0 * STEP_ANGLE)
@@ -444,37 +406,37 @@
     along = stay * along + turn_abs * along_turn
     across = stay * across + turn_abs * across_turn
     local = [base + along, across, base - along]
-    local = [local[s] - ((fluxes[0][s] + fluxes[1][s]) + (fluxes[2][s] + fluxes[3][s])) for s in range(3)]
-
-    for n in range(4):
-
-        @pl.when(receives[n])
-        def _():
-            flux_copy(n).wait_recv()
-
-    row = iota((ROWS, LANES), 0)
+    west, east, south, north = fluxes
+    rims = zero
     for s in range(3):
-        from_west = jnp.where(lane == 0, pltpu.roll(flux_cols[0, s], 1, 1), pltpu.roll(fluxes[0][s], 1, 1))
-        from_east = jnp.where(
-            lane == LANES - 1, pltpu.roll(flux_cols[1, s], LANES - 1, 1), pltpu.roll(fluxes[1][s], LANES - 1, 1)
-        )
-        from_south = jnp.where(row == 0, flux_rows[0, s, 7:8, :], pltpu.roll(fluxes[2][s], 1, 0))
-        from_north = jnp.where(row == ROWS - 1, flux_rows[1, s, 0:1, :], pltpu.roll(fluxes[3][s], ROWS - 1, 0))
-        stress[0, s, 0:ROWS, :] = (
-            wave_mask * local[s]
-            + field(3) * from_west
-            + field(4) * from_east
-            + field(5) * from_south
-            + field(6) * from_north
-        )
+        partial = field(2) * (local[s] - ((west[s] + east[s]) + (south[s] + north[s])))
+        partial = partial + field(3) * jnp.where(lane == 0, 0.0, pltpu.roll(west[s], 1, 1))
+        partial = partial + field(4) * jnp.where(lane == LANES - 1, 0.0, pltpu.roll(east[s], LANES - 1, 1))
+        partial = partial + field(5) * jnp.where(row == 0, 0.0, pltpu.roll(south[s], 1, 0))
+        partial = partial + field(6) * jnp.where(row == ROWS - 1, 0.0, pltpu.roll(north[s], ROWS - 1, 0))
+        beside_send[s] = partial
+        across_send[0, s] = partial[8:]
+        across_send[0, s, 0:1, :] = south[s][ROWS - 1 :]
+        across_send[1, s] = partial[:8]
+        across_send[1, s, 7:8, :] = north[s][:1]
+        beside_send[4, s : s + 1, :] = south[s][ROWS - 1 :]
+        beside_send[4, 8 + s : 9 + s, :] = north[s][:1]
+        rims = jnp.where(lane == LANES - 1 - s, pltpu.roll(west[s], (LANES - s) % LANES, 1) if s else west[s], rims)
+        rims = jnp.where(lane == s, pltpu.roll(east[s], s, 1) if s else east[s], rims)
+    beside_send[3] = rims
+    across_send[0, 3] = rims[8:]
+    across_send[1, 3] = rims[:8]
 
     def stress_copy(n):
         dy, dx = AROUND[n]
-        source = pl.ds({0: 0, 1: 8, -1: 0}[dy], 16 if dy == 0 else 8)
-        target = pl.ds({0: 0, 1: 24, -1: 16}[dy], 16 if dy == 0 else 8)
+        if dy == 0:
+            source, target = beside_send, beside_land.at[{1: 1, -1: 0}[dx]]
+        else:
+            source = across_send.at[{1: 0, -1: 1}[dy]]
+            target = across_land.at[{0: 0, 1: 2, -1: 1}[dx], {1: 1, -1: 0}[dy]]
         return pltpu.make_async_remote_copy(
-            src_ref=stress.at[0, :, source, :],
-            dst_ref=stress.at[{0: 0, 1: 2, -1: 1}[dx], :, target, :],
+            src_ref=source,
+            dst_ref=target,
             send_sem=stress_sem.at[0, n],
             recv_sem=stress_sem.at[1, n],
             device_id=device(dy, dx),
@@ -486,6 +448,37 @@
         @pl.when(exists(dy, dx))
         def _():
             stress_copy(n).start()
+
+    sends = (exists(0, 1), exists(0, -1), exists(1, 0), exists(-1, 0))
+    receives = (exists(0, -1), exists(0, 1), exists(-1, 0), exists(1, 0))
+
+    def halo_ends(n):
+        return (cols_send, cols_out.at[n]) if n < 2 else (rows_send.at[n - 2], rows_out.at[n - 2])
+
+    def halo_copy(n):
+        source, target = halo_ends(n)
+        return pltpu.make_async_remote_copy(
+            src_ref=source,
+            dst_ref=target,
+            send_sem=halo_sem.at[0, n],
+            recv_sem=halo_sem.at[1, n],
+            device_id=(device(0, 1), device(0, -1), device(1, 0), device(-1, 0))[n],
+            device_id_type=MESH,
+        )
+
+    def halo_fill(n):
+        source, target = halo_ends(n)
+        return pltpu.make_async_copy(source, target, local_sem.at[n])
+
+    for n in range(4):
+
+        @pl.when(sends[n])
+        def _():
+            halo_copy(n).start()
+
+        @pl.when(jnp.logical_not(receives[n]))
+        def _():
+            halo_fill(n).start()
 
     safe = [jnp.where(bottom[c] > 0.0, bottom[c], 1.0) for c in range(3)]
     inverse = [-STRESS_GAIN / safe[c] for c in range(3)]
@@ -508,11 +501,7 @@
     surface = raise_surface(surface, eastward, northward)
     pushed = push(surface, eastward, northward)
     wave_lane, fine = iota(wide, 0), iota(wide, 1)
-    wave_lane = jnp.where(
-        wave_lane < LANES,
-        wave_lane + MARGIN_W,
-        jnp.where(wave_lane < LANES + 64, wave_lane + MARGIN_W, wave_lane - 2 * LANES + MARGIN_W),
-    )
+    wave_lane = jnp.where(wave_lane < LANES + 64, wave_lane + MARGIN_W, wave_lane - 2 * LANES + MARGIN_W)
     first = 2 * (fine // 3)
     part = fine % 3
     hits = jnp.where(wave_lane == first, 1.0, 0.0) * jnp.where(part == 0, 1.0, jnp.where(part == 1, 0.5, 0.0)) + jnp.where(
@@ -526,12 +515,42 @@
         def _():
             stress_copy(n).wait_recv()
 
-    side_lane = iota((SLOTS, LANES), 1)
+    side_lane = iota((2 * ROWS, LANES), 1) < 64
+
+    def assemble(s):
+        columns = [
+            jnp.concatenate([body, across_land[n, 0, s], across_land[n, 1, s]], axis=0)
+            for n, body in enumerate((beside_send[s], beside_land[0, s], beside_land[1, s]))
+        ]
+        return jnp.concatenate([columns[0], jnp.where(side_lane, columns[1], columns[2])], axis=1)
+
+    def edge_row(place):
+        rows = [ref[place : place + 1, :] for ref in (beside_send.at[4], beside_land.at[0, 4], beside_land.at[1, 4])]
+        return jnp.concatenate([rows[0], jnp.where(side_lane[:1], rows[1], rows[2])], axis=1)
+
+    around_row = iota((2 * ROWS, 2 * LANES), 0)
+    around_lane = iota((2 * ROWS, 2 * LANES), 1)
+    west_side = west_mask * jnp.where(around_lane % LANES == 0, 1.0, 0.0)
+    east_side = east_mask * jnp.where(around_lane % LANES == LANES - 1, 1.0, 0.0)
+    side_flux = assemble(3)
     pieces = []
     for s in range(3):
+        body = assemble(s)
+        from_south = jnp.where(
+            around_row == 0, body[24:25], jnp.where(around_row == ROWS, edge_row(s), 0.0)
+        )
+        from_north = jnp.where(
+            around_row == ROWS - 1, body[23:24], jnp.where(around_row == 2 * ROWS - 1, edge_row(8 + s), 0.0)
+        )
+        body = body + west_side * pltpu.roll(side_flux, s + 1, 1)
+        body = body + east_side * pltpu.roll(side_flux, 2 * LANES - 1 - s, 1)
+        body = body + south_mask * from_south + north_mask * from_north
+        for t in range(2):
+            stress[s, t] = body[:, LANES * t : LANES * (t + 1)]
         for c in range(2):
-            own, right, left = [stress[n, s, pl.ds(c, SLOTS, stride=2), :] for n in range(3)]
-            pieces.append(jnp.concatenate([own, jnp.where(side_lane < 64, right, left)], axis=1))
+            pieces.append(
+                jnp.concatenate([stress[s, t, pl.ds(c, SLOTS, stride=2), :] for t in range(2)], axis=1)
+            )
     spread_stress = exact_dot(jnp.concatenate(pieces, axis=0), prolong)
     tensor = []
     for s in range(3):
@@ -593,11 +612,11 @@
     for step in range(1, PEERS):
         pack_copy(step).wait_send()
         result_copy(step).wait_send()
-    for n in range(2):
-
-        @pl.when(vertical[n])
-        def _():
-            band_copy(n).wait_send()
+
+    @pl.when(far)
+    def _():
+        for column in range(PEERS):
+            far_copy(column).wait_send()
 
     for n, (dy, dx) in enumerate(AROUND):
 
@@ -609,7 +628,6 @@
 
         @pl.when(sends[n])
         def _():
-            flux_copy(n).wait_send()
             halo_copy(n).wait_send()
 
         @pl.when(receives[n])
@@ -621,7 +639,23 @@
             halo_fill(n).wait()
 
 
-def wave_kernel(spectrum, fields, rows_in, cols_in, out, cells, updated, beside, rows, cols, load_sem, store_sem, halo_sem):
+def wave_kernel(
+    spectrum,
+    fields,
+    rows_in,
+    cols_in,
+    ocean_in,
+    out,
+    ocean_out,
+    cells,
+    updated,
+    beside,
+    rows,
+    cols,
+    load_sem,
+    store_sem,
+    halo_sem,
+):
     def load(direction):
         return pltpu.make_async_copy(
             spectrum.at[pl.ds(direction * NFREQ, NFREQ)],
@@ -636,6 +670,8 @@
     halos = [pltpu.make_async_copy(rows_in, rows, halo_sem.at[0]), pltpu.make_async_copy(cols_in, cols, halo_sem.at[1])]
     for copy in halos:
         copy.start()
+    handed = pltpu.make_async_copy(ocean_in, ocean_out, halo_sem.at[2])
+    handed.start()
     for q in range(4):
         load(q * QUARTER + QUARTER - 1).start()
     for q in range(4):
@@ -681,20 +717,25 @@
             columns.append(pltpu.roll(merged, lax.rem(LANES - part * (2 * NFREQ), LANES), 1))
         return columns
 
-    def prepare(i, h, j, columns):
-        rim = [pltpu.roll(column, LANES - 1 - 2 * j, 1) for column in columns]
+    def rim_at(columns, j):
+        return [pltpu.roll(column, LANES - 1 - 2 * j, 1) for column in columns]
+
+    def prepare(i, h, j, columns, rim):
+        following = rim_at(columns, j + 1)
         for q in range(4):
             value = cell(q * QUARTER + i, j, 8 * h)
             if q in (0, 3):
                 moved = jnp.where(lane == 0, rim[q // 2], pltpu.roll(value, 1, 1))
             else:
-                moved = jnp.where(lane == LANES - 1, rim[q // 2], pltpu.roll(value, LANES - 1, 1))
+                moved = jnp.where(lane == LANES - 1, following[q // 2], pltpu.roll(value, LANES - 1, 1))
             beside[q * NFREQ + j, 8 * h : 8 * h + 8, :] = moved
+        return following
 
     def update(i, cosine, sine):
         following_step = jnp.minimum(i + 1, QUARTER - 1)
         for h in range(2):
             columns = rims(following_step, h)
+            rim = rim_at(columns, 0)
             turn_left = half(0, h) > 0.0
             shift_up = half(1, h) > 0.0
             mask = half(2, h)
@@ -729,7 +770,7 @@
                         total = total - faces[q]
                         values[q] = following
                     updated[direction * NFREQ + j, 8 * h : 8 * h + 8, :] = total
-                prepare(following_step, h, j, columns)
+                rim = prepare(following_step, h, j, columns, rim)
 
     for q in range(4):
         load(q * QUARTER + QUARTER - 1).wait()
@@ -737,8 +778,9 @@
         load(q * QUARTER).wait()
     for h in range(2):
         first_columns = rims(0, h)
+        first_rim = rim_at(first_columns, 0)
         for j in range(NFREQ):
-            prepare(0, h, j, first_columns)
+            first_rim = prepare(0, h, j, first_columns, first_rim)
 
     def one_step(i, angle):
         @pl.when(i < QUARTER - 2)
@@ -758,6 +800,7 @@
         return carry
 
     lax.fori_loop(0, NDIR, finish, 0)
+    handed.wait()
 
 
 def shards(mesh_shape, spectrum, sea_mask, ocean_state, depth):
@@ -768,7 +811,7 @@
     anywhere = pl.BlockSpec(memory_space=pl.ANY)
     f32 = jnp.float32
     dma = pltpu.SemaphoreType.DMA
-    ocean_out, fields, rows, cols = pl.pallas_call(
+    ocean_part, fields, rows, cols = pl.pallas_call(
         functools.partial(coupled_kernel, groups_y, groups),
         out_shape=(
             jax.ShapeDtypeStruct(ocean_state.shape, f32),
@@ -776,27 +819,32 @@
             jax.ShapeDtypeStruct((2, HALF, LANES), f32),
             jax.ShapeDtypeStruct((2, 6, ROWS, LANES), f32),
         ),
-        in_specs=[anywhere, vmem, vmem, vmem],
+        in_specs=[anywhere] * 4,
         out_specs=(vmem, vmem, anywhere, anywhere),
         scratch_shapes=[
             pltpu.VMEM((CELLS, LANES), f32),
+            pltpu.VMEM(ocean_state.shape, f32),
+            pltpu.VMEM(depth.shape, f32),
+            pltpu.VMEM(sea_mask.shape, jnp.int32),
             pltpu.VMEM((SLOTS, 1792), f32),
             pltpu.VMEM((SLOTS, 1280), f32),
             pltpu.VMEM((PEERS, 2, SLOTS, LANES), f32),
             pltpu.VMEM((2, SLOTS * SLOTS, LANES), f32),
-            pltpu.VMEM((4, 3, ROWS, LANES), f32),
-            pltpu.VMEM((2, 3, ROWS, LANES), f32),
-            pltpu.VMEM((2, 3, 8, LANES), f32),
-            pltpu.VMEM((3, 3, 32, LANES), f32),
+            pltpu.VMEM((2, 2 * ROWS, LANES), f32),
+            pltpu.VMEM((5, ROWS, LANES), f32),
+            pltpu.VMEM((2, 4, 8, LANES), f32),
+            pltpu.VMEM((2, 5, ROWS, LANES), f32),
+            pltpu.VMEM((3, 2, 4, 8, LANES), f32),
+            pltpu.VMEM((3, 2, 2 * ROWS, LANES), f32),
             pltpu.VMEM((2, 72, LANES), f32),
             pltpu.VMEM((PEERS, 2, SLOTS, LANES), f32),
             pltpu.VMEM((PEERS, 2, SLOTS, LANES), f32),
             pltpu.VMEM((2, HALF, LANES), f32),
-            pltpu.VMEM((2, 6, ROWS, LANES), f32),
+            pltpu.VMEM((6, ROWS, LANES), f32),
+            dma((3,)),
             dma((NDIR,)),
             dma((2, PEERS)),
-            dma((2, 2)),
-            dma((2, 4)),
+            dma((2, PEERS)),
             dma((2, 8)),
             dma((2, PEERS)),
             dma((2, 4)),
@@ -807,11 +855,14 @@
         ),
         name="coupled",
     )(cells, sea_mask, ocean_state, depth)
-    spectrum_out = pl.pallas_call(
+    spectrum_out, ocean_out = pl.pallas_call(
         wave_kernel,
-        out_shape=jax.ShapeDtypeStruct((NDIR * NFREQ, ROWS, LANES), f32),
-        in_specs=[anywhere, vmem, anywhere, anywhere],
-        out_specs=anywhere,
+        out_shape=(
+            jax.ShapeDtypeStruct((NDIR * NFREQ, ROWS, LANES), f32),
+            jax.ShapeDtypeStruct(ocean_state.shape, f32),
+        ),
+        in_specs=[anywhere, vmem, anywhere, anywhere, anywhere],
+        out_specs=(anywhere, anywhere),
         scratch_shapes=[
             pltpu.VMEM((NDIR * NFREQ + 1, PITCH, LANES), f32),
             pltpu.VMEM((NDIR * NFREQ, ROWS, LANES), f32),
@@ -820,11 +871,11 @@
             pltpu.VMEM((2, 6, ROWS, LANES), f32),
             dma((NDIR,)),
             dma((NDIR,)),
-            dma((2,)),
+            dma((3,)),
         ],
         compiler_params=pltpu.CompilerParams(vmem_limit_bytes=VMEM_LIMIT),
         name="wave",
-    )(spectrum.reshape(NDIR * NFREQ, ROWS, LANES), fields, rows, cols)
+    )(spectrum.reshape(NDIR * NFREQ, ROWS, LANES), fields, rows, cols, ocean_part)
     return (spectrum_out.reshape(spectrum.shape), ocean_out)
 
 

time: 41.4 us -> 36.2 us (0.87)
  Pallas kernels: 40 us -> 35.4 us
  local copies, waits for them, and re-layouts: 0.64 us -> 0 us
    pallas_call x1, Pallas kernels: 31.7 us -> 27.4 us  [shards(): pl.pallas_call(functools.partial(coupled_kernel, groups_y, groups), out_s...]
    unnamed x3 -> x0, local copies, waits for them, and re-layouts: 0.64 us -> none
where the time goes in v3:
time: 36.2 us; the launch traced here: 36 us
  Pallas kernels  35.4 us (98%)
  between operations  0.64 us (2%)
    pallas_call x1, Pallas kernels, shards(): pl.pallas_call(functools.partial(coupled_kernel, groups_y, groups), out_s...  27.4 us
    pallas_call x1, Pallas kernels, shards(): pl.pallas_call(wave_kernel, out_shape=(jax.ShapeDtypeStruct((NDIR * NFREQ...  7.97 us

profile of v3, /device:TPU:25, one launch (start us, length us, event | category | flops | bytes accessed | tf_op | source)
XLA Modules:
  0.0 36.0 jit_solution(310997208194451046)
XLA Ops:
  0.6 27.4 %coupled.1 = (f32[3,3,1536]{2,1,0:T(4,128)}, f32[112,128]{1,0:T(8,128)}, f32[2,360,128]{2,1,0:T(8,128)}, f32[2,6,16,128]{3,2,1,0:T(8,128)}) custom-call(f32[11520,128]{1,0:T(8,128)} %bitcast.3, s32[2,1024]{1,0:T(2,128)} %sea_mask.1, f32[3,3,1536]{2,1,0:T(4,128)} %ocean_state.1, f32[3,1536]{1,0:T(4,128)} %depth.1), custom_call_target="tpu_custom_call" | custom-call | tf_op jit(solution)/shard_map/coupled/pallas_call | solution.py:814
  28.1 8.0 %wave.1 = (f32[720,16,128]{2,1,0:T(8,128)}, f32[3,3,1536]{2,1,0:T(4,128)}) custom-call(f32[720,16,128]{2,1,0:T(8,128)} %bitcast.4, f32[112,128]{1,0:T(8,128)} %get-tuple-element.8.fields, f32[2,360,128]{2,1,0:T(8,128)} %get-tuple-element.9.rows_in, f32[2,6,16,128]{3,2,1,0:T(8,128)} %get-tuple-element.10.cols_in, f32[3,3,1536]{2,1,0:T(4,128)} %get-tuple-element.11.ocean_in), custom_call_target="tpu_custom_call" | custom-call | tf_op jit(solution)/shard_map/wave/pallas_call | solution.py:858

commit v4 on v3

v4 whole, which is shorter than its diff:
```python
import functools
import math

import jax
import jax.numpy as jnp
from jax import lax
from jax.experimental import pallas as pl
from jax.experimental.pallas import tpu as pltpu
from jax.sharding import PartitionSpec as P

ITERS = 4
GRAVITY_STEP = 0.3
CORIOLIS_STEP = 0.2
STRESS_GAIN = 2.0
TURN_GAIN = 0.2
SPEED_BASE = 0.35
SPEED_RATIO = 0.9

NDIR = 36
NFREQ = 20
ROWS = 16
LANES = 128
CELLS = NDIR * NFREQ * ROWS
PER_DIR = NFREQ * ROWS
QUARTER = NDIR // 4
PAD = 8
DURING_STRESS = 5
CHUNKS = 8
LOADS = 3
VMEM_LIMIT = 28 * 1024 * 1024
HALF = NDIR // 2 * NFREQ
PEERS = 8
SLOTS = 16
MARGIN_O = 24
MARGIN_W = 16
SPEEDS = [SPEED_BASE * SPEED_RATIO**j for j in range(NFREQ)]
STEP_ANGLE = 2.0 * math.pi / NDIR
MESH = pl.DeviceIdType.MESH
AROUND = [(1, 0), (-1, 0), (0, 1), (0, -1), (1, 1), (1, -1), (-1, 1), (-1, -1)]


def iota(shape, dim):
    return lax.broadcasted_iota(jnp.int32, shape, dim)


def next_angle(cosine, sine):
    turn_c, turn_s = math.cos(STEP_ANGLE), math.sin(STEP_ANGLE)
    return cosine * turn_c - sine * turn_s, sine * turn_c + cosine * turn_s


def angle_at(i):
    return jnp.float32(math.cos((i + 0.5) * STEP_ANGLE)), jnp.float32(math.sin((i + 0.5) * STEP_ANGLE))


def exact_dot(values, weights):
    rows = values.shape[0]
    high = values.astype(jnp.bfloat16)
    rest = values - high.astype(jnp.float32)
    middle = rest.astype(jnp.bfloat16)
    low = (rest - middle.astype(jnp.float32)).astype(jnp.bfloat16)
    stacked = jnp.concatenate([high, middle, low], axis=0)
    product = jnp.dot(stacked, weights, preferred_element_type=jnp.float32)
    return product[:rows] + product[rows : 2 * rows] + product[2 * rows :]


def ocean_shift(values, amount):
    return pltpu.roll(values, amount % values.shape[1], 1)


def along_x(values):
    return (ocean_shift(values, -1) - ocean_shift(values, 1)) * 0.5


def along_y(classes):
    above = [classes[1], classes[2], pltpu.roll(classes[0], SLOTS - 1, 0)]
    below = [pltpu.roll(classes[2], 1, 0), classes[0], classes[1]]
    return [(above[c] - below[c]) * 0.5 for c in range(3)]


def wave_tools(fields, rows, cols, cells, beside, target):
    lane = iota((8, LANES), 1)
    row = iota((8, LANES), 0)

    def half(n, h):
        return fields[ROWS * n + 8 * h : ROWS * n + 8 * h + 8, :]

    def turn_part(h):
        return half(2, h) * jnp.abs(half(0, h))

    def cell(direction, j, offset):
        place = direction * PER_DIR + (PAD + j * ROWS + offset)
        return cells[pl.ds(pl.multiple_of(place, 8) if offset % 8 == 0 else place, 8), :]

    odd = lax.rem(lane, 2) == 1

    def rims(i, h):
        columns = []
        for place in (i, QUARTER + i):
            group, part = place // 3, lax.rem(place, 3)
            span = slice(8 * h, 8 * h + 8)
            merged = jnp.where(odd, cols[0, group, span, :], cols[1, group, span, :])
            columns.append(pltpu.roll(merged, lax.rem(LANES - part * (2 * NFREQ), LANES), 1))
        return columns

    def rim_at(columns, j):
        return [pltpu.roll(column, LANES - 1 - 2 * j, 1) for column in columns]

    def prepare(i, h, j, columns, rim):
        following = rim_at(columns, j + 1)
        for q in range(4):
            value = cell(q * QUARTER + i, j, 8 * h)
            if q in (0, 3):
                moved = jnp.where(lane == 0, rim[q // 2], pltpu.roll(value, 1, 1))
            else:
                moved = jnp.where(lane == LANES - 1, following[q // 2], pltpu.roll(value, LANES - 1, 1))
            beside[q * NFREQ + j, 8 * h : 8 * h + 8, :] = moved
        return following

    def update(i, angle):
        cosine, sine = angle
        following_step = jnp.minimum(i + 1, QUARTER - 1)
        for h in range(2):
            columns = rims(following_step, h)
            rim = rim_at(columns, 0)
            turn_left = half(0, h) > 0.0
            shift_up = half(1, h) > 0.0
            mask = half(2, h)
            turned = turn_part(h)
            stay = mask - turned
            shifted = mask * half(1, h)
            leave = mask * (cosine + sine)
            factors = []
            for q in range(4):
                speed_x, speed_y = (cosine, sine) if q % 2 == 0 else (sine, cosine)
                inner = half(5 if q in (0, 1) else 6, h) * speed_y
                if q in (0, 1) and h == 0:
                    inner = jnp.where(row == 0, 0.0, inner)
                if q in (2, 3) and h == 1:
                    inner = jnp.where(row == 7, 0.0, inner)
                factors.append((half(3 if q in (0, 3) else 4, h) * speed_x, inner))
            values = [cell(q * QUARTER + i, 0, 8 * h) for q in range(4)]
            faces = [None] * 4
            for j in range(NFREQ):
                keep = stay - SPEEDS[j] * leave
                for q in range(4):
                    direction = q * QUARTER + i
                    before, after = direction - 1, direction + 1
                    if q == 0:
                        before = jnp.where(i == 0, NDIR - 1, before)
                    if q == 3:
                        after = jnp.where(i == QUARTER - 1, 0, after)
                    along = cell(direction, j, 8 * h + (-1 if q in (0, 1) else 1))
                    moved = factors[q][0] * beside[q * NFREQ + j, 8 * h : 8 * h + 8, :] + factors[q][1] * along
                    total = keep * values[q] + SPEEDS[j] * moved
                    total = total + turned * jnp.where(turn_left, cell(before, j, 8 * h), cell(after, j, 8 * h))
                    if j > 0:
                        total = total + faces[q]
                    if j < NFREQ - 1:
                        following = cell(direction, j + 1, 8 * h)
                        faces[q] = shifted * jnp.where(shift_up, values[q], following)
                        total = total - faces[q]
                        values[q] = following
                    place = (direction * NFREQ + j) * ROWS + 8 * h
                    target[pl.ds(pl.multiple_of(place, 8), 8), :] = total
                rim = prepare(following_step, h, j, columns, rim)

    def prepare_first():
        for h in range(2):
            columns = rims(0, h)
            rim = rim_at(columns, 0)
            for j in range(NFREQ):
                rim = prepare(0, h, j, columns, rim)

    def finish_rows(i, angle):
        for q in range(4):
            speed_y = angle[1] if q % 2 == 0 else angle[0]
            from_south = q in (0, 1)
            edge = (5 * ROWS) if from_south else (7 * ROWS - 1)
            factor = fields[edge : edge + 1, :] * speed_y
            direction = q * QUARTER + i
            source = (direction if from_south else direction - 2 * QUARTER) * NFREQ
            for first in (0, 8, 16):
                count = min(8, NFREQ - first)
                speeds = jnp.zeros((count, LANES), jnp.float32)
                for r in range(count):
                    speeds = jnp.where(row[:count] == r, SPEEDS[first + r], speeds)
                span = pl.ds((direction * NFREQ + first) * ROWS + (0 if from_south else ROWS - 1), count, stride=ROWS)
                rim = rows[0 if from_south else 1, pl.ds(source + first, count), :]
                target[span, :] = target[span, :] + speeds * (factor * rim)

    return prepare_first, update, finish_rows


def coupled_kernel(
    groups_y,
    groups,
    spectrum,
    sea_mask,
    ocean_state,
    depth,
    ocean_out,
    updated,
    fields_out,
    rows_out,
    cols_out,
    cells,
    beside,
    state_in,
    depth_in,
    mask_in,
    raw,
    raw_mask,
    pack,
    pack_late,
    window,
    window_late,
    brink,
    mask_window,
    beside_send,
    across_send,
    beside_land,
    across_land,
    stress,
    result,
    result_send,
    result_land,
    rows_send,
    cols_send,
    input_sem,
    load_sem,
    pack_sem,
    late_sem,
    far_sem,
    band_sem,
    stress_sem,
    result_sem,
    halo_sem,
    local_sem,
):
    x = lax.axis_index("gx")
    y = lax.axis_index("sec") * groups_y + lax.axis_index("gy")

    def exists(dy, dx):
        checks = []
        if dy > 0:
            checks.append(y < groups - 1)
        if dy < 0:
            checks.append(y > 0)
        if dx > 0:
            checks.append(x < PEERS - 1)
        if dx < 0:
            checks.append(x > 0)
        answer = checks[0]
        for check in checks[1:]:
            answer = jnp.logical_and(answer, check)
        return answer

    def device_at(row, column):
        return (row // groups_y, lax.rem(row, groups_y), column)

    def device(dy, dx):
        return device_at(y + dy, x + dx)

    def peer(step):
        return (lax.axis_index("sec"), lax.axis_index("gy"), lax.rem(x + step, PEERS))

    inputs = [
        pltpu.make_async_copy(ocean_state, state_in, input_sem.at[0]),
        pltpu.make_async_copy(depth, depth_in, input_sem.at[1]),
        pltpu.make_async_copy(sea_mask, mask_in, input_sem.at[2]),
    ]
    for copy in inputs:
        copy.start()

    barrier = pltpu.get_barrier_semaphore()
    for step in range(1, PEERS):
        pl.semaphore_signal(barrier, inc=1, device_id=peer(step), device_id_type=MESH)
    greeted = PEERS - 1
    for dy in (1, -1):
        here = exists(dy, 0)

        @pl.when(here)
        def _():
            for column in range(PEERS):
                pl.semaphore_signal(barrier, inc=1, device_id=device_at(y + dy, column), device_id_type=MESH)

        greeted = greeted + here.astype(jnp.int32) * PEERS

    def load(q, part):
        size = QUARTER // LOADS * PER_DIR
        start = pl.multiple_of(q * (QUARTER * PER_DIR) + part * size, PER_DIR)
        return pltpu.make_async_copy(
            spectrum.at[pl.ds(start, size)],
            cells.at[pl.ds(pl.multiple_of(start + PAD, 8), size)],
            load_sem.at[part * 4 + q],
        )

    for part in range(LOADS):
        for q in range(4):
            load(q, part).start()

    raw[...] = jnp.zeros_like(raw)
    raw_mask[...] = jnp.zeros_like(raw_mask)
    width = state_in.shape[2]
    for copy in inputs:
        copy.wait()
    raw[0:3, :width] = state_in[1]
    raw[3:6, :width] = state_in[2]
    raw[8:11, :width] = state_in[0]
    raw[11:14, :width] = depth_in[...]
    raw_mask[6:8, : mask_in.shape[1]] = mask_in[...].astype(jnp.float32)
    even = ocean_shift(raw[...], MARGIN_O)
    odd = ocean_shift(raw[...], MARGIN_O - 64)
    mask_rows = ocean_shift(raw_mask[...], MARGIN_W)
    is_ocean = iota((8, LANES), 0) < 6
    for dest in range(PEERS):
        source = odd if dest % 2 else even
        origin = 384 * (dest // 2) + (128 if dest % 2 else 0)
        for tile in range(2):
            piece = source[:, origin + LANES * tile : origin + LANES * (tile + 1)]
            pack[dest, tile] = jnp.where(
                is_ocean, piece[:8], mask_rows[:, LANES * (dest + tile) : LANES * (dest + tile + 1)]
            )
            pack_late[dest, tile] = piece[8:]

    slot = pl.ds(pl.multiple_of(x * 8, 8), 8)

    def pack_copy(step, late):
        dest = peer(step)
        return pltpu.make_async_remote_copy(
            src_ref=(pack_late if late else pack).at[dest[2]],
            dst_ref=(window_late if late else window).at[:, slot, :],
            send_sem=(late_sem if late else pack_sem).at[0, step],
            recv_sem=(late_sem if late else pack_sem).at[1, step],
            device_id=dest,
            device_id_type=MESH,
        )

    last, first = x == PEERS - 1, x == 0
    to_north, to_south = jnp.logical_and(last, y < groups - 1), jnp.logical_and(first, y > 0)

    def brink_copy(n, column):
        return pltpu.make_async_remote_copy(
            src_ref=pack.at[column],
            dst_ref=brink.at[n],
            send_sem=far_sem.at[n, column],
            recv_sem=far_sem.at[2, n],
            device_id=device_at(y + (1 if n == 0 else -1), column),
            device_id_type=MESH,
        )

    pl.semaphore_wait(barrier, greeted)
    for n, needed in enumerate((to_north, to_south)):

        @pl.when(needed)
        def _():
            for column in range(PEERS):
                brink_copy(n, column).start()

    for step in range(1, PEERS):
        pack_copy(step, False).start()
    for step in range(1, PEERS):
        pack_copy(step, True).start()
    mask_window[...] = jnp.zeros_like(mask_window)
    cells[:PAD, :] = jnp.zeros((PAD, LANES), jnp.float32)
    cells[PAD + CELLS :, :] = jnp.zeros((PAD, LANES), jnp.float32)
    for ref in (window, window_late):
        ref[:, 11 * 8 : 13 * 8, :] = jnp.zeros((2, 16, LANES), jnp.float32)
    edge = jnp.zeros((2, 24, LANES), jnp.float32)

    @pl.when(y == 0)
    def _():
        window[:, 13 * 8 : 16 * 8, :] = edge
        window_late[:, 13 * 8 : 16 * 8, :] = edge
        brink[0] = jnp.zeros((2, 8, LANES), jnp.float32)
        across_land[:, 1] = jnp.zeros((3, 4, 8, LANES), jnp.float32)

    @pl.when(y == groups - 1)
    def _():
        window[:, 8 * 8 : 11 * 8, :] = edge
        window_late[:, 8 * 8 : 11 * 8, :] = edge
        brink[1] = jnp.zeros((2, 8, LANES), jnp.float32)
        across_land[:, 0] = jnp.zeros((3, 4, 8, LANES), jnp.float32)

    @pl.when(x == 0)
    def _():
        beside_land[1] = jnp.zeros((5, ROWS, LANES), jnp.float32)
        across_land[2] = jnp.zeros((2, 4, 8, LANES), jnp.float32)

    @pl.when(x == PEERS - 1)
    def _():
        beside_land[0] = jnp.zeros((5, ROWS, LANES), jnp.float32)
        across_land[1] = jnp.zeros((2, 4, 8, LANES), jnp.float32)

    window[:, slot, :] = pack[x]
    window_late[:, slot, :] = pack_late[x]

    lane = iota((ROWS, LANES), 1)
    row = iota((ROWS, LANES), 0)
    zero = jnp.zeros((ROWS, LANES), jnp.float32)

    def gather(i, carry):
        (cosine, sine), plain, fluxes = carry
        part = QUARTER // LOADS

        @pl.when(lax.rem(i, part) == 0)
        def _():
            for q in range(4):
                load(q, i // part).wait()

        totals, weighted, rims = [None] * 4, [None] * 4, [zero, zero]
        for j in range(NFREQ):
            values = []
            for q in range(4):
                base = (q * QUARTER + i) * PER_DIR + PAD
                values.append(cells[pl.ds(pl.multiple_of(base + j * ROWS, 8), ROWS), :])
                scaled = values[q] * SPEEDS[j]
                totals[q] = values[q] if j == 0 else totals[q] + values[q]
                weighted[q] = scaled if j == 0 else weighted[q] + scaled
            here = jnp.logical_or(lane == 2 * j + 1, lane == 2 * j + 2)
            for n, (east, west) in enumerate(((0, 1), (3, 2))):
                both = jnp.where(lane == LANES - 1, values[east], values[west])
                rims[n] = jnp.where(here, pltpu.roll(both, 2 * j + 2, 1), rims[n])
        for n in range(2):
            place = i + n * QUARTER
            group, part = place // 3, lax.rem(place, 3)
            earlier = jnp.where(part > 0, cols_send[group], zero)
            cols_send[group] = earlier + pltpu.roll(rims[n], part * (2 * NFREQ), 1)
        scale = 0.5 / (NDIR * NFREQ)
        cc, cs, ss = cosine * cosine * scale, cosine * sine * scale, sine * sine * scale
        pair = (totals[0] + totals[2]) - (totals[1] + totals[3])
        plain = (
            plain[0] + ((totals[0] + totals[2]) + (totals[1] + totals[3])),
            plain[1] + (cc - ss) * pair,
            plain[2] + (2.0 * cs) * pair,
        )
        straight, crossed = (cc, cs, ss), (ss, -cs, cc)
        west, east, south, north = fluxes
        west = tuple(
            west[s] + (cosine * straight[s]) * weighted[0] + (sine * crossed[s]) * weighted[3] for s in range(3)
        )
        east = tuple(
            east[s] + (cosine * straight[s]) * weighted[2] + (sine * crossed[s]) * weighted[1] for s in range(3)
        )
        south = tuple(
            south[s] + (sine * straight[s]) * weighted[0] + (cosine * crossed[s]) * weighted[1] for s in range(3)
        )
        north = tuple(
            north[s] + (sine * straight[s]) * weighted[2] + (cosine * crossed[s]) * weighted[3] for s in range(3)
        )
        return next_angle(cosine, sine), plain, (west, east, south, north)

    cols_send[...] = jnp.zeros_like(cols_send)
    triple = (zero, zero, zero)
    carry = (angle_at(0), triple, (triple, triple, triple, triple))
    _, plain, fluxes = lax.fori_loop(0, QUARTER, gather, carry)

    def pack_rows(n, carry):
        for m in range(5):
            start = n * 40 + m * 8
            span = pl.ds(pl.multiple_of(start, 8), 8)
            rows_send[0, span, :] = cells[pl.ds(start * ROWS + (PAD + ROWS - 1), 8, stride=ROWS), :]
            rows_send[1, span, :] = cells[pl.ds(start * ROWS + (PAD + HALF * ROWS), 8, stride=ROWS), :]
        return carry

    lax.fori_loop(0, HALF // 40, pack_rows, 0)

    sends = (exists(0, 1), exists(0, -1), exists(1, 0), exists(-1, 0))
    receives = (exists(0, -1), exists(0, 1), exists(-1, 0), exists(1, 0))

    def halo_ends(n):
        return (cols_send, cols_out.at[n]) if n < 2 else (rows_send.at[n - 2], rows_out.at[n - 2])

    def halo_copy(n):
        source, target = halo_ends(n)
        return pltpu.make_async_remote_copy(
            src_ref=source,
            dst_ref=target,
            send_sem=halo_sem.at[0, n],
            recv_sem=halo_sem.at[1, n],
            device_id=(device(0, 1), device(0, -1), device(1, 0), device(-1, 0))[n],
            device_id_type=MESH,
        )

    def halo_fill(n):
        source, target = halo_ends(n)
        return pltpu.make_async_copy(source, target, local_sem.at[n])

    def start_halo(n):
        @pl.when(sends[n])
        def _():
            halo_copy(n).start()

        @pl.when(jnp.logical_not(receives[n]))
        def _():
            halo_fill(n).start()

    def wait_halo(n):
        @pl.when(receives[n])
        def _():
            halo_copy(n).wait_recv()

        @pl.when(jnp.logical_not(receives[n]))
        def _():
            halo_fill(n).wait()

    start_halo(0)
    start_halo(1)

    for step in range(1, PEERS):
        pack_copy(step, False).wait_recv()

    def band_copy(n, late):
        source = pl.ds((5 if n == 0 else 0) * 8, 24)
        target = pl.ds((13 if n == 0 else 8) * 8, 24)
        ref = window_late if late else window
        return pltpu.make_async_remote_copy(
            src_ref=ref.at[:, source, :],
            dst_ref=ref.at[:, target, :],
            send_sem=band_sem.at[0, 2 * n + late],
            recv_sem=band_sem.at[1, 2 * n + late],
            device_id=device(1 if n == 0 else -1, 0),
            device_id_type=MESH,
        )

    vertical = (exists(1, 0), exists(-1, 0))
    from_side = (exists(-1, 0), exists(1, 0))
    for n in range(2):

        @pl.when(vertical[n])
        def _():
            band_copy(n, 0).start()

    for n in range(2):

        @pl.when(from_side[n])
        def _():
            brink_copy(n, 0).wait_recv()

    def tiles_of(ref, rows):
        return jnp.concatenate([ref[t, rows, :] for t in range(2)], axis=1)

    def own_rows(first):
        return tiles_of(window, pl.ds(first, 8, stride=8))

    def brink_row(n, place):
        return tiles_of(brink.at[n], pl.ds(place, 1))

    wide = (2 * LANES, 2 * LANES)
    spread = (iota(wide, 0) == (2 * iota(wide, 1)) // 3).astype(jnp.bfloat16)
    wave_masks = [own_rows(6), own_rows(7)]
    brink_masks = [brink_row(0, 7), brink_row(1, 6)]
    top = iota((8, 2 * LANES), 0) == 0
    bottom_row = iota((8, 2 * LANES), 0) == 7
    both = jnp.where(top, brink_masks[0], brink_masks[1])
    masks = jnp.dot(
        jnp.concatenate(wave_masks + [both], axis=0).astype(jnp.bfloat16), spread, preferred_element_type=jnp.float32
    )
    near_mask = [masks[:8], masks[:8], masks[8:16]]
    brink_ocean = [masks[16:17], masks[17:18]]

    def near(base):
        inner = [own_rows(base + c) * near_mask[c] for c in range(3)]
        below = jnp.where(top, brink_row(0, base + 2) * brink_ocean[0], pltpu.roll(inner[2], 1, 0))
        above = jnp.where(bottom_row, brink_row(1, base) * brink_ocean[1], pltpu.roll(inner[0], 7, 0))
        slope = [(inner[1] - below) * 0.5, (inner[2] - inner[0]) * 0.5, (above - inner[1]) * 0.5]
        return inner, slope

    (near_east, east_y), (near_north, north_y) = near(0), near(3)
    vorticity = [along_x(near_north[c]) - east_y[c] for c in range(3)]
    divergence = [along_x(near_east[c]) + north_y[c] for c in range(3)]
    coarse = []
    for field in (vorticity, divergence):
        coarse.append(2.0 * field[0] + field[1])
        coarse.append(field[1] + 2.0 * field[2])
    narrow = (2 * LANES, LANES)
    fine, wave = iota(narrow, 0), iota(narrow, 1) + MARGIN_W
    group = 3 * (wave // 2)
    ends = jnp.where(wave % 2 == 0, group, group + 2)
    weights = jnp.where(fine == ends, 2.0, jnp.where(fine == group + 1, 1.0, 0.0)).astype(jnp.bfloat16)
    coarse = exact_dot(jnp.concatenate(coarse, axis=0), weights) * (1.0 / 9.0)
    for n in range(2):
        for c in range(2):
            place = pl.ds(ROWS * n + c, 8, stride=2)
            fields_out[place, :] = TURN_GAIN * jnp.tanh(coarse[16 * n + 8 * c : 16 * n + 8 * c + 8])

    for c in range(2):
        placed = ocean_shift(wave_masks[c], -MARGIN_W)
        rim_mask = ocean_shift(brink_masks[1 - c], -MARGIN_W)
        for t in range(2):
            span = slice(LANES * t, LANES * (t + 1))
            mask_window[t, pl.ds(c, 8, stride=2), :] = placed[:, span]
            mask_window[t, 16 if c == 0 else 31, :] = rim_mask[0, span]

    def mask_products():
        around = tiles_of(mask_window, slice(None))
        return (
            around,
            around * pltpu.roll(around, 1, 1),
            around * pltpu.roll(around, 2 * LANES - 1, 1),
            around * pltpu.roll(around, 1, 0),
            around * pltpu.roll(around, 2 * ROWS - 1, 0),
        )

    for n, values in enumerate(mask_products()):
        fields_out[(2 + n) * ROWS : (3 + n) * ROWS, :] = values[:ROWS, :LANES]

    def field(n):
        return fields_out[ROWS * n : ROWS * (n + 1), :]

    turning = field(0)
    turn_abs = jnp.abs(turning)
    scale = 0.25 / (NDIR * NFREQ)
    base, along, across = plain[0] * scale, plain[1] * 0.5, plain[2] * 0.5
    turn_c, turn_s = math.cos(2.0 * STEP_ANGLE), math.sin(2.0 * STEP_ANGLE)
    signed = jnp.where(turning > 0.0, turn_s, -turn_s)
    along_turn = along * turn_c - across * signed
    across_turn = across * turn_c + along * signed
    stay = 1.0 - turn_abs
    along = stay * along + turn_abs * along_turn
    across = stay * across + turn_abs * across_turn
    local = [base + along, across, base - along]
    west, east, south, north = fluxes
    rims = zero
    for s in range(3):
        partial = field(2) * (local[s] - ((west[s] + east[s]) + (south[s] + north[s])))
        partial = partial + field(3) * jnp.where(lane == 0, 0.0, pltpu.roll(west[s], 1, 1))
        partial = partial + field(4) * jnp.where(lane == LANES - 1, 0.0, pltpu.roll(east[s], LANES - 1, 1))
        partial = partial + field(5) * jnp.where(row == 0, 0.0, pltpu.roll(south[s], 1, 0))
        partial = partial + field(6) * jnp.where(row == ROWS - 1, 0.0, pltpu.roll(north[s], ROWS - 1, 0))
        beside_send[s] = partial
        across_send[0, s] = partial[8:]
        across_send[0, s, 0:1, :] = south[s][ROWS - 1 :]
        across_send[1, s] = partial[:8]
        across_send[1, s, 7:8, :] = north[s][:1]
        beside_send[4, s : s + 1, :] = south[s][ROWS - 1 :]
        beside_send[4, 8 + s : 9 + s, :] = north[s][:1]
        rims = jnp.where(lane == LANES - 1 - s, pltpu.roll(west[s], (LANES - s) % LANES, 1) if s else west[s], rims)
        rims = jnp.where(lane == s, pltpu.roll(east[s], s, 1) if s else east[s], rims)
    beside_send[3] = rims
    across_send[0, 3] = rims[8:]
    across_send[1, 3] = rims[:8]

    def stress_copy(n):
        dy, dx = AROUND[n]
        if dy == 0:
            source, target = beside_send, beside_land.at[{1: 1, -1: 0}[dx]]
        else:
            source = across_send.at[{1: 0, -1: 1}[dy]]
            target = across_land.at[{0: 0, 1: 2, -1: 1}[dx], {1: 1, -1: 0}[dy]]
        return pltpu.make_async_remote_copy(
            src_ref=source,
            dst_ref=target,
            send_sem=stress_sem.at[0, n],
            recv_sem=stress_sem.at[1, n],
            device_id=device(dy, dx),
            device_id_type=MESH,
        )

    for n, (dy, dx) in enumerate(AROUND):

        @pl.when(exists(dy, dx))
        def _():
            stress_copy(n).start()

    for step in range(1, PEERS):
        pack_copy(step, True).wait_recv()
    for n in range(2):

        @pl.when(vertical[n])
        def _():
            band_copy(n, 1).start()

    start_halo(2)
    start_halo(3)
    prepare_first, update, finish_rows = wave_tools(fields_out, rows_out, cols_out, cells, beside, updated)
    for n in range(2):
        wait_halo(n)
    prepare_first()

    def one_step(i, angle):
        update(i, angle)
        return next_angle(*angle)

    angle = lax.fori_loop(0, DURING_STRESS, one_step, angle_at(0))

    for n in range(2):

        @pl.when(from_side[n])
        def _():
            band_copy(n, 0).wait_recv()
            band_copy(n, 1).wait_recv()

    def all_rows(ref, first):
        return tiles_of(ref, pl.ds(first, SLOTS, stride=8))

    far_masks = [all_rows(window, 6), all_rows(window, 7)]
    masks = jnp.dot(
        jnp.concatenate(far_masks, axis=0).astype(jnp.bfloat16), spread, preferred_element_type=jnp.float32
    )
    ocean_mask = [masks[:SLOTS], masks[:SLOTS], masks[SLOTS:]]
    surface = [all_rows(window_late, c) * ocean_mask[c] for c in range(3)]
    eastward = [all_rows(window, c) * ocean_mask[c] for c in range(3)]
    northward = [all_rows(window, 3 + c) * ocean_mask[c] for c in range(3)]
    bottom = [all_rows(window_late, 3 + c) for c in range(3)]
    for c in range(2):
        placed = ocean_shift(far_masks[c], -MARGIN_W)
        for t in range(2):
            mask_window[t, pl.ds(c, SLOTS, stride=2), :] = placed[:, LANES * t : LANES * (t + 1)]
    _, west_mask, east_mask, south_mask, north_mask = mask_products()

    safe = [jnp.where(bottom[c] > 0.0, bottom[c], 1.0) for c in range(3)]
    inverse = [-STRESS_GAIN / safe[c] for c in range(3)]

    def raise_surface(surface, eastward, northward):
        flow_y = along_y([bottom[c] * northward[c] for c in range(3)])
        return [
            (surface[c] - GRAVITY_STEP * (along_x(bottom[c] * eastward[c]) + flow_y[c])) * ocean_mask[c]
            for c in range(3)
        ]

    def push(surface, eastward, northward):
        slope = along_y(surface)
        new_east = [
            eastward[c] + GRAVITY_STEP * (CORIOLIS_STEP * northward[c] - along_x(surface[c])) for c in range(3)
        ]
        new_north = [northward[c] + GRAVITY_STEP * (-CORIOLIS_STEP * eastward[c] - slope[c]) for c in range(3)]
        return new_east, new_north

    surface = raise_surface(surface, eastward, northward)
    pushed = push(surface, eastward, northward)
    wave_lane, fine = iota(wide, 0), iota(wide, 1)
    wave_lane = jnp.where(wave_lane < LANES + 64, wave_lane + MARGIN_W, wave_lane - 2 * LANES + MARGIN_W)
    first = 2 * (fine // 3)
    part = fine % 3
    hits = jnp.where(wave_lane == first, 1.0, 0.0) * jnp.where(part == 0, 1.0, jnp.where(part == 1, 0.5, 0.0)) + jnp.where(
        wave_lane == first + 1, 1.0, 0.0
    ) * jnp.where(part == 2, 1.0, jnp.where(part == 1, 0.5, 0.0))
    prolong = hits.astype(jnp.bfloat16)

    for n, (dy, dx) in enumerate(AROUND):

        @pl.when(exists(-dy, -dx))
        def _():
            stress_copy(n).wait_recv()

    side_lane = iota((2 * ROWS, LANES), 1) < 64

    def assemble(s):
        columns = [
            jnp.concatenate([body, across_land[n, 0, s], across_land[n, 1, s]], axis=0)
            for n, body in enumerate((beside_send[s], beside_land[0, s], beside_land[1, s]))
        ]
        return jnp.concatenate([columns[0], jnp.where(side_lane, columns[1], columns[2])], axis=1)

    def edge_row(place):
        rows = [ref[place : place + 1, :] for ref in (beside_send.at[4], beside_land.at[0, 4], beside_land.at[1, 4])]
        return jnp.concatenate([rows[0], jnp.where(side_lane[:1], rows[1], rows[2])], axis=1)

    around_row = iota((2 * ROWS, 2 * LANES), 0)
    around_lane = iota((2 * ROWS, 2 * LANES), 1)
    west_side = west_mask * jnp.where(around_lane % LANES == 0, 1.0, 0.0)
    east_side = east_mask * jnp.where(around_lane % LANES == LANES - 1, 1.0, 0.0)
    side_flux = assemble(3)
    pieces = []
    for s in range(3):
        body = assemble(s)
        from_south = jnp.where(
            around_row == 0, body[24:25], jnp.where(around_row == ROWS, edge_row(s), 0.0)
        )
        from_north = jnp.where(
            around_row == ROWS - 1, body[23:24], jnp.where(around_row == 2 * ROWS - 1, edge_row(8 + s), 0.0)
        )
        body = body + west_side * pltpu.roll(side_flux, s + 1, 1)
        body = body + east_side * pltpu.roll(side_flux, 2 * LANES - 1 - s, 1)
        body = body + south_mask * from_south + north_mask * from_north
        for t in range(2):
            stress[s, t] = body[:, LANES * t : LANES * (t + 1)]
        for c in range(2):
            pieces.append(
                jnp.concatenate([stress[s, t, pl.ds(c, SLOTS, stride=2), :] for t in range(2)], axis=1)
            )
    spread_stress = exact_dot(jnp.concatenate(pieces, axis=0), prolong)
    tensor = []
    for s in range(3):
        low = spread_stress[2 * SLOTS * s : 2 * SLOTS * s + SLOTS]
        high = spread_stress[2 * SLOTS * s + SLOTS : 2 * SLOTS * (s + 1)]
        tensor.append([low, 0.5 * low + 0.5 * high, high])
    cross_y, normal_y = along_y(tensor[1]), along_y(tensor[2])
    force_x = [inverse[c] * (along_x(tensor[0][c]) + cross_y[c]) for c in range(3)]
    force_y = [inverse[c] * (along_x(tensor[1][c]) + normal_y[c]) for c in range(3)]

    for step in range(ITERS):
        if step > 0:
            surface = raise_surface(surface, eastward, northward)
            pushed = push(surface, eastward, northward)
        eastward = [(pushed[0][c] + force_x[c]) * ocean_mask[c] for c in range(3)]
        northward = [(pushed[1][c] + force_y[c]) * ocean_mask[c] for c in range(3)]

    is_even = lax.rem(x, 2) == 0
    low_lanes = iota((8, LANES), 1) < 64
    halves = []
    for f, values in enumerate((surface, eastward, northward)):
        for c in range(3):
            own = values[c][:8]
            low, high = ocean_shift(own, -MARGIN_O), ocean_shift(own, 64 - MARGIN_O)
            place = 8 * (3 * f + c)
            result[place : place + 8, :] = jnp.where(is_even, low[:, :LANES], high[:, LANES:])
            halves.append(jnp.where(is_even, low[:, LANES:], pltpu.roll(high[:, :LANES], 64, 1)))
    for m in range(5):
        merged = halves[m] if m == 4 else jnp.where(low_lanes, halves[m], pltpu.roll(halves[5 + m], 64, 1))
        result[72 + 8 * m : 80 + 8 * m, :] = merged
    for dest in range(PEERS):
        result_send[dest, 0:8, :] = result[pl.ds(dest, 8, stride=8), :]
        result_send[dest, 8:14, :] = result[pl.ds(64 + dest, 6, stride=8), :]

    def result_copy(step):
        dest = peer(step)
        return pltpu.make_async_remote_copy(
            src_ref=result_send.at[dest[2]],
            dst_ref=result_land.at[x],
            send_sem=result_sem.at[0, step],
            recv_sem=result_sem.at[1, step],
            device_id=dest,
            device_id_type=MESH,
        )

    for step in range(1, PEERS):
        result_copy(step).start()
    result_land[x] = result_send[x]
    lax.fori_loop(DURING_STRESS, QUARTER, one_step, angle)
    for step in range(1, PEERS):
        result_copy(step).wait_recv()
    for q in range(PEERS // 2):
        left, right = result_land[2 * q], result_land[2 * q + 1]
        left_turned, right_turned = pltpu.roll(left, 64, 1), pltpu.roll(right, 64, 1)
        side = iota((5, LANES), 1) < 64
        middle = jnp.concatenate(
            [
                jnp.where(side, left[9:14], right_turned[9:14]),
                jnp.where(side[:4], left_turned[9:13], right[9:13]),
            ],
            axis=0,
        )
        for t, tile in enumerate((left, middle, right)):
            lanes = pl.ds((3 * q + t) * LANES, LANES)
            for f in range(3):
                ocean_out[f, :, lanes] = tile[3 * f : 3 * f + 3]

    for step in range(1, PEERS):
        pack_copy(step, False).wait_send()
        pack_copy(step, True).wait_send()
        result_copy(step).wait_send()
    for n, needed in enumerate((to_north, to_south)):

        @pl.when(needed)
        def _():
            for column in range(PEERS):
                brink_copy(n, column).wait_send()

        @pl.when(vertical[n])
        def _():
            band_copy(n, 0).wait_send()
            band_copy(n, 1).wait_send()

    for n, (dy, dx) in enumerate(AROUND):

        @pl.when(exists(dy, dx))
        def _():
            stress_copy(n).wait_send()

    for n in range(2, 4):
        wait_halo(n)

    def fix_step(i, angle):
        finish_rows(i, angle)
        return next_angle(*angle)

    lax.fori_loop(0, QUARTER, fix_step, angle_at(0))
    for n in range(4):

        @pl.when(sends[n])
        def _():
            halo_copy(n).wait_send()


def hand_over(ocean_in, updated, out, ocean_out, store_sem, local_sem):
    handed = pltpu.make_async_copy(ocean_in, ocean_out, local_sem)
    handed.start()
    size = CELLS // CHUNKS
    copies = [
        pltpu.make_async_copy(updated.at[pl.ds(n * size, size)], out.at[pl.ds(n * size, size)], store_sem.at[n])
        for n in range(CHUNKS)
    ]
    for copy in copies:
        copy.start()
    for copy in copies:
        copy.wait()
    handed.wait()


def shards(mesh_shape, spectrum, sea_mask, ocean_state, depth):
    groups_y = mesh_shape["gy"]
    groups = groups_y * mesh_shape["sec"]
    cells = spectrum.reshape(CELLS, LANES)
    vmem = pl.BlockSpec(memory_space=pltpu.VMEM)
    anywhere = pl.BlockSpec(memory_space=pl.ANY)
    f32 = jnp.float32
    dma = pltpu.SemaphoreType.DMA
    ocean_part, updated = pl.pallas_call(
        functools.partial(coupled_kernel, groups_y, groups),
        out_shape=(
            jax.ShapeDtypeStruct(ocean_state.shape, f32),
            jax.ShapeDtypeStruct((CELLS, LANES), f32),
        ),
        in_specs=[anywhere] * 4,
        out_specs=(vmem, vmem),
        scratch_shapes=[
            pltpu.VMEM((7 * ROWS, LANES), f32),
            pltpu.VMEM((2, HALF, LANES), f32),
            pltpu.VMEM((2, 6, ROWS, LANES), f32),
            pltpu.VMEM((CELLS + 2 * PAD, LANES), f32),
            pltpu.VMEM((4 * NFREQ, ROWS, LANES), f32),
            pltpu.VMEM(ocean_state.shape, f32),
            pltpu.VMEM(depth.shape, f32),
            pltpu.VMEM(sea_mask.shape, jnp.int32),
            pltpu.VMEM((SLOTS, 1792), f32),
            pltpu.VMEM((8, 1280), f32),
            pltpu.VMEM((PEERS, 2, 8, LANES), f32),
            pltpu.VMEM((PEERS, 2, 8, LANES), f32),
            pltpu.VMEM((2, SLOTS * 8, LANES), f32),
            pltpu.VMEM((2, SLOTS * 8, LANES), f32),
            pltpu.VMEM((2, 2, 8, LANES), f32),
            pltpu.VMEM((2, 2 * ROWS, LANES), f32),
            pltpu.VMEM((5, ROWS, LANES), f32),
            pltpu.VMEM((2, 4, 8, LANES), f32),
            pltpu.VMEM((2, 5, ROWS, LANES), f32),
            pltpu.VMEM((3, 2, 4, 8, LANES), f32),
            pltpu.VMEM((3, 2, 2 * ROWS, LANES), f32),
            pltpu.VMEM((112, LANES), f32),
            pltpu.VMEM((PEERS, SLOTS, LANES), f32),
            pltpu.VMEM((PEERS, SLOTS, LANES), f32),
            pltpu.VMEM((2, HALF, LANES), f32),
            pltpu.VMEM((6, ROWS, LANES), f32),
            dma((3,)),
            dma((4 * LOADS,)),
            dma((2, PEERS)),
            dma((2, PEERS)),
            dma((3, PEERS)),
            dma((2, 4)),
            dma((2, 8)),
            dma((2, PEERS)),
            dma((2, 4)),
            dma((4,)),
        ],
        compiler_params=pltpu.CompilerParams(
            collective_id=0, has_side_effects=True, vmem_limit_bytes=VMEM_LIMIT
        ),
        name="coupled",
    )(*[pltpu.with_memory_space_constraint(a, pltpu.HBM) for a in (cells, sea_mask, ocean_state, depth)])
    spectrum_out, ocean_out = pl.pallas_call(
        hand_over,
        out_shape=(jax.ShapeDtypeStruct((CELLS, LANES), f32), jax.ShapeDtypeStruct(ocean_state.shape, f32)),
        in_specs=[anywhere, anywhere],
        out_specs=(anywhere, anywhere),
        scratch_shapes=[dma((CHUNKS,)), dma],
        compiler_params=pltpu.CompilerParams(vmem_limit_bytes=VMEM_LIMIT),
        name="hand_over",
    )(ocean_part, updated)
    return (spectrum_out.reshape(spectrum.shape), ocean_out)


def solution(mesh):
    return jax.shard_map(
        functools.partial(shards, dict(mesh.shape)),
        mesh=mesh,
        in_specs=(
            P(None, None, ("sec", "gy"), "gx"),
            P(("sec", "gy", "gx"), None),
            P(None, ("sec", "gy", "gx"), None),
            P(("sec", "gy", "gx"), None),
        ),
        out_specs=(P(None, None, ("sec", "gy"), "gx"), P(None, ("sec", "gy", "gx"), None)),
        check_vma=False,
    )
```

time: 36.2 us -> 30 us (0.83)
  Pallas kernels: 35.4 us -> 29.3 us
    pallas_call x1, Pallas kernels: 7.97 us -> 2.64 us  [shards(): pl.pallas_call(hand_over, out_shape=(jax.ShapeDtypeStruct((CELLS, LANES),...]
    pallas_call x1, Pallas kernels: 27.4 us -> 26.6 us  [shards(): pl.pallas_call(functools.partial(coupled_kernel, groups_y, groups), out_s...]
where the time goes in v4:
time: 30 us; the launch traced here: 29.9 us
  Pallas kernels  29.3 us (98%)
  between operations  0.64 us (2%)
    pallas_call x1, Pallas kernels, shards(): pl.pallas_call(functools.partial(coupled_kernel, groups_y, groups), out_s...  26.6 us
    pallas_call x1, Pallas kernels, shards(): pl.pallas_call(hand_over, out_shape=(jax.ShapeDtypeStruct((CELLS, LANES),...  2.64 us

profile of v4, /device:TPU:25, one launch (start us, length us, event | category | flops | bytes accessed | tf_op | source)
XLA Modules:
  0.0 29.9 jit_solution(13918665442560854971)
XLA Ops:
  0.6 26.6 %coupled.1 = (f32[3,3,1536]{2,1,0:T(4,128)S(1)}, f32[11520,128]{1,0:T(8,128)S(1)}) custom-call(f32[11520,128]{1,0:T(8,128)} %bitcast.2, s32[2,1024]{1,0:T(2,128)} %sea_mask.1, f32[3,3,1536]{2,1,0:T(4,128)} %ocean_state.1, f32[3,1536]{1,0:T(4,128)} %depth.1), custom_call_target="tpu_custom_call" | custom-call | tf_op jit(solution)/shard_map/coupled/pallas_call | solution.py:910
  27.3 2.6 %hand_over.1 = (f32[11520,128]{1,0:T(8,128)}, f32[3,3,1536]{2,1,0:T(4,128)}) custom-call(f32[3,3,1536]{2,1,0:T(4,128)S(1)} %get-tuple-element.6.ocean_in, f32[11520,128]{1,0:T(8,128)S(1)} %get-tuple-element.7.updated), custom_call_target="tpu_custom_call" | custom-call | tf_op jit(solution)/shard_map/hand_over/pallas_call | solution.py:961

commit v5 on v4

--- a/solution.py
+++ b/solution.py
@@ -214,8 +214,8 @@
     pack_late,
     window,
     window_late,
-    brink,
     mask_window,
+    turn_window,
     beside_send,
     across_send,
     beside_land,
@@ -230,7 +230,6 @@
     load_sem,
     pack_sem,
     late_sem,
-    far_sem,
     band_sem,
     stress_sem,
     result_sem,
@@ -276,15 +275,15 @@
     for step in range(1, PEERS):
         pl.semaphore_signal(barrier, inc=1, device_id=peer(step), device_id_type=MESH)
     greeted = PEERS - 1
-    for dy in (1, -1):
-        here = exists(dy, 0)
-
-        @pl.when(here)
-        def _():
-            for column in range(PEERS):
-                pl.semaphore_signal(barrier, inc=1, device_id=device_at(y + dy, column), device_id_type=MESH)
-
-        greeted = greeted + here.astype(jnp.int32) * PEERS
+    for dy, dx in AROUND:
+        if dy != 0:
+            here = exists(dy, dx)
+
+            @pl.when(here)
+            def _():
+                pl.semaphore_signal(barrier, inc=1, device_id=device(dy, dx), device_id_type=MESH)
+
+            greeted = greeted + here.astype(jnp.int32)
 
     def load(q, part):
         size = QUARTER // LOADS * PER_DIR
@@ -336,27 +335,7 @@
             device_id_type=MESH,
         )
 
-    last, first = x == PEERS - 1, x == 0
-    to_north, to_south = jnp.logical_and(last, y < groups - 1), jnp.logical_and(first, y > 0)
-
-    def brink_copy(n, column):
-        return pltpu.make_async_remote_copy(
-            src_ref=pack.at[column],
-            dst_ref=brink.at[n],
-            send_sem=far_sem.at[n, column],
-            recv_sem=far_sem.at[2, n],
-            device_id=device_at(y + (1 if n == 0 else -1), column),
-            device_id_type=MESH,
-        )
-
     pl.semaphore_wait(barrier, greeted)
-    for n, needed in enumerate((to_north, to_south)):
-
-        @pl.when(needed)
-        def _():
-            for column in range(PEERS):
-                brink_copy(n, column).start()
-
     for step in range(1, PEERS):
         pack_copy(step, False).start()
     for step in range(1, PEERS):
@@ -372,14 +351,12 @@
     def _():
         window[:, 13 * 8 : 16 * 8, :] = edge
         window_late[:, 13 * 8 : 16 * 8, :] = edge
-        brink[0] = jnp.zeros((2, 8, LANES), jnp.float32)
         across_land[:, 1] = jnp.zeros((3, 4, 8, LANES), jnp.float32)
 
     @pl.when(y == groups - 1)
     def _():
         window[:, 8 * 8 : 11 * 8, :] = edge
         window_late[:, 8 * 8 : 11 * 8, :] = edge
-        brink[1] = jnp.zeros((2, 8, LANES), jnp.float32)
         across_land[:, 0] = jnp.zeros((3, 4, 8, LANES), jnp.float32)
 
     @pl.when(x == 0)
@@ -531,66 +508,42 @@
         def _():
             band_copy(n, 0).start()
 
-    for n in range(2):
-
-        @pl.when(from_side[n])
-        def _():
-            brink_copy(n, 0).wait_recv()
-
     def tiles_of(ref, rows):
         return jnp.concatenate([ref[t, rows, :] for t in range(2)], axis=1)
 
     def own_rows(first):
         return tiles_of(window, pl.ds(first, 8, stride=8))
-
-    def brink_row(n, place):
-        return tiles_of(brink.at[n], pl.ds(place, 1))
 
     wide = (2 * LANES, 2 * LANES)
     spread = (iota(wide, 0) == (2 * iota(wide, 1)) // 3).astype(jnp.bfloat16)
     wave_masks = [own_rows(6), own_rows(7)]
-    brink_masks = [brink_row(0, 7), brink_row(1, 6)]
-    top = iota((8, 2 * LANES), 0) == 0
-    bottom_row = iota((8, 2 * LANES), 0) == 7
-    both = jnp.where(top, brink_masks[0], brink_masks[1])
     masks = jnp.dot(
-        jnp.concatenate(wave_masks + [both], axis=0).astype(jnp.bfloat16), spread, preferred_element_type=jnp.float32
+        jnp.concatenate(wave_masks, axis=0).astype(jnp.bfloat16), spread, preferred_element_type=jnp.float32
     )
-    near_mask = [masks[:8], masks[:8], masks[8:16]]
-    brink_ocean = [masks[16:17], masks[17:18]]
-
-    def near(base):
-        inner = [own_rows(base + c) * near_mask[c] for c in range(3)]
-        below = jnp.where(top, brink_row(0, base + 2) * brink_ocean[0], pltpu.roll(inner[2], 1, 0))
-        above = jnp.where(bottom_row, brink_row(1, base) * brink_ocean[1], pltpu.roll(inner[0], 7, 0))
-        slope = [(inner[1] - below) * 0.5, (inner[2] - inner[0]) * 0.5, (above - inner[1]) * 0.5]
-        return inner, slope
-
-    (near_east, east_y), (near_north, north_y) = near(0), near(3)
-    vorticity = [along_x(near_north[c]) - east_y[c] for c in range(3)]
-    divergence = [along_x(near_east[c]) + north_y[c] for c in range(3)]
-    coarse = []
-    for field in (vorticity, divergence):
-        coarse.append(2.0 * field[0] + field[1])
-        coarse.append(field[1] + 2.0 * field[2])
-    narrow = (2 * LANES, LANES)
-    fine, wave = iota(narrow, 0), iota(narrow, 1) + MARGIN_W
-    group = 3 * (wave // 2)
-    ends = jnp.where(wave % 2 == 0, group, group + 2)
-    weights = jnp.where(fine == ends, 2.0, jnp.where(fine == group + 1, 1.0, 0.0)).astype(jnp.bfloat16)
-    coarse = exact_dot(jnp.concatenate(coarse, axis=0), weights) * (1.0 / 9.0)
-    for n in range(2):
-        for c in range(2):
-            place = pl.ds(ROWS * n + c, 8, stride=2)
-            fields_out[place, :] = TURN_GAIN * jnp.tanh(coarse[16 * n + 8 * c : 16 * n + 8 * c + 8])
-
+    near_mask = [masks[:8], masks[:8], masks[8:]]
+
+    def restriction(width):
+        fine, wave = iota((2 * LANES, width), 0), iota((2 * LANES, width), 1)
+        wave = jnp.where(wave < 3 * LANES // 2, wave, wave - 2 * LANES) + MARGIN_W
+        group = 3 * (wave // 2)
+        ends = jnp.where(wave % 2 == 0, group, group + 2)
+        return jnp.where(fine == ends, 2.0, jnp.where(fine == group + 1, 1.0, 0.0)).astype(jnp.bfloat16)
+
+    near_east = [own_rows(c) * near_mask[c] for c in range(3)]
+    near_north = [own_rows(3 + c) * near_mask[c] for c in range(3)]
+    near_slope = [
+        (near_east[1] - pltpu.roll(near_east[2], 1, 0)) * 0.5,
+        (near_east[2] - near_east[0]) * 0.5,
+        (pltpu.roll(near_east[0], 7, 0) - near_east[1]) * 0.5,
+    ]
+    vorticity = [along_x(near_north[c]) - near_slope[c] for c in range(3)]
+    coarse = jnp.concatenate([2.0 * vorticity[0] + vorticity[1], vorticity[1] + 2.0 * vorticity[2]], axis=0)
+    coarse = TURN_GAIN * jnp.tanh(exact_dot(coarse, restriction(LANES)) * (1.0 / 9.0))
     for c in range(2):
+        turn_window[0, pl.ds(c, 8, stride=2), :] = coarse[8 * c : 8 * c + 8]
         placed = ocean_shift(wave_masks[c], -MARGIN_W)
-        rim_mask = ocean_shift(brink_masks[1 - c], -MARGIN_W)
         for t in range(2):
-            span = slice(LANES * t, LANES * (t + 1))
-            mask_window[t, pl.ds(c, 8, stride=2), :] = placed[:, span]
-            mask_window[t, 16 if c == 0 else 31, :] = rim_mask[0, span]
+            mask_window[t, pl.ds(c, 8, stride=2), :] = placed[:, LANES * t : LANES * (t + 1)]
 
     def mask_products():
         around = tiles_of(mask_window, slice(None))
@@ -602,17 +555,15 @@
             around * pltpu.roll(around, 2 * ROWS - 1, 0),
         )
 
-    for n, values in enumerate(mask_products()):
-        fields_out[(2 + n) * ROWS : (3 + n) * ROWS, :] = values[:ROWS, :LANES]
-
-    def field(n):
-        return fields_out[ROWS * n : ROWS * (n + 1), :]
-
-    turning = field(0)
+    near_products = [values[:ROWS, :LANES] for values in mask_products()]
+
+    inside = jnp.logical_and(row > 0, row < ROWS - 1)
+    turning = jnp.where(inside, turn_window[0, :ROWS, :], 0.0)
     turn_abs = jnp.abs(turning)
     scale = 0.25 / (NDIR * NFREQ)
     base, along, across = plain[0] * scale, plain[1] * 0.5, plain[2] * 0.5
     turn_c, turn_s = math.cos(2.0 * STEP_ANGLE), math.sin(2.0 * STEP_ANGLE)
+    plain_along, plain_across = along, across
     signed = jnp.where(turning > 0.0, turn_s, -turn_s)
     along_turn = along * turn_c - across * signed
     across_turn = across * turn_c + along * signed
@@ -623,11 +574,11 @@
     west, east, south, north = fluxes
     rims = zero
     for s in range(3):
-        partial = field(2) * (local[s] - ((west[s] + east[s]) + (south[s] + north[s])))
-        partial = partial + field(3) * jnp.where(lane == 0, 0.0, pltpu.roll(west[s], 1, 1))
-        partial = partial + field(4) * jnp.where(lane == LANES - 1, 0.0, pltpu.roll(east[s], LANES - 1, 1))
-        partial = partial + field(5) * jnp.where(row == 0, 0.0, pltpu.roll(south[s], 1, 0))
-        partial = partial + field(6) * jnp.where(row == ROWS - 1, 0.0, pltpu.roll(north[s], ROWS - 1, 0))
+        partial = near_products[0] * (local[s] - ((west[s] + east[s]) + (south[s] + north[s])))
+        partial = partial + near_products[1] * jnp.where(lane == 0, 0.0, pltpu.roll(west[s], 1, 1))
+        partial = partial + near_products[2] * jnp.where(lane == LANES - 1, 0.0, pltpu.roll(east[s], LANES - 1, 1))
+        partial = partial + near_products[3] * jnp.where(row == 0, 0.0, pltpu.roll(south[s], 1, 0))
+        partial = partial + near_products[4] * jnp.where(row == ROWS - 1, 0.0, pltpu.roll(north[s], ROWS - 1, 0))
         beside_send[s] = partial
         across_send[0, s] = partial[8:]
         across_send[0, s, 0:1, :] = south[s][ROWS - 1 :]
@@ -637,6 +588,11 @@
         beside_send[4, 8 + s : 9 + s, :] = north[s][:1]
         rims = jnp.where(lane == LANES - 1 - s, pltpu.roll(west[s], (LANES - s) % LANES, 1) if s else west[s], rims)
         rims = jnp.where(lane == s, pltpu.roll(east[s], s, 1) if s else east[s], rims)
+    for n, values in enumerate((plain_along, plain_across)):
+        across_send[0, n, 1:2, :] = values[ROWS - 1 :]
+        across_send[1, n, 6:7, :] = values[:1]
+        beside_send[4, 3 + n : 4 + n, :] = values[ROWS - 1 :]
+        beside_send[4, 11 + n : 12 + n, :] = values[:1]
     beside_send[3] = rims
     across_send[0, 3] = rims[8:]
     across_send[1, 3] = rims[:8]
@@ -673,23 +629,11 @@
 
     start_halo(2)
     start_halo(3)
-    prepare_first, update, finish_rows = wave_tools(fields_out, rows_out, cols_out, cells, beside, updated)
     for n in range(2):
-        wait_halo(n)
-    prepare_first()
-
-    def one_step(i, angle):
-        update(i, angle)
-        return next_angle(*angle)
-
-    angle = lax.fori_loop(0, DURING_STRESS, one_step, angle_at(0))
-
-    for n in range(2):
 
         @pl.when(from_side[n])
         def _():
             band_copy(n, 0).wait_recv()
-            band_copy(n, 1).wait_recv()
 
     def all_rows(ref, first):
         return tiles_of(ref, pl.ds(first, SLOTS, stride=8))
@@ -699,16 +643,49 @@
         jnp.concatenate(far_masks, axis=0).astype(jnp.bfloat16), spread, preferred_element_type=jnp.float32
     )
     ocean_mask = [masks[:SLOTS], masks[:SLOTS], masks[SLOTS:]]
-    surface = [all_rows(window_late, c) * ocean_mask[c] for c in range(3)]
     eastward = [all_rows(window, c) * ocean_mask[c] for c in range(3)]
     northward = [all_rows(window, 3 + c) * ocean_mask[c] for c in range(3)]
-    bottom = [all_rows(window_late, 3 + c) for c in range(3)]
+    east_y, north_y = along_y(eastward), along_y(northward)
+    vorticity = [along_x(northward[c]) - east_y[c] for c in range(3)]
+    divergence = [along_x(eastward[c]) + north_y[c] for c in range(3)]
+    coarse = []
+    for values in (vorticity, divergence):
+        coarse.append(2.0 * values[0] + values[1])
+        coarse.append(values[1] + 2.0 * values[2])
+    coarse = exact_dot(jnp.concatenate(coarse, axis=0), restriction(2 * LANES)) * (1.0 / 9.0)
+    coarse = TURN_GAIN * jnp.tanh(coarse)
     for c in range(2):
         placed = ocean_shift(far_masks[c], -MARGIN_W)
         for t in range(2):
-            mask_window[t, pl.ds(c, SLOTS, stride=2), :] = placed[:, LANES * t : LANES * (t + 1)]
-    _, west_mask, east_mask, south_mask, north_mask = mask_products()
-
+            span = slice(LANES * t, LANES * (t + 1))
+            mask_window[t, pl.ds(c, SLOTS, stride=2), :] = placed[:, span]
+            turn_window[t, pl.ds(c, SLOTS, stride=2), :] = coarse[SLOTS * c : SLOTS * (c + 1), span]
+        fields_out[pl.ds(ROWS + c, 8, stride=2), :] = coarse[SLOTS * (2 + c) : SLOTS * (2 + c) + 8, :LANES]
+    fields_out[:ROWS, :] = turn_window[0, :ROWS, :]
+    products = mask_products()
+    for n, values in enumerate(products):
+        fields_out[(2 + n) * ROWS : (3 + n) * ROWS, :] = values[:ROWS, :LANES]
+    around, west_mask, east_mask, south_mask, north_mask = products
+
+    prepare_first, update, finish_rows = wave_tools(fields_out, rows_out, cols_out, cells, beside, updated)
+    for n in range(2):
+        wait_halo(n)
+    prepare_first()
+
+    def one_step(i, angle):
+        update(i, angle)
+        return next_angle(*angle)
+
+    angle = lax.fori_loop(0, DURING_STRESS, one_step, angle_at(0))
+
+    for n in range(2):
+
+        @pl.when(from_side[n])
+        def _():
+            band_copy(n, 1).wait_recv()
+
+    surface = [all_rows(window_late, c) * ocean_mask[c] for c in range(3)]
+    bottom = [all_rows(window_late, 3 + c) for c in range(3)]
     safe = [jnp.where(bottom[c] > 0.0, bottom[c], 1.0) for c in range(3)]
     inverse = [-STRESS_GAIN / safe[c] for c in range(3)]
 
@@ -763,13 +740,28 @@
     east_side = east_mask * jnp.where(around_lane % LANES == LANES - 1, 1.0, 0.0)
     side_flux = assemble(3)
     pieces = []
+    bodies = [assemble(s) for s in range(3)]
+
+    def edge_rows(n):
+        low, high = edge_row(11 + n), edge_row(3 + n)
+        values = jnp.where(around_row == 0, low, jnp.where(around_row == ROWS - 1, high, 0.0))
+        values = jnp.where(around_row == ROWS, bodies[n][22:23], values)
+        return jnp.where(around_row == 2 * ROWS - 1, bodies[n][25:26], values)
+
+    edge_along, edge_across = edge_rows(0), edge_rows(1)
+    edge_turn = tiles_of(turn_window, slice(None))
+    edge_signed = jnp.where(edge_turn > 0.0, turn_s, -turn_s)
+    edge_scale = around * jnp.abs(edge_turn)
+    along_change = edge_scale * (edge_along * (turn_c - 1.0) - edge_across * edge_signed)
+    across_change = edge_scale * (edge_across * (turn_c - 1.0) + edge_along * edge_signed)
+    changes = (along_change, across_change, -along_change)
     for s in range(3):
-        body = assemble(s)
+        body = bodies[s] + changes[s]
         from_south = jnp.where(
-            around_row == 0, body[24:25], jnp.where(around_row == ROWS, edge_row(s), 0.0)
+            around_row == 0, bodies[s][24:25], jnp.where(around_row == ROWS, edge_row(s), 0.0)
         )
         from_north = jnp.where(
-            around_row == ROWS - 1, body[23:24], jnp.where(around_row == 2 * ROWS - 1, edge_row(8 + s), 0.0)
+            around_row == ROWS - 1, bodies[s][23:24], jnp.where(around_row == 2 * ROWS - 1, edge_row(8 + s), 0.0)
         )
         body = body + west_side * pltpu.roll(side_flux, s + 1, 1)
         body = body + east_side * pltpu.roll(side_flux, 2 * LANES - 1 - s, 1)
@@ -851,12 +843,7 @@
         pack_copy(step, False).wait_send()
         pack_copy(step, True).wait_send()
         result_copy(step).wait_send()
-    for n, needed in enumerate((to_north, to_south)):
-
-        @pl.when(needed)
-        def _():
-            for column in range(PEERS):
-                brink_copy(n, column).wait_send()
+    for n in range(2):
 
         @pl.when(vertical[n])
         def _():
@@ -930,7 +917,7 @@
             pltpu.VMEM((PEERS, 2, 8, LANES), f32),
             pltpu.VMEM((2, SLOTS * 8, LANES), f32),
             pltpu.VMEM((2, SLOTS * 8, LANES), f32),
-            pltpu.VMEM((2, 2, 8, LANES), f32),
+            pltpu.VMEM((2, 2 * ROWS, LANES), f32),
             pltpu.VMEM((2, 2 * ROWS, LANES), f32),
             pltpu.VMEM((5, ROWS, LANES), f32),
             pltpu.VMEM((2, 4, 8, LANES), f32),
@@ -946,7 +933,6 @@
             dma((4 * LOADS,)),
             dma((2, PEERS)),
             dma((2, PEERS)),
-            dma((3, PEERS)),
             dma((2, 4)),
             dma((2, 8)),
             dma((2, PEERS)),

time: 30 us -> 27.8 us (0.927)
  Pallas kernels: 29.3 us -> 27.1 us
    pallas_call x1, Pallas kernels: 26.6 us -> 24.4 us  [shards(): pl.pallas_call(functools.partial(coupled_kernel, groups_y, groups), out_s...]
where the time goes in v5:
time: 27.8 us; the launch traced here: 27.7 us
  Pallas kernels  27.1 us (97%)
  between operations  0.64 us (2%)
    pallas_call x1, Pallas kernels, shards(): pl.pallas_call(functools.partial(coupled_kernel, groups_y, groups), out_s...  24.4 us
    pallas_call x1, Pallas kernels, shards(): pl.pallas_call(hand_over, out_shape=(jax.ShapeDtypeStruct((CELLS, LANES),...  2.64 us

profile of v5, /device:TPU:25, one launch (start us, length us, event | category | flops | bytes accessed | tf_op | source)
XLA Modules:
  0.0 27.7 jit_solution(14239056227527992460)
XLA Ops:
  0.6 24.4 %coupled.1 = (f32[3,3,1536]{2,1,0:T(4,128)S(1)}, f32[11520,128]{1,0:T(8,128)S(1)}) custom-call(f32[11520,128]{1,0:T(8,128)} %bitcast.2, s32[2,1024]{1,0:T(2,128)} %sea_mask.1, f32[3,3,1536]{2,1,0:T(4,128)} %ocean_state.1, f32[3,1536]{1,0:T(4,128)} %depth.1), custom_call_target="tpu_custom_call" | custom-call | tf_op jit(solution)/shard_map/coupled/pallas_call | solution.py:897
  25.1 2.6 %hand_over.1 = (f32[11520,128]{1,0:T(8,128)}, f32[3,3,1536]{2,1,0:T(4,128)}) custom-call(f32[3,3,1536]{2,1,0:T(4,128)S(1)} %get-tuple-element.6.ocean_in, f32[11520,128]{1,0:T(8,128)S(1)} %get-tuple-element.7.updated), custom_call_target="tpu_custom_call" | custom-call | tf_op jit(solution)/shard_map/hand_over/pallas_call | solution.py:947

commit v6 on v5

--- a/solution.py
+++ b/solution.py
@@ -24,7 +24,7 @@
 PER_DIR = NFREQ * ROWS
 QUARTER = NDIR // 4
 PAD = 8
-DURING_STRESS = 5
+DURING_STRESS = 2
 CHUNKS = 8
 LOADS = 3
 VMEM_LIMIT = 28 * 1024 * 1024
@@ -822,6 +822,36 @@
     result_land[x] = result_send[x]
     lax.fori_loop(DURING_STRESS, QUARTER, one_step, angle)
     for step in range(1, PEERS):
+        pack_copy(step, False).wait_send()
+        pack_copy(step, True).wait_send()
+    for n in range(2):
+
+        @pl.when(vertical[n])
+        def _():
+            band_copy(n, 0).wait_send()
+            band_copy(n, 1).wait_send()
+
+    for n, (dy, dx) in enumerate(AROUND):
+
+        @pl.when(exists(dy, dx))
+        def _():
+            stress_copy(n).wait_send()
+
+    for n in range(2, 4):
+        wait_halo(n)
+
+    def fix_step(i, angle):
+        finish_rows(i, angle)
+        return next_angle(*angle)
+
+    lax.fori_loop(0, QUARTER, fix_step, angle_at(0))
+    for n in range(4):
+
+        @pl.when(sends[n])
+        def _():
+            halo_copy(n).wait_send()
+
+    for step in range(1, PEERS):
         result_copy(step).wait_recv()
     for q in range(PEERS // 2):
         left, right = result_land[2 * q], result_land[2 * q + 1]
@@ -840,35 +870,7 @@
                 ocean_out[f, :, lanes] = tile[3 * f : 3 * f + 3]
 
     for step in range(1, PEERS):
-        pack_copy(step, False).wait_send()
-        pack_copy(step, True).wait_send()
         result_copy(step).wait_send()
-    for n in range(2):
-
-        @pl.when(vertical[n])
-        def _():
-            band_copy(n, 0).wait_send()
-            band_copy(n, 1).wait_send()
-
-    for n, (dy, dx) in enumerate(AROUND):
-
-        @pl.when(exists(dy, dx))
-        def _():
-            stress_copy(n).wait_send()
-
-    for n in range(2, 4):
-        wait_halo(n)
-
-    def fix_step(i, angle):
-        finish_rows(i, angle)
-        return next_angle(*angle)
-
-    lax.fori_loop(0, QUARTER, fix_step, angle_at(0))
-    for n in range(4):
-
-        @pl.when(sends[n])
-        def _():
-            halo_copy(n).wait_send()
 
 
 def hand_over(ocean_in, updated, out, ocean_out, store_sem, local_sem):

time: 27.8 us -> 26.3 us (0.946)
  Pallas kernels: 27.1 us -> 25.5 us
    pallas_call x1, Pallas kernels: 24.4 us -> 22.9 us  [shards(): pl.pallas_call(functools.partial(coupled_kernel, groups_y, groups), out_s...]
where the time goes in v6:
time: 26.3 us; the launch traced here: 26.2 us
  Pallas kernels  25.5 us (97%)
  between operations  0.64 us (2%)
    pallas_call x1, Pallas kernels, shards(): pl.pallas_call(functools.partial(coupled_kernel, groups_y, groups), out_s...  22.9 us
    pallas_call x1, Pallas kernels, shards(): pl.pallas_call(hand_over, out_shape=(jax.ShapeDtypeStruct((CELLS, LANES),...  2.64 us

profile of v6, /device:TPU:25, one launch (start us, length us, event | category | flops | bytes accessed | tf_op | source)
XLA Modules:
  0.0 26.2 jit_solution(15166276765229565752)
XLA Ops:
  0.6 22.9 %coupled.1 = (f32[3,3,1536]{2,1,0:T(4,128)S(1)}, f32[11520,128]{1,0:T(8,128)S(1)}) custom-call(f32[11520,128]{1,0:T(8,128)} %bitcast.2, s32[2,1024]{1,0:T(2,128)} %sea_mask.1, f32[3,3,1536]{2,1,0:T(4,128)} %ocean_state.1, f32[3,1536]{1,0:T(4,128)} %depth.1), custom_call_target="tpu_custom_call" | custom-call | tf_op jit(solution)/shard_map/coupled/pallas_call | solution.py:899
  23.5 2.6 %hand_over.1 = (f32[11520,128]{1,0:T(8,128)}, f32[3,3,1536]{2,1,0:T(4,128)}) custom-call(f32[3,3,1536]{2,1,0:T(4,128)S(1)} %get-tuple-element.6.ocean_in, f32[11520,128]{1,0:T(8,128)S(1)} %get-tuple-element.7.updated), custom_call_target="tpu_custom_call" | custom-call | tf_op jit(solution)/shard_map/hand_over/pallas_call | solution.py:949

commit v7 on v6

--- a/solution.py
+++ b/solution.py
@@ -36,7 +36,8 @@
 SPEEDS = [SPEED_BASE * SPEED_RATIO**j for j in range(NFREQ)]
 STEP_ANGLE = 2.0 * math.pi / NDIR
 MESH = pl.DeviceIdType.MESH
-AROUND = [(1, 0), (-1, 0), (0, 1), (0, -1), (1, 1), (1, -1), (-1, 1), (-1, -1)]
+AROUND = [(1, 1), (1, -1), (-1, 1), (-1, -1), (1, 0), (-1, 0), (0, 1), (0, -1)]
+FAR_FIRST = (4, 3, 5, 2, 6, 1, 7)
 
 
 def iota(shape, dim):
@@ -272,8 +273,6 @@
         copy.start()
 
     barrier = pltpu.get_barrier_semaphore()
-    for step in range(1, PEERS):
-        pl.semaphore_signal(barrier, inc=1, device_id=peer(step), device_id_type=MESH)
     greeted = PEERS - 1
     for dy, dx in AROUND:
         if dy != 0:
@@ -284,6 +283,9 @@
                 pl.semaphore_signal(barrier, inc=1, device_id=device(dy, dx), device_id_type=MESH)
 
             greeted = greeted + here.astype(jnp.int32)
+
+    for step in FAR_FIRST:
+        pl.semaphore_signal(barrier, inc=1, device_id=peer(step), device_id_type=MESH)
 
     def load(q, part):
         size = QUARTER // LOADS * PER_DIR
@@ -336,9 +338,9 @@
         )
 
     pl.semaphore_wait(barrier, greeted)
-    for step in range(1, PEERS):
+    for step in FAR_FIRST:
         pack_copy(step, False).start()
-    for step in range(1, PEERS):
+    for step in FAR_FIRST:
         pack_copy(step, True).start()
     mask_window[...] = jnp.zeros_like(mask_window)
     cells[:PAD, :] = jnp.zeros((PAD, LANES), jnp.float32)
@@ -484,7 +486,7 @@
     start_halo(0)
     start_halo(1)
 
-    for step in range(1, PEERS):
+    for step in FAR_FIRST:
         pack_copy(step, False).wait_recv()
 
     def band_copy(n, late):
@@ -619,7 +621,7 @@
         def _():
             stress_copy(n).start()
 
-    for step in range(1, PEERS):
+    for step in FAR_FIRST:
         pack_copy(step, True).wait_recv()
     for n in range(2):
 
@@ -817,11 +819,11 @@
             device_id_type=MESH,
         )
 
-    for step in range(1, PEERS):
+    for step in FAR_FIRST:
         result_copy(step).start()
     result_land[x] = result_send[x]
     lax.fori_loop(DURING_STRESS, QUARTER, one_step, angle)
-    for step in range(1, PEERS):
+    for step in FAR_FIRST:
         pack_copy(step, False).wait_send()
         pack_copy(step, True).wait_send()
     for n in range(2):
@@ -851,7 +853,7 @@
         def _():
             halo_copy(n).wait_send()
 
-    for step in range(1, PEERS):
+    for step in FAR_FIRST:
         result_copy(step).wait_recv()
     for q in range(PEERS // 2):
         left, right = result_land[2 * q], result_land[2 * q + 1]
@@ -869,7 +871,7 @@
             for f in range(3):
                 ocean_out[f, :, lanes] = tile[3 * f : 3 * f + 3]
 
-    for step in range(1, PEERS):
+    for step in FAR_FIRST:
         result_copy(step).wait_send()
 
 

time: 26.3 us -> 25.9 us (0.985)
  Pallas kernels: 25.5 us -> 25.2 us
    pallas_call x1, Pallas kernels: 22.9 us -> 22.5 us  [shards(): pl.pallas_call(functools.partial(coupled_kernel, groups_y, groups), out_s...]
where the time goes in v7:
time: 25.9 us; the launch traced here: 25.8 us
  Pallas kernels  25.2 us (97%)
  between operations  0.64 us (2%)
    pallas_call x1, Pallas kernels, shards(): pl.pallas_call(functools.partial(coupled_kernel, groups_y, groups), out_s...  22.5 us
    pallas_call x1, Pallas kernels, shards(): pl.pallas_call(hand_over, out_shape=(jax.ShapeDtypeStruct((CELLS, LANES),...  2.64 us

profile of v7, /device:TPU:25, one launch (start us, length us, event | category | flops | bytes accessed | tf_op | source)
XLA Modules:
  0.0 25.8 jit_solution(12544222752722099994)
XLA Ops:
  0.6 22.5 %coupled.1 = (f32[3,3,1536]{2,1,0:T(4,128)S(1)}, f32[11520,128]{1,0:T(8,128)S(1)}) custom-call(f32[11520,128]{1,0:T(8,128)} %bitcast.2, s32[2,1024]{1,0:T(2,128)} %sea_mask.1, f32[3,3,1536]{2,1,0:T(4,128)} %ocean_state.1, f32[3,1536]{1,0:T(4,128)} %depth.1), custom_call_target="tpu_custom_call" | custom-call | tf_op jit(solution)/shard_map/coupled/pallas_call | solution.py:901
  23.2 2.6 %hand_over.1 = (f32[11520,128]{1,0:T(8,128)}, f32[3,3,1536]{2,1,0:T(4,128)}) custom-call(f32[3,3,1536]{2,1,0:T(4,128)S(1)} %get-tuple-element.6.ocean_in, f32[11520,128]{1,0:T(8,128)S(1)} %get-tuple-element.7.updated), custom_call_target="tpu_custom_call" | custom-call | tf_op jit(solution)/shard_map/hand_over/pallas_call | solution.py:951

commit v8 on v7

--- a/solution.py
+++ b/solution.py
@@ -180,13 +180,12 @@
             factor = fields[edge : edge + 1, :] * speed_y
             direction = q * QUARTER + i
             source = (direction if from_south else direction - 2 * QUARTER) * NFREQ
-            for first in (0, 8, 16):
-                count = min(8, NFREQ - first)
-                speeds = jnp.zeros((count, LANES), jnp.float32)
-                for r in range(count):
-                    speeds = jnp.where(row[:count] == r, SPEEDS[first + r], speeds)
-                span = pl.ds((direction * NFREQ + first) * ROWS + (0 if from_south else ROWS - 1), count, stride=ROWS)
-                rim = rows[0 if from_south else 1, pl.ds(source + first, count), :]
+            for first, done in ((0, 0), (8, 0), (NFREQ - 8, 4)):
+                speeds = jnp.zeros((8, LANES), jnp.float32)
+                for r in range(done, 8):
+                    speeds = jnp.where(row == r, SPEEDS[first + r], speeds)
+                span = pl.ds((direction * NFREQ + first) * ROWS + (0 if from_south else ROWS - 1), 8, stride=ROWS)
+                rim = rows[0 if from_south else 1, pl.ds(source + first, 8), :]
                 target[span, :] = target[span, :] + speeds * (factor * rim)
 
     return prepare_first, update, finish_rows
@@ -928,7 +927,7 @@
             pltpu.VMEM((2, 5, ROWS, LANES), f32),
             pltpu.VMEM((3, 2, 4, 8, LANES), f32),
             pltpu.VMEM((3, 2, 2 * ROWS, LANES), f32),
-            pltpu.VMEM((112, LANES), f32),
+            pltpu.VMEM((128, LANES), f32),
             pltpu.VMEM((PEERS, SLOTS, LANES), f32),
             pltpu.VMEM((PEERS, SLOTS, LANES), f32),
             pltpu.VMEM((2, HALF, LANES), f32),

time: 25.9 us -> 25.9 us (level)
  no operation moved by 1% of the time
where the time goes in v8:
time: 25.9 us; the launch traced here: 25.8 us
  Pallas kernels  25.2 us (97%)
  between operations  0.64 us (2%)
    pallas_call x1, Pallas kernels, shards(): pl.pallas_call(functools.partial(coupled_kernel, groups_y, groups), out_s...  22.5 us
    pallas_call x1, Pallas kernels, shards(): pl.pallas_call(hand_over, out_shape=(jax.ShapeDtypeStruct((CELLS, LANES),...  2.64 us

profile of v8, /device:TPU:25, one launch (start us, length us, event | category | flops | bytes accessed | tf_op | source)
XLA Modules:
  0.0 25.8 jit_solution(3533996177152634925)
XLA Ops:
  0.6 22.5 %coupled.1 = (f32[3,3,1536]{2,1,0:T(4,128)S(1)}, f32[11520,128]{1,0:T(8,128)S(1)}) custom-call(f32[11520,128]{1,0:T(8,128)} %bitcast.2, s32[2,1024]{1,0:T(2,128)} %sea_mask.1, f32[3,3,1536]{2,1,0:T(4,128)} %ocean_state.1, f32[3,1536]{1,0:T(4,128)} %depth.1), custom_call_target="tpu_custom_call" | custom-call | tf_op jit(solution)/shard_map/coupled/pallas_call | solution.py:900
  23.2 2.6 %hand_over.1 = (f32[11520,128]{1,0:T(8,128)}, f32[3,3,1536]{2,1,0:T(4,128)}) custom-call(f32[3,3,1536]{2,1,0:T(4,128)S(1)} %get-tuple-element.6.ocean_in, f32[11520,128]{1,0:T(8,128)S(1)} %get-tuple-element.7.updated), custom_call_target="tpu_custom_call" | custom-call | tf_op jit(solution)/shard_map/hand_over/pallas_call | solution.py:950
